TPU v7x, 256 devices: a whole 4x4x8 slice. The times are simulated.
256 devices in a mesh: frame: 8 (over z_hi, y), space: 32 (over z_lo, x, core).
Axes of the slice: x: 4, y: 4, z: 8 (z_hi: 2, z_lo: 4; z = z_hi * 4 + z_lo), core: 2. Of those that a mesh axis runs over, the one named last changes fastest.
Arguments:
- query: bfloat16 [32, 32, 4, 8, 1536], P('frame', 'space'), may hold values from -6 to 6
- key: bfloat16 [32, 32, 4, 8, 1536], P('frame', 'space'), may hold values from -6 to 6
- value: bfloat16 [32, 32, 4, 8, 1536], P('frame', 'space'), may hold values from -6 to 6
- grad_out: bfloat16 [32, 32, 4, 8, 1536], P('frame', 'space'), may hold values from -1.5 to 1.5
- log_norm: float32 [32, 32, 4, 8, 12], P('frame', 'space'), may hold values from 3 to 5
- delta: float32 [32, 32, 4, 8, 12], P('frame', 'space'), may hold values from -12 to 12
- tile_valid: int32 [16], replicated, may hold values from 1 to 4
Outputs:
- grad_query: bfloat16 [32, 32, 4, 8, 1536], P('frame', 'space')
- grad_key: bfloat16 [32, 32, 4, 8, 1536], P('frame', 'space')
- grad_value: bfloat16 [32, 32, 4, 8, 1536], P('frame', 'space')
All inputs are finite; a program needn't handle non-finite values.
Results may differ from a plain program's by a relative error of at most 0.0049.
Values may be sent and summed in bfloat16 or wider, within the bound.
No kernel may reach another device: no remote copies, remote signals or barrier semaphores. Data moves between devices by JAX's collectives and lax.ppermute only.
A program may use at most 192 MiB of HBM per device.

v0:
```python
import math

import jax
import jax.numpy as jnp
from jax import lax
from jax.sharding import PartitionSpec as P

HEADS = 12
HEAD_DIM = 128
TILE = 4
SPACE_W = 4
COL_TILES = 2
BCOLS = 8


def with_halo(value, sides, width):
    for axis, dim in sides:
        count, length = (lax.axis_size(axis), value.shape[dim])
        up = [(i, (i + 1) % count) for i in range(count - 1)]
        down = [(j, i) for i, j in up]
        last = lax.slice_in_dim(value, length - width, length, axis=dim)
        first = lax.slice_in_dim(value, 0, width, axis=dim)
        before = lax.ppermute(last, axis, up)
        after = lax.ppermute(first, axis, down)
        value = jnp.concatenate([before, value, after], axis=dim)
    return value


def from_behind(block, axis, distance):
    devices = range(lax.axis_size(axis))
    route = [(i - distance, i) for i in devices if i - distance in devices]
    return lax.ppermute(block, axis, route)


def lookup(table, where_at):
    slots = jnp.arange(table.shape[0], dtype=jnp.int32)
    return jnp.sum(jnp.where(where_at[:, None] == slots[None, :], table[None, :], 0), axis=1)


def line_ok(start, extent, total, table):
    where_at = start + jnp.arange(extent, dtype=jnp.int32)
    inside = (where_at >= 0) & (where_at < total)
    if table is None:
        return inside
    return inside & (where_at % TILE < lookup(table, where_at // TILE))


def frame_section(tensors, stats):
    tensors = with_halo(tensors, (("frame", 2),), TILE)
    stats = with_halo(stats, (("frame", 2),), TILE)
    return (tensors, stats)


def space_section(tensors, stats, col_at):
    for axis_dim, stride in ((4, 1), (3, SPACE_W)):
        before = []
        after = []
        for toward in (1, -1):
            extent = tensors.shape[axis_dim]
            start = extent - TILE if toward > 0 else 0
            if axis_dim == 4:
                usable = col_at != 0 if toward > 0 else col_at != SPACE_W - 1
            else:
                usable = jnp.ones((), dtype=bool)
            border = lax.slice_in_dim(tensors, start, start + TILE, axis=axis_dim)
            arrived = from_behind(border, "space", toward * stride)
            arrived = jnp.where(usable, arrived, jnp.zeros_like(arrived))
            stat_arrived = None
            stat_border = lax.slice_in_dim(stats, start, start + TILE, axis=axis_dim)
            stat_arrived = from_behind(stat_border, "space", toward * stride)
            stat_arrived = jnp.where(usable, stat_arrived, jnp.zeros_like(stat_arrived))
            if toward > 0:
                before = [arrived, stat_arrived]
            else:
                after = [arrived, stat_arrived]
        tensors = jnp.concatenate([before[0], tensors, after[0]], axis=axis_dim)
        stats = jnp.concatenate([before[1], stats, after[1]], axis=axis_dim)
    return (tensors, stats)


def widen(tensors, stats, col_at):
    tensors, stats = frame_section(tensors, stats)
    tensors, stats = space_section(tensors, stats, col_at)
    return (tensors, stats)


def head_major(shard):
    frames, rows, cols = (shard.shape[0], shard.shape[1], shard.shape[2])
    return shard.reshape(frames, rows, cols, HEADS, HEAD_DIM).transpose(3, 0, 1, 2, 4)


def own_tile(shard, column):
    piece = shard[:, :, :, TILE * column : TILE * (column + 1)]
    return piece.reshape(HEADS, TILE**3, *shard.shape[4:])


def near_tiles(widened, column):
    piece = widened[:, :, :, TILE * column : TILE * column + 3 * TILE]
    return piece.reshape(HEADS, 27 * TILE**3, *widened.shape[4:])


def query_side(own_query, own_out, own_norm, own_delta, own_mask, near_key, near_value, near_mask):
    scaling = 1.0 / math.sqrt(HEAD_DIM)
    pair_mask = own_mask[:, None] & near_mask[None, :]
    scores = (
        jnp.einsum("hqd,hkd->hqk", own_query, near_key, preferred_element_type=jnp.float32)
        * scaling
    )
    probs = jnp.where(pair_mask[None], jnp.exp(scores - own_norm[:, :, None]), 0.0)
    grad_probs = jnp.einsum("hqd,hkd->hqk", own_out, near_value, preferred_element_type=jnp.float32)
    grad_scores = (probs * (grad_probs - own_delta[:, :, None])).astype(jnp.bfloat16)
    result = (
        jnp.einsum("hqk,hkd->hqd", grad_scores, near_key, preferred_element_type=jnp.float32)
        * scaling
    )
    return result.astype(jnp.bfloat16)


def key_side(own_key, own_value, own_mask, near_query, near_out, near_norm, near_delta, near_mask):
    scaling = 1.0 / math.sqrt(HEAD_DIM)
    pair_mask = own_mask[:, None] & near_mask[None, :]
    scores = (
        jnp.einsum("hkd,hqd->hkq", own_key, near_query, preferred_element_type=jnp.float32)
        * scaling
    )
    probs = jnp.where(pair_mask[None], jnp.exp(scores - near_norm[:, None, :]), 0.0)
    probs_half = probs.astype(jnp.bfloat16)
    grad_value = jnp.einsum(
        "hkq,hqd->hkd", probs_half, near_out, preferred_element_type=jnp.float32
    )
    grad_probs = jnp.einsum("hkd,hqd->hkq", own_value, near_out, preferred_element_type=jnp.float32)
    grad_scores = (probs * (grad_probs - near_delta[:, None, :])).astype(jnp.bfloat16)
    grad_key = (
        jnp.einsum("hkq,hqd->hkd", grad_scores, near_query, preferred_element_type=jnp.float32)
        * scaling
    )
    return (grad_key.astype(jnp.bfloat16), grad_value.astype(jnp.bfloat16))


def assemble(pieces):
    blocks = [piece.reshape(HEADS, TILE, TILE, TILE, HEAD_DIM) for piece in pieces]
    joined = jnp.concatenate(blocks, axis=3)
    joined = joined.transpose(1, 2, 3, 0, 4)
    return joined.reshape(TILE, TILE, joined.shape[2], HEADS * HEAD_DIM)[:, None]


def shards(query, key, value, grad_out, log_norm, delta, tile_valid):
    frame_at = lax.axis_index("frame")
    space_at = lax.axis_index("space")
    frame_count = lax.axis_size("frame")
    frame_valid = tile_valid[:frame_count]
    row_valid = tile_valid[frame_count:]
    frame_total = TILE * frame_count
    row_total = TILE * (lax.axis_size("space") // SPACE_W)
    col_at = space_at % SPACE_W
    row_at = space_at // SPACE_W
    frame_ok = line_ok(frame_at * TILE - TILE, 3 * TILE, frame_total, frame_valid)
    row_ok = line_ok(row_at * TILE - TILE, 3 * TILE, row_total, row_valid)
    col_ok = line_ok(col_at * BCOLS - TILE, BCOLS + 2 * TILE, BCOLS * SPACE_W, None)
    usable = frame_ok[:, None, None] & row_ok[None, :, None] & col_ok[None, None, :]
    query_shard = head_major(query[:, 0])
    key_shard = head_major(key[:, 0])
    value_shard = head_major(value[:, 0])
    out_shard = head_major(grad_out[:, 0])
    norm_shard = log_norm[:, 0].transpose(3, 0, 1, 2)
    delta_shard = delta[:, 0].transpose(3, 0, 1, 2)
    stat_pair = jnp.stack([norm_shard, delta_shard])

    def own_mask(column):
        return usable[
            TILE : 2 * TILE, TILE : 2 * TILE, TILE * (column + 1) : TILE * (column + 2)
        ].reshape(-1)

    def near_mask(column):
        return usable[:, :, TILE * column : TILE * column + 3 * TILE].reshape(-1)

    every_wide, stat_wide = widen(
        jnp.stack([query_shard, key_shard, value_shard, out_shard]), stat_pair, col_at
    )
    near_keys = every_wide[1]
    near_values = every_wide[2]
    pieces = []
    for column in range(COL_TILES):
        pieces.append(
            query_side(
                own_tile(query_shard, column),
                own_tile(out_shard, column),
                own_tile(norm_shard, column),
                own_tile(delta_shard, column),
                own_mask(column),
                near_tiles(near_keys, column),
                near_tiles(near_values, column),
                near_mask(column),
            )
        )
    grad_query = assemble(pieces)
    near_queries = every_wide[0]
    near_outs = every_wide[3]
    key_pieces = []
    value_pieces = []
    for column in range(COL_TILES):
        grad_key, grad_value = key_side(
            own_tile(key_shard, column),
            own_tile(value_shard, column),
            own_mask(column),
            near_tiles(near_queries, column),
            near_tiles(near_outs, column),
            near_tiles(stat_wide[0], column),
            near_tiles(stat_wide[1], column),
            near_mask(column),
        )
        key_pieces.append(grad_key)
        value_pieces.append(grad_value)
    grad_key = assemble(key_pieces)
    grad_value = assemble(value_pieces)
    return (grad_query, grad_key, grad_value)


def solution(mesh):
    placed = (
        P("frame", "space", None, None, None),
        P("frame", "space", None, None, None),
        P("frame", "space", None, None, None),
        P("frame", "space", None, None, None),
        P("frame", "space", None, None, None),
        P("frame", "space", None, None, None),
        P(),
    )
    return jax.shard_map(
        shards,
        mesh=mesh,
        in_specs=placed,
        out_specs=(
            P("frame", "space", None, None, None),
            P("frame", "space", None, None, None),
            P("frame", "space", None, None, None),
        ),
        check_vma=False,
    )
```

profile of v0, /device:TPU:193, one launch (start us, length us, event | category | flops | bytes accessed | tf_op | source)
XLA Modules:
  0.0 867.8 jit_solution(9567972089949591936)
XLA Ops:
  1.6 2.3 copy_bitcast_fusion.4
  3.9 2.4 copy_bitcast_fusion.8
  6.4 4.6 collective-permute-start.1
  11.1 1.9 collective-permute-start
  13.0 65.0 %collective-permute-done.1 = bf16[4,12,4,4,8,128]{5,4,3,2,1,0:T(8,128)(2,1)S(1)} collective-permute-done((bf16[4,12,4,4,8,128]{5,4,3,2,1,0:T(8,128)(2,1)S(1)}, bf16[4,12,4,4,8,128]{5,4,3,2,1,0:T(8,128)(2,1)S(1)}, u32[]{:S(2)}, u32[]{:S(2)}) %collective-permute-start.1) | collective-permute-done | bytes 1572896 | tf_op jit(solution)/shard_map/ppermute | solution.py:24
  78.0 10.1 %collective-permute-done = bf16[4,12,4,4,8,128]{5,4,3,2,1,0:T(8,128)(2,1)S(1)} collective-permute-done((bf16[4,12,4,4,8,128]{5,4,3,2,1,0:T(8,128)(2,1)S(1)}, bf16[4,12,4,4,8,128]{5,4,3,2,1,0:T(8,128)(2,1)S(1)}, u32[]{:S(2)}, u32[]{:S(2)}) %collective-permute-start) | collective-permute-done | bytes 1572896 | tf_op jit(solution)/shard_map/ppermute | solution.py:23
  89.9 4.0 fusion.52
  93.8 2.4 collective-permute-start.3
  96.2 3.2 collective-permute-start.2
  99.4 25.0 %collective-permute-done.3 = bf16[4,12,12,4,4,128]{5,4,3,2,1,0:T(4,128)(2,1)} collective-permute-done((bf16[4,12,12,4,4,128]{5,4,3,2,1,0:T(4,128)(2,1)S(1)}, bf16[4,12,12,4,4,128]{5,4,3,2,1,0:T(4,128)(2,1)}, u32[]{:S(2)}, u32[]{:S(2)}) %collective-permute-start.3) | collective-permute-done | bytes 2359328 | tf_op jit(solution)/shard_map/ppermute | solution.py:32
  124.4 2.6 broadcast_select_fusion
  127.0 2.6 broadcast_select_fusion.1
  129.7 10.6 %pad_maximum_fusion.1 = bf16[4,12,12,4,16,128]{5,4,3,2,1,0:T(8,128)(2,1)} fusion(bf16[4,12,12,4,4,128]{5,4,3,2,1,0:T(4,128)(2,1)S(1)} %broadcast_select_fusion, bf16[4,12,4,4,8,128]{5,4,3,2,1,0:T(8,128)(2,1)} %copy-done.3, bf16[1,12,4,4,8,128]{5,4,3,2,1,0:T(8,128)(2,1)S(1)} %get-tuple-element.38, bf16[1,12,4,4,8,128]{5,4,3,2,1,0:T(8,128)(2,1)S(1)} %get-tuple-element.51, ...), kind=kLoop, calls=%fused_computation.1 | loop fusion | flops 75497472 | bytes 18874368 | tf_op jit(solution)/shard_map/concatenate | solution.py:76
  140.3 4.7 collective-permute-start.5
  144.9 2.1 collective-permute-start.4
  147.8 2.3 copy.122
  150.0 1.9 collective-permute-start.7
  151.9 3.4 collective-permute-start.6
  160.4 2.1 fusion.59
  162.5 2.1 fusion.58
  164.6 2.1 fusion.56
  168.9 2.1 fusion.55
  172.6 4.6 collective-permute-start.9
  179.8 383.1 %collective-permute-done.9 = f32[2,12,12,4,4]{2,4,3,1,0:T(4,128)S(1)} collective-permute-done((f32[2,12,12,4,4]{2,4,3,1,0:T(4,128)S(1)}, f32[2,12,12,4,4]{2,4,3,1,0:T(4,128)S(1)}, u32[]{:S(2)}, u32[]{:S(2)}) %collective-permute-start.9) | collective-permute-done | bytes 18464 | tf_op jit(solution)/shard_map/ppermute | solution.py:32
  564.2 2.5 pad_maximum_fusion.5
  566.7 2.6 copy.125
  571.2 5.1 collective-permute-start.10
  582.4 9.2 %collective-permute-done.11 = f32[2,12,12,4,16]{4,3,2,1,0:T(4,128)} collective-permute-done((f32[2,12,12,4,16]{4,3,2,1,0:T(4,128)}, f32[2,12,12,4,16]{4,3,2,1,0:T(4,128)}, u32[]{:S(2)}, u32[]{:S(2)}) %collective-permute-start.11) | collective-permute-done | bytes 73760 | tf_op jit(solution)/shard_map/ppermute | solution.py:32
  591.6 2.6 copy.128
  594.2 2.6 copy.127
  596.8 2.5 pad_maximum_fusion.3
  599.5 2.3 fusion.53
  601.8 3.7 copy.132
  605.5 2.3 sub.146
  607.8 3.6 copy.131
  611.4 2.3 sub.143
  613.8 3.7 copy.130
  617.4 2.4 sub.139
  619.8 3.6 copy.129
  623.4 2.3 sub.136
  625.8 32.6 %pad_maximum_fusion = bf16[4,12,12,12,16,128]{5,4,3,2,1,0:T(8,128)(2,1)} fusion(bf16[4,12,12,4,16,128]{5,4,3,2,1,0:T(8,128)(2,1)} %collective-permute-done.5, bf16[4,12,12,4,4,128]{5,4,3,2,1,0:T(4,128)(2,1)S(1)} %broadcast_select_fusion, bf16[4,12,4,4,8,128]{5,4,3,2,1,0:T(8,128)(2,1)} %copy-done.3, bf16[1,12,4,4,8,128]{5,4,3,2,1,0:T(8,128)(2,1)S(1)} %get-tuple-element.38, ...), kind=kLoop, calls=%fused_computation | loop fusion | flops 283115520 | bytes 56623104 | tf_op jit(solution)/shard_map/concatenate | solution.py:76
  658.4 17.2 %slice_bitcast_fusion = (bf16[12,12,12,16,128]{4,3,2,1,0:T(8,128)(2,1)}, bf16[12,12,12,16,128]{4,3,2,1,0:T(8,128)(2,1)}, bf16[12,12,12,16,128]{4,3,2,1,0:T(8,128)(2,1)}, bf16[12,12,12,16,128]{4,3,2,1,0:T(8,128)(2,1)S(1)}) fusion(bf16[4,12,12,12,16,128]{5,4,3,2,1,0:T(8,128)(2,1)} %pad_maximum_fusion), kind=kLoop, calls=%fused_computation.2 | loop fusion | bytes 56623104 | tf_op jit(solution)/shard_map/squeeze | solution.py:198
  675.6 6.4 fusion.51
  682.0 9.6 %reshape.274 = bf16[12,1728,128]{2,1,0:T(8,128)(2,1)} reshape(bf16[12,12,12,12,128]{4,3,2,1,0:T(8,128)(2,1)} %get-tuple-element.14) | data formatting | bytes 10616832 | tf_op jit(solution)/shard_map/reshape | solution.py:99
  691.6 12.2 %fusion.50 = (bf16[12,12,12,12,128]{4,3,2,1,0:T(8,128)(2,1)}, bf16[12,12,12,12,128]{4,3,2,1,0:T(8,128)(2,1)}) fusion(bf16[12,12,12,16,128]{4,3,2,1,0:T(8,128)(2,1)} %get-tuple-element.5), kind=kLoop, calls=%fused_computation.107 | loop fusion | bytes 21233664 | tf_op jit(solution)/shard_map/slice | solution.py:98
  703.8 9.6 %reshape.276 = bf16[12,1728,128]{2,1,0:T(8,128)(2,1)} reshape(bf16[12,12,12,12,128]{4,3,2,1,0:T(8,128)(2,1)} %get-tuple-element.12) | data formatting | bytes 10616832 | tf_op jit(solution)/shard_map/reshape | solution.py:99
  713.3 9.5 %reshape.269 = bf16[12,1728,128]{2,1,0:T(8,128)(2,1)} reshape(bf16[12,12,12,12,128]{4,3,2,1,0:T(8,128)(2,1)} %get-tuple-element.13) | data formatting | bytes 10616832 | tf_op jit(solution)/shard_map/reshape | solution.py:99
  722.9 9.6 %reshape.271 = bf16[12,1728,128]{2,1,0:T(8,128)(2,1)} reshape(bf16[12,12,12,12,128]{4,3,2,1,0:T(8,128)(2,1)} %get-tuple-element.11) | data formatting | bytes 10616832 | tf_op jit(solution)/shard_map/reshape | solution.py:99
  732.5 12.2 %fusion.49 = (bf16[12,12,12,12,128]{4,3,2,1,0:T(8,128)(2,1)}, bf16[12,12,12,12,128]{4,3,2,1,0:T(8,128)(2,1)}) fusion(bf16[12,12,12,16,128]{4,3,2,1,0:T(8,128)(2,1)} %get-tuple-element.4), kind=kLoop, calls=%fused_computation.106 | loop fusion | bytes 21233664 | tf_op jit(solution)/shard_map/slice | solution.py:98
  744.7 9.6 %reshape.284 = bf16[12,1728,128]{2,1,0:T(8,128)(2,1)} reshape(bf16[12,12,12,12,128]{4,3,2,1,0:T(8,128)(2,1)} %get-tuple-element.10) | data formatting | bytes 10616832 | tf_op jit(solution)/shard_map/reshape | solution.py:99
  754.2 12.2 %fusion.48 = (bf16[12,12,12,12,128]{4,3,2,1,0:T(8,128)(2,1)}, bf16[12,12,12,12,128]{4,3,2,1,0:T(8,128)(2,1)}) fusion(bf16[12,12,12,16,128]{4,3,2,1,0:T(8,128)(2,1)} %get-tuple-element.3), kind=kLoop, calls=%fused_computation.105 | loop fusion | bytes 21233664 | tf_op jit(solution)/shard_map/slice | solution.py:98
  766.4 9.6 %reshape.286 = bf16[12,1728,128]{2,1,0:T(8,128)(2,1)} reshape(bf16[12,12,12,12,128]{4,3,2,1,0:T(8,128)(2,1)} %get-tuple-element.8) | data formatting | bytes 10616832 | tf_op jit(solution)/shard_map/reshape | solution.py:99
  776.0 9.6 %reshape.279 = bf16[12,1728,128]{2,1,0:T(8,128)(2,1)} reshape(bf16[12,12,12,12,128]{4,3,2,1,0:T(8,128)(2,1)} %get-tuple-element.9) | data formatting | bytes 10616832 | tf_op jit(solution)/shard_map/reshape | solution.py:99
  785.5 9.7 %reshape.281 = bf16[12,1728,128]{2,1,0:T(8,128)(2,1)} reshape(bf16[12,12,12,12,128]{4,3,2,1,0:T(8,128)(2,1)} %get-tuple-element.7) | data formatting | bytes 10616832 | tf_op jit(solution)/shard_map/reshape | solution.py:99
  795.3 6.9 fusion.66
  802.2 6.9 fusion.65
  809.1 8.8 %fusion.33 = bf16[12,64,128]{2,1,0:T(8,128)(2,1)S(1)} fusion(bf16[12,1728,128]{2,1,0:T(8,128)(2,1)} %reshape.274, f32[12,1728,64]{1,2,0:T(8,128)} %fusion.66, bf16[12,1728,128]{2,1,0:T(8,128)(2,1)} %reshape.276, bf16[12,64,128]{2,1,0:T(8,128)(2,1)S(1)} %bitcast.210, f32[12,64]{1,0:T(8,128)S(1)} %copy-done.30, f32[12,64]{1,0:T(8,128)S(1)} %copy-done.31, ...), kind=kOutput, calls=%fused_computation.48 | convolution fusion | flops 687636480 | bytes 16435200 | tf_op jit(solution)/shard_map/hqk,hkd->hqd/dot_general | solution.py:113
  818.0 8.7 fusion.32
  827.6 4.4 fusion.68
  832.1 6.0 fusion.29
  838.1 8.6 fusion.35
  846.8 4.4 fusion.67
  851.2 6.0 fusion.26
  857.3 8.4 fusion.34
  (109 shorter events, 27.5 us)
Async XLA Ops:
  0.6 1.0 copy-start
  6.2 83.6 %copy-start.5 = (bf16[1,12,4,4,8,128]{5,4,3,2,1,0:T(8,128)(2,1)}, bf16[1,12,4,4,8,128]{5,4,3,2,1,0:T(8,128)(2,1)S(1)}, u32[]{:S(2)}) copy-start(bf16[1,12,4,4,8,128]{5,4,3,2,1,0:T(8,128)(2,1)S(1)} %get-tuple-element.53) | copy-start | bytes 1179652
  6.4 71.5 %collective-permute-start.1 = (bf16[4,12,4,4,8,128]{5,4,3,2,1,0:T(8,128)(2,1)S(1)}, bf16[4,12,4,4,8,128]{5,4,3,2,1,0:T(8,128)(2,1)S(1)}, u32[]{:S(2)}, u32[]{:S(2)}) collective-permute-start(bf16[4,12,4,4,8,128]{5,4,3,2,1,0:T(8,128)(2,1)S(1)} %pad_maximum_fusion.4), channel_id=1, source_target_pairs={{32,0},{64,32},{96,64},{128,96},{160,128},{192,160},{224,192},{33,... | collective-permute-start | bytes 4718600 | tf_op jit(solution)/shard_map/ppermute | solution.py:24
  11.1 77.0 %collective-permute-start = (bf16[4,12,4,4,8,128]{5,4,3,2,1,0:T(8,128)(2,1)S(1)}, bf16[4,12,4,4,8,128]{5,4,3,2,1,0:T(8,128)(2,1)S(1)}, u32[]{:S(2)}, u32[]{:S(2)}) collective-permute-start(bf16[4,12,4,4,8,128]{5,4,3,2,1,0:T(8,128)(2,1)S(1)} %pad_maximum_fusion.4), channel_id=1, source_target_pairs={{0,32},{32,64},{64,96},{96,128},{128,160},{160,192},{192,224},{1,3... | collective-permute-start | bytes 4718600 | tf_op jit(solution)/shard_map/ppermute | solution.py:23
  78.0 10.1 %copy-start.3 = (bf16[4,12,4,4,8,128]{5,4,3,2,1,0:T(8,128)(2,1)}, bf16[4,12,4,4,8,128]{5,4,3,2,1,0:T(8,128)(2,1)S(1)}, u32[]{:S(2)}) copy-start(bf16[4,12,4,4,8,128]{5,4,3,2,1,0:T(8,128)(2,1)S(1)} %collective-permute-done.1) | copy-start | bytes 4718596
  88.1 1.1 copy-start.4
  93.8 30.6 %collective-permute-start.3 = (bf16[4,12,12,4,4,128]{5,4,3,2,1,0:T(4,128)(2,1)S(1)}, bf16[4,12,12,4,4,128]{5,4,3,2,1,0:T(4,128)(2,1)}, u32[]{:S(2)}, u32[]{:S(2)}) collective-permute-start(bf16[4,12,12,4,4,128]{5,4,3,2,1,0:T(4,128)(2,1)S(1)} %get-tuple-element.16), channel_id=1, source_target_pairs={{1,0},{2,1},{3,2},{4,3},{5,4},{6,5},{7,6},{8,7},{9,8},{10,9},{11,1... | collective-permute-start | bytes 7077896 | tf_op jit(solution)/shard_map/ppermute | solution.py:32
  96.2 30.8 %collective-permute-start.2 = (bf16[4,12,12,4,4,128]{5,4,3,2,1,0:T(4,128)(2,1)}, bf16[4,12,12,4,4,128]{5,4,3,2,1,0:T(4,128)(2,1)}, u32[]{:S(2)}, u32[]{:S(2)}) collective-permute-start(bf16[4,12,12,4,4,128]{5,4,3,2,1,0:T(4,128)(2,1)} %get-tuple-element.15), channel_id=1, source_target_pairs={{0,1},{1,2},{2,3},{3,4},{4,5},{5,6},{6,7},{7,8},{8,9},{9,10},{10,1... | collective-permute-start | bytes 7077896 | tf_op jit(solution)/shard_map/ppermute | solution.py:32
  99.4 30.2 %copy-start.6 = (bf16[1,12,4,4,8,128]{5,4,3,2,1,0:T(8,128)(2,1)S(1)}, bf16[1,12,4,4,8,128]{5,4,3,2,1,0:T(8,128)(2,1)}, u32[]{:S(2)}) copy-start(bf16[1,12,4,4,8,128]{5,4,3,2,1,0:T(8,128)(2,1)} %copy-done.5) | copy-start | bytes 1179652
  129.6 10.6 %copy-start.2 = (bf16[4,12,12,4,4,128]{5,4,3,2,1,0:T(4,128)(2,1)}, bf16[4,12,12,4,4,128]{5,4,3,2,1,0:T(4,128)(2,1)S(1)}, u32[]{:S(2)}) copy-start(bf16[4,12,12,4,4,128]{5,4,3,2,1,0:T(4,128)(2,1)S(1)} %broadcast_select_fusion.1) | copy-start | bytes 7077892
  129.6 17.4 %copy-start.16 = (f32[4,1,4,8,12]{4,3,2,1,0:T(8,128)S(1)}, f32[4,1,4,8,12]{4,3,2,1,0:T(8,128)}, u32[]{:S(2)}) copy-start(f32[4,1,4,8,12]{4,3,2,1,0:T(8,128)} %param.12) | copy-start | bytes 18436
  129.7 17.4 %copy-start.18 = (f32[4,1,4,8,12]{4,3,2,1,0:T(8,128)S(1)}, f32[4,1,4,8,12]{4,3,2,1,0:T(8,128)}, u32[]{:S(2)}) copy-start(f32[4,1,4,8,12]{4,3,2,1,0:T(8,128)} %param.11) | copy-start | bytes 18436
  129.7 25.7 %copy-start.32 = (s32[16]{0:T(128)S(1)}, s32[16]{0:T(128)}, u32[]{:S(2)}) copy-start(s32[16]{0:T(128)} %param.13) | copy-start | bytes 196
  140.3 485.5 %collective-permute-start.5 = (bf16[4,12,12,4,16,128]{5,4,3,2,1,0:T(8,128)(2,1)}, bf16[4,12,12,4,16,128]{5,4,3,2,1,0:T(8,128)(2,1)}, u32[]{:S(2)}, u32[]{:S(2)}) collective-permute-start(bf16[4,12,12,4,16,128]{5,4,3,2,1,0:T(8,128)(2,1)} %pad_maximum_fusion.1), channel_id=1, source_target_pairs={{4,0},{5,1},{6,2},{7,3},{8,4},{9,5},{10,6},{11,7},{12,8},{13,9},{1... | collective-permute-start | bytes 28311560 | tf_op jit(solution)/shard_map/ppermute | solution.py:32
  144.9 480.8 %collective-permute-start.4 = (bf16[4,12,12,4,16,128]{5,4,3,2,1,0:T(8,128)(2,1)}, bf16[4,12,12,4,16,128]{5,4,3,2,1,0:T(8,128)(2,1)}, u32[]{:S(2)}, u32[]{:S(2)}) collective-permute-start(bf16[4,12,12,4,16,128]{5,4,3,2,1,0:T(8,128)(2,1)} %pad_maximum_fusion.1), channel_id=1, source_target_pairs={{0,4},{1,5},{2,6},{3,7},{4,8},{5,9},{6,10},{7,11},{8,12},{9,13},{1... | collective-permute-start | bytes 28311560 | tf_op jit(solution)/shard_map/ppermute | solution.py:32
  150.0 21.0 %collective-permute-start.7 = (f32[2,12,4,4,8]{2,4,3,1,0:T(8,128)}, f32[2,12,4,4,8]{2,4,3,1,0:T(8,128)}, u32[]{:S(2)}, u32[]{:S(2)}) collective-permute-start(f32[2,12,4,4,8]{2,4,3,1,0:T(8,128)} %copy.122), channel_id=1, source_target_pairs={{32,0},{64,32},{96,64},{128,96},{160,128},{192,160},{224,192},{33,... | collective-permute-start | bytes 36872 | tf_op jit(solution)/shard_map/ppermute | solution.py:24
  151.9 19.1 %collective-permute-start.6 = (f32[2,12,4,4,8]{2,4,3,1,0:T(8,128)}, f32[2,12,4,4,8]{2,4,3,1,0:T(8,128)}, u32[]{:S(2)}, u32[]{:S(2)}) collective-permute-start(f32[2,12,4,4,8]{2,4,3,1,0:T(8,128)} %copy.122), channel_id=1, source_target_pairs={{0,32},{32,64},{64,96},{96,128},{128,160},{160,192},{192,224},{1,3... | collective-permute-start | bytes 36872 | tf_op jit(solution)/shard_map/ppermute | solution.py:23
  155.8 0.6 copy-start.19
  160.4 16.8 %copy-start.17 = (f32[4,1,4,8,12]{4,3,2,1,0:T(8,128)S(1)}, f32[4,1,4,8,12]{4,3,2,1,0:T(8,128)}, u32[]{:S(2)}) copy-start(f32[4,1,4,8,12]{4,3,2,1,0:T(8,128)} %param.12) | copy-start | bytes 18436
  160.4 403.8 %copy-start.7 = (f32[2,12,4,4,8]{2,4,3,1,0:T(8,128)S(1)}, f32[2,12,4,4,8]{2,4,3,1,0:T(8,128)}, u32[]{:S(2)}) copy-start(f32[2,12,4,4,8]{2,4,3,1,0:T(8,128)} %copy.122) | copy-start | bytes 36868
  172.6 390.2 %collective-permute-start.9 = (f32[2,12,12,4,4]{2,4,3,1,0:T(4,128)S(1)}, f32[2,12,12,4,4]{2,4,3,1,0:T(4,128)S(1)}, u32[]{:S(2)}, u32[]{:S(2)}) collective-permute-start(f32[2,12,12,4,4]{2,4,3,1,0:T(4,128)S(1)} %get-tuple-element.28), channel_id=1, source_target_pairs={{1,0},{2,1},{3,2},{4,3},{5,4},{6,5},{7,6},{8,7},{9,8},{10,9},{11,1... | collective-permute-start | bytes 55304 | tf_op jit(solution)/shard_map/ppermute | solution.py:32
  177.9 385.0 %collective-permute-start.8 = (f32[2,12,12,4,4]{2,4,3,1,0:T(4,128)S(1)}, f32[2,12,12,4,4]{2,4,3,1,0:T(4,128)S(1)}, u32[]{:S(2)}, u32[]{:S(2)}) collective-permute-start(f32[2,12,12,4,4]{2,4,3,1,0:T(4,128)S(1)} %get-tuple-element.27), channel_id=1, source_target_pairs={{0,1},{1,2},{2,3},{3,4},{4,5},{5,6},{6,7},{7,8},{8,9},{9,10},{10,1... | collective-permute-start | bytes 55304 | tf_op jit(solution)/shard_map/ppermute | solution.py:32
  562.9 0.7 copy-start.10
  563.5 0.7 copy-start.11
  569.3 22.3 %collective-permute-start.11 = (f32[2,12,12,4,16]{4,3,2,1,0:T(4,128)}, f32[2,12,12,4,16]{4,3,2,1,0:T(4,128)}, u32[]{:S(2)}, u32[]{:S(2)}) collective-permute-start(f32[2,12,12,4,16]{4,3,2,1,0:T(4,128)} %copy.125), channel_id=1, source_target_pairs={{4,0},{5,1},{6,2},{7,3},{8,4},{9,5},{10,6},{11,7},{12,8},{13,9},{1... | collective-permute-start | bytes 221192 | tf_op jit(solution)/shard_map/ppermute | solution.py:32
  571.2 23.0 %collective-permute-start.10 = (f32[2,12,12,4,16]{4,3,2,1,0:T(4,128)}, f32[2,12,12,4,16]{4,3,2,1,0:T(4,128)}, u32[]{:S(2)}, u32[]{:S(2)}) collective-permute-start(f32[2,12,12,4,16]{4,3,2,1,0:T(4,128)} %copy.125), channel_id=1, source_target_pairs={{0,4},{1,5},{2,6},{3,7},{4,8},{5,9},{6,10},{7,11},{8,12},{9,13},{1... | collective-permute-start | bytes 221192 | tf_op jit(solution)/shard_map/ppermute | solution.py:32
  785.5 9.8 %copy-start.15 = (bf16[12,4,4,4,128]{4,3,2,1,0:T(4,128)(2,1)S(1)}, bf16[12,4,4,4,128]{4,3,2,1,0:T(4,128)(2,1)}, u32[]{:S(2)}) copy-start(bf16[12,4,4,4,128]{4,3,2,1,0:T(4,128)(2,1)} %get-tuple-element.36) | copy-start | bytes 589828
  795.3 6.9 copy-start.14
  802.2 6.9 copy-start.23
  802.2 6.9 copy-start.29
  802.2 6.9 copy-start.30
  802.2 6.9 copy-start.31
  809.1 8.9 %copy-start.21 = (bf16[12,4,4,4,128]{4,3,2,1,0:T(4,128)(2,1)S(1)}, bf16[12,4,4,4,128]{4,3,2,1,0:T(4,128)(2,1)}, u32[]{:S(2)}) copy-start(bf16[12,4,4,4,128]{4,3,2,1,0:T(4,128)(2,1)} %get-tuple-element.33) | copy-start | bytes 589828
  809.1 8.9 %copy-start.28 = (pred[64,1728]{1,0:T(8,128)(4,1)S(1)}, pred[64,1728]{1,0:T(8,128)(4,1)}, u32[]{:S(2)}) copy-start(pred[64,1728]{1,0:T(8,128)(4,1)} %broadcast_and_fusion.1) | copy-start | bytes 331780
  818.0 9.6 %copy-start.13 = (bf16[12,4,4,4,128]{4,3,2,1,0:T(4,128)(2,1)S(1)}, bf16[12,4,4,4,128]{4,3,2,1,0:T(4,128)(2,1)}, u32[]{:S(2)}) copy-start(bf16[12,4,4,4,128]{4,3,2,1,0:T(4,128)(2,1)} %get-tuple-element.26) | copy-start | bytes 589828
  827.6 4.4 copy-start.27
  832.0 6.0 copy-start.9
  832.0 6.0 copy-start.22
  832.0 6.0 copy-start.26
  838.1 8.7 copy-start.12
  846.7 4.4 copy-start.25
  851.2 6.0 copy-start.8
  851.2 6.0 copy-start.20
  851.2 6.0 copy-start.24
  857.2 10.3 %copy-start.1 = (bf16[4,1,4,8,1536]{4,3,2,1,0:T(8,128)(2,1)S(1)}, bf16[4,1,4,8,1536]{4,3,2,1,0:T(8,128)(2,1)}, u32[]{:S(2)}) copy-start(bf16[4,1,4,8,1536]{4,3,2,1,0:T(8,128)(2,1)} %param.9) | copy-start | bytes 1179652
where the time goes:
time: 879 us; the launch traced here: 868 us
  waiting for transfers between devices  492 us (56%)
  local copies, waits for them, and re-layouts  205 us (23%)
  matrix products  69.1 us (8%)
  other arithmetic  61.8 us (7%)
  starting transfers between devices  37.7 us (4%)
    ppermute x8, waiting for transfers between devices, from_behind(): return lax.ppermute(block, axis, route)  417 us
    reshape x8, local copies, waits for them, and re-layouts, near_tiles(): return piece.reshape(HEADS, 27 * TILE ** 3, *widened.shape[4:])  76.8 us
    ppermute x2, waiting for transfers between devices, with_halo(): after = lax.ppermute(first, axis, down)  65 us
    slice x9, local copies, waits for them, and re-layouts, near_tiles(): piece = widened[:, :, :, TILE * column:TILE * column + 3 * TILE]  59.8 us
    concatenate x2, other arithmetic, space_section(): tensors = jnp.concatenate([before[0], tensors, after[0]], axis=axis_dim)  43.2 us
    ppermute x8, starting transfers between devices, from_behind(): return lax.ppermute(block, axis, route)  25.9 us
  transfers between devices with their start and end apart: 12, of which 5 were waited for; matrix products, arithmetic and copies ran while one was open for 8% of the time, Pallas kernels for 0%

commit v1 on v0

v1 whole, which is shorter than its diff:
```python
import functools
import math

import jax
import jax.numpy as jnp
from jax import lax
from jax.experimental import pallas as pl
from jax.experimental.pallas import tpu as pltpu
from jax.sharding import PartitionSpec as P

HEAD_DIM = 128
GROUPS = 4
GROUP_HEADS = 3
COL_BLOCKS = 4
TOKENS = 128
HALF = 64
STAT_ROWS = 16
SCALE = 1.0 / math.sqrt(HEAD_DIM)
LOG2E = math.log2(math.e)
GROUP_WIDTH = GROUP_HEADS * HEAD_DIM
VMEM_LIMIT = 56 * 1024 * 1024

SMEM_SPEC = pl.BlockSpec(memory_space=pltpu.SMEM)


def reorder_matrix(frame_valid, row_valid):
    tiled = lax.broadcasted_iota(jnp.int32, (TOKENS, TOKENS), 0)
    stored = lax.broadcasted_iota(jnp.int32, (TOKENS, TOKENS), 1)
    tile, frame = tiled >> 6, (tiled >> 4) & 3
    row, col = (tiled >> 2) & 3, tiled & 3
    same = stored == frame * 32 + row * 8 + tile * 4 + col
    keep = same & (frame < frame_valid) & (row < row_valid)
    return jnp.where(keep, 1.0, 0.0)


def reorder_back(frame_valid, row_valid):
    stored = lax.broadcasted_iota(jnp.int32, (TOKENS, TOKENS), 0)
    tiled = lax.broadcasted_iota(jnp.int32, (TOKENS, TOKENS), 1)
    tile, frame = tiled >> 6, (tiled >> 4) & 3
    row, col = (tiled >> 2) & 3, tiled & 3
    same = stored == frame * 32 + row * 8 + tile * 4 + col
    keep = same & (frame < frame_valid) & (row < row_valid)
    return jnp.where(keep, 1.0, 0.0)


def group_lanes(group):
    return pl.ds(pl.multiple_of(group * GROUP_WIDTH, HEAD_DIM), GROUP_WIDTH)


def pack_pair(place, first, second, outs, matrix):
    for m in range(GROUPS):
        lanes = group_lanes(place ^ m)
        for part, ref in enumerate((first, second)):
            moved = jnp.dot(matrix, ref[:, lanes], preferred_element_type=jnp.float32)
            moved = moved.astype(jnp.bfloat16)
            for h in range(GROUP_HEADS):
                outs[m][h, part * TOKENS : (part + 1) * TOKENS, :] = moved[
                    :, h * HEAD_DIM : (h + 1) * HEAD_DIM
                ]


def pack_plain_kernel(where, first, second, *outs):
    matrix = reorder_matrix(where[1], where[2]).astype(jnp.bfloat16)
    pack_pair(where[0], first, second, outs, matrix)


def pack_stat_kernel(where, first, second, log_norm, delta, *rest):
    outs, table = rest[:GROUPS], rest[GROUPS]
    matrix = reorder_matrix(where[1], where[2]).astype(jnp.bfloat16)
    pack_pair(where[0], first, second, outs, matrix)
    table[...] = jnp.zeros_like(table)
    for base, stat in ((0, log_norm[...] * LOG2E), (3, delta[...])):
        left = stat
        for step in range(3):
            piece = left.astype(jnp.bfloat16)
            left = left - piece.astype(jnp.float32)
            moved = jnp.dot(matrix, piece, preferred_element_type=jnp.float32)
            turned = moved.T
            for head in range(GROUPS * GROUP_HEADS):
                table[head, base + step : base + step + 1, :] = turned[head : head + 1, :]
    for m in range(GROUPS):
        group = where[0] ^ m
        for h in range(GROUP_HEADS):
            outs[m][h, 2 * TOKENS :, :] = table[group * GROUP_HEADS + h].astype(jnp.bfloat16)


def vmem_specs(count):
    return [pl.BlockSpec(memory_space=pltpu.VMEM)] * count


def pack_plain(where, first, second):
    shape = jax.ShapeDtypeStruct((GROUP_HEADS, 2 * TOKENS, HEAD_DIM), jnp.bfloat16)
    return pl.pallas_call(
        pack_plain_kernel,
        out_shape=[shape] * GROUPS,
        in_specs=[SMEM_SPEC] + vmem_specs(2),
        out_specs=vmem_specs(GROUPS),
        compiler_params=pltpu.CompilerParams(vmem_limit_bytes=VMEM_LIMIT),
        name="pack_kv",
    )(where, first, second)


def pack_stat(where, first, second, log_norm, delta):
    shape = jax.ShapeDtypeStruct((GROUP_HEADS, 2 * TOKENS + STAT_ROWS, HEAD_DIM), jnp.bfloat16)
    return pl.pallas_call(
        pack_stat_kernel,
        out_shape=[shape] * GROUPS,
        in_specs=[SMEM_SPEC] + vmem_specs(4),
        out_specs=vmem_specs(GROUPS),
        scratch_shapes=[pltpu.VMEM((GROUPS * GROUP_HEADS, STAT_ROWS, TOKENS), jnp.float32)],
        compiler_params=pltpu.CompilerParams(vmem_limit_bytes=VMEM_LIMIT),
        name="pack_qd",
    )(where, first, second, log_norm, delta)


def dot_t(a, b):
    return lax.dot_general(a, b, (((1,), (1,)), ((), ())), preferred_element_type=jnp.float32)


def dot(a, b):
    return jnp.dot(a, b, preferred_element_type=jnp.float32)


def window(column):
    pieces = []
    if column > 0:
        pieces.append((column - 1, HALF, TOKENS))
    pieces.append((column, 0, TOKENS))
    if column < COL_BLOCKS - 1:
        pieces.append((column + 1, 0, HALF))
    return pieces


def near_rows(cell, slots, column, offset):
    parts = [cell[slots[b], 0, offset + lo : offset + hi, :] for b, lo, hi in window(column)]
    return jnp.concatenate(parts, axis=0)


def near_stat(cell, slots, column, base):
    parts = []
    for b, lo, hi in window(column):
        rows = cell[slots[b], 0, 2 * TOKENS :, :].astype(jnp.float32)
        total = rows[base : base + 1] + rows[base + 1 : base + 2] + rows[base + 2 : base + 3]
        parts.append(total[:, lo:hi])
    return jnp.concatenate(parts, axis=1)


def tile_mask(column):
    extent = sum(hi - lo for _, lo, hi in window(column))
    skip = 1 if column > 0 else 0
    own = lax.broadcasted_iota(jnp.int32, (TOKENS, extent), 0) >> 6
    near = (lax.broadcasted_iota(jnp.int32, (TOKENS, extent), 1) >> 6) - skip
    return (own - near <= 1) & (near - own <= 1)


def query_kernel(where, own, *rest):
    cells, out = rest[:-1], rest[-1]
    slots = [where[3] ^ b for b in range(COL_BLOCKS)]
    for column in range(COL_BLOCKS):
        slot = slots[column]
        query = own[slot, 0, :TOKENS, :]
        grad = own[slot, 0, TOKENS : 2 * TOKENS, :]
        stat = own[slot, 0, 2 * TOKENS :, :].astype(jnp.float32).T
        norm = stat[:, 0:1] + stat[:, 1:2] + stat[:, 2:3]
        delta = stat[:, 3:4] + stat[:, 4:5] + stat[:, 5:6]
        mask = tile_mask(column)
        total = jnp.zeros((TOKENS, HEAD_DIM), jnp.float32)
        for cell in cells:
            keys = near_rows(cell, slots, column, 0)
            values = near_rows(cell, slots, column, TOKENS)
            probs = jnp.exp2(dot_t(query, keys) * (SCALE * LOG2E) - norm)
            probs = jnp.where(mask, probs, 0.0)
            slope = probs * (dot_t(grad, values) - delta)
            total = total + dot(slope.astype(jnp.bfloat16), keys)
        out[slot, 0] = (total * SCALE).astype(jnp.bfloat16)


def key_kernel(where, own, *rest):
    cells, out = rest[:-1], rest[-1]
    slots = [where[3] ^ b for b in range(COL_BLOCKS)]
    for column in range(COL_BLOCKS):
        slot = slots[column]
        key = own[slot, 0, :TOKENS, :]
        value = own[slot, 0, TOKENS : 2 * TOKENS, :]
        mask = tile_mask(column)
        key_total = jnp.zeros((TOKENS, HEAD_DIM), jnp.float32)
        value_total = jnp.zeros((TOKENS, HEAD_DIM), jnp.float32)
        for cell in cells:
            queries = near_rows(cell, slots, column, 0)
            grads = near_rows(cell, slots, column, TOKENS)
            norm = near_stat(cell, slots, column, 0)
            delta = near_stat(cell, slots, column, 3)
            probs = jnp.exp2(dot_t(key, queries) * (SCALE * LOG2E) - norm)
            probs = jnp.where(mask, probs, 0.0)
            value_total = value_total + dot(probs.astype(jnp.bfloat16), grads)
            slope = probs * (dot_t(value, grads) - delta)
            key_total = key_total + dot(slope.astype(jnp.bfloat16), queries)
        out[slot, 0, :TOKENS, :] = (key_total * SCALE).astype(jnp.bfloat16)
        out[slot, 0, TOKENS:, :] = value_total.astype(jnp.bfloat16)


def attend(kernel, name, where, own, cells, out_rows, flops):
    def spec(array):
        rows = array.shape[2]
        return pl.BlockSpec((COL_BLOCKS, 1, rows, HEAD_DIM), lambda h: (0, h, 0, 0))

    return pl.pallas_call(
        kernel,
        grid=(GROUP_HEADS,),
        out_shape=jax.ShapeDtypeStruct(
            (COL_BLOCKS, GROUP_HEADS, out_rows, HEAD_DIM), jnp.bfloat16
        ),
        in_specs=[SMEM_SPEC, spec(own)] + [spec(cell) for cell in cells],
        out_specs=pl.BlockSpec((COL_BLOCKS, 1, out_rows, HEAD_DIM), lambda h: (0, h, 0, 0)),
        compiler_params=pltpu.CompilerParams(vmem_limit_bytes=VMEM_LIMIT),
        cost_estimate=pl.CostEstimate(flops=flops, bytes_accessed=8 << 20, transcendentals=0),
        name=name,
    )(where, own, *cells)


def unpack_kernel(parts, where, *rest):
    messages, outs = rest[:GROUPS], rest[GROUPS:]
    matrix = reorder_back(where[1], where[2]).astype(jnp.bfloat16)
    for m in range(GROUPS):
        lanes = group_lanes(where[0] ^ m)
        for part in range(parts):
            block = jnp.concatenate(
                [
                    messages[m][h, part * TOKENS : (part + 1) * TOKENS, :]
                    for h in range(GROUP_HEADS)
                ],
                axis=1,
            )
            outs[part][:, lanes] = dot(matrix, block).astype(jnp.bfloat16)


def unpack(name, where, messages, parts):
    shape = jax.ShapeDtypeStruct((TOKENS, GROUPS * GROUP_WIDTH), jnp.bfloat16)
    return pl.pallas_call(
        functools.partial(unpack_kernel, parts),
        out_shape=[shape] * parts,
        in_specs=[SMEM_SPEC] + vmem_specs(GROUPS),
        out_specs=vmem_specs(parts),
        compiler_params=pltpu.CompilerParams(vmem_limit_bytes=VMEM_LIMIT),
        name=name,
    )(where, *messages)


def exchange_route(m, space_count):
    route = []
    for s in range(space_count):
        z, high, column = s // 8, (s // 4) % 2, s % 4
        route.append((s, z * 8 + (column ^ m) * 2 + high))
    return route


def core_route(space_count):
    return [(s, s ^ 1) for s in range(space_count)]


def row_route(space_count):
    route = []
    for s in range(1, space_count - 8, 2):
        route += [(s, s + 7), (s + 7, s)]
    return route


def frame_route(frame_count, step):
    return [(f, f + step) for f in range(frame_count) if 0 <= f + step < frame_count]


def spread(messages):
    count = lax.axis_size("space")
    arrived = [lax.ppermute(v, "space", exchange_route(m, count)) for m, v in enumerate(messages)]
    return jnp.stack(arrived)


def gather_back(array):
    count = lax.axis_size("space")
    back = [[(b, a) for a, b in exchange_route(m, count)] for m in range(GROUPS)]
    return [lax.ppermute(array[m], "space", back[m]) for m in range(GROUPS)]


def cells_of(own):
    frames, spaces = lax.axis_size("frame"), lax.axis_size("space")
    column = [own] + [
        lax.ppermute(own, "frame", frame_route(frames, step)) for step in (1, -1)
    ]
    cells = []
    for cell in column:
        cells += [
            cell,
            lax.ppermute(cell, "space", core_route(spaces)),
            lax.ppermute(cell, "space", row_route(spaces)),
        ]
    return cells


def shards(query, key, value, grad_out, log_norm, delta, tile_valid):
    frame_at = lax.axis_index("frame")
    space_at = lax.axis_index("space")
    frame_count = lax.axis_size("frame")
    shape = query.shape
    where = jnp.stack(
        [
            space_at % 4,
            tile_valid[frame_at],
            tile_valid[frame_count + space_at // 4],
            (space_at // 2) % 4,
        ]
    ).astype(jnp.int32)

    def flat(array):
        return array.reshape(TOKENS, array.shape[-1])

    own_kv = spread(pack_plain(where, flat(key), flat(value)))
    own_qd = spread(
        pack_stat(where, flat(query), flat(grad_out), flat(log_norm), flat(delta))
    )
    kv_cells = cells_of(own_kv)
    qd_cells = cells_of(own_qd)
    unit = 2 * 64 * 1728 * 128 * 8 * 3
    grad_q = attend(query_kernel, "query_side", where, own_qd, kv_cells, TOKENS, 3 * unit)
    grad_kv = attend(key_kernel, "key_side", where, own_kv, qd_cells, 2 * TOKENS, 4 * unit)
    (out_q,) = unpack("unpack_q", where, gather_back(grad_q), 1)
    out_k, out_v = unpack("unpack_kv", where, gather_back(grad_kv), 2)
    return (out_q.reshape(shape), out_k.reshape(shape), out_v.reshape(shape))


def solution(mesh):
    blocks = P("frame", "space", None, None, None)
    return jax.shard_map(
        shards,
        mesh=mesh,
        in_specs=(blocks,) * 6 + (P(),),
        out_specs=(blocks,) * 3,
        check_vma=False,
    )
```

time: 879 us -> 217 us (0.25)
  the two profiles are of different devices: /device:TPU:193 before, /device:TPU:192 now
where the time goes in v1:
time: 217 us
  starting transfers between devices  114 us (53%)
  waiting for transfers between devices  52.2 us (24%)
  Pallas kernels  42.1 us (19%)
  local copies, waits for them, and re-layouts  5.72 us (3%)
    ppermute x4, waiting for transfers between devices, cells_of(): lax.ppermute(own, 'frame', frame_route(frames, step))  39 us
    ppermute x6, starting transfers between devices, cells_of(): lax.ppermute(cell, 'space', core_route(spaces))  33 us
    pallas_call x2, Pallas kernels, attend(): pl.pallas_call(kernel, grid=(GROUP_HEADS,), out_shape=jax.ShapeDtypeStruc...  32.8 us
    ppermute x4, starting transfers between devices, cells_of(): lax.ppermute(own, 'frame', frame_route(frames, step))  23.7 us
    ppermute x8, starting transfers between devices, gather_back(): return [lax.ppermute(array[m], 'space', back[m]) for m in range(GROUPS)]  22.8 us
    ppermute x8, starting transfers between devices, spread(): lax.ppermute(v, 'space', exchange_route(m, count))  18.5 us
    ppermute x6, starting transfers between devices, cells_of(): lax.ppermute(cell, 'space', row_route(spaces))  15.5 us
    ppermute x8, waiting for transfers between devices, gather_back(): return [lax.ppermute(array[m], 'space', back[m]) for m in range(GROUPS)]  7.28 us
  transfers between devices with their start and end apart: 32, of which 6 were waited for; matrix products, arithmetic and copies ran while one was open for 1% of the time, Pallas kernels for 17%

profile of v1, /device:TPU:192, one launch (start us, length us, event | category | flops | bytes accessed | tf_op | source)
XLA Modules:
  0.0 216.7 jit_solution(5692586505614565535)
XLA Ops:
  0.7 0.6 copy-done.18
  1.3 0.6 fusion
  1.9 1.8 pad_add_fusion.where
  3.8 2.2 %pack_kv.1 = (bf16[3,256,128]{2,1,0:T(8,128)(2,1)}, bf16[3,256,128]{2,1,0:T(8,128)(2,1)}, bf16[3,256,128]{2,1,0:T(8,128)(2,1)}, bf16[3,256,128]{2,1,0:T(8,128)(2,1)}) custom-call(s32[4]{0:T(128)} %pad_add_fusion.where, bf16[128,1536]{1,0:T(8,128)(2,1)} %bitcast.43, bf16[128,1536]{1,0:T(8,128)(2,1)} %bitcast.44), custom_call_target="tpu_custom_call" | custom-call | tf_op jit(solution)/shard_map/pack_kv/pallas_call | solution.py:93
  6.0 1.6 collective-permute-start.4
  7.6 3.4 %collective-permute-start.5 = (bf16[3,256,128]{2,1,0:T(8,128)(2,1)}, bf16[3,256,128]{2,1,0:T(8,128)(2,1)S(1)}, u32[]{:S(2)}, u32[]{:S(2)}) collective-permute-start(bf16[3,256,128]{2,1,0:T(8,128)(2,1)} %get-tuple-element.18), channel_id=1, source_target_pairs={{0,2},{1,0},{2,6},{3,4},{4,3},{5,1},{6,7},{7,5},{8,10},{9,8},{10,1... | collective-permute-start | bytes 589832 | tf_op jit(solution)/shard_map/ppermute | solution.py:274
  11.0 2.4 %collective-permute-start.6 = (bf16[3,256,128]{2,1,0:T(8,128)(2,1)}, bf16[3,256,128]{2,1,0:T(8,128)(2,1)S(1)}, u32[]{:S(2)}, u32[]{:S(2)}) collective-permute-start(bf16[3,256,128]{2,1,0:T(8,128)(2,1)} %get-tuple-element.19), channel_id=1, source_target_pairs={{0,4},{1,6},{2,0},{3,2},{4,5},{5,7},{6,1},{7,3},{8,12},{9,14},{10,... | collective-permute-start | bytes 589832 | tf_op jit(solution)/shard_map/ppermute | solution.py:274
  13.4 1.9 collective-permute-start.7
  15.3 4.2 %collective-permute-done.6 = bf16[3,256,128]{2,1,0:T(8,128)(2,1)S(1)} collective-permute-done((bf16[3,256,128]{2,1,0:T(8,128)(2,1)}, bf16[3,256,128]{2,1,0:T(8,128)(2,1)S(1)}, u32[]{:S(2)}, u32[]{:S(2)}) %collective-permute-start.6) | collective-permute-done | bytes 196640 | tf_op jit(solution)/shard_map/ppermute | solution.py:274
  19.5 1.6 collective-permute-done.7
  21.1 0.1 pad_maximum_fusion.1.rest_0_.own
  21.2 3.5 %collective-permute-start.10 = (bf16[4,3,256,128]{3,2,1,0:T(8,128)(2,1)S(1)}, bf16[4,3,256,128]{3,2,1,0:T(8,128)(2,1)S(1)}, u32[]{:S(2)}, u32[]{:S(2)}) collective-permute-start(bf16[4,3,256,128]{3,2,1,0:T(8,128)(2,1)S(1)} %pad_maximum_fusion.1.rest_0_.own), channel_id=1, source_target_pairs={{0,32},{32,64},{64,96},{96,128},{128,160},{160,192},{192,224},{1,3... | collective-permute-start | bytes 2359304 | tf_op jit(solution)/shard_map/ppermute | solution.py:287
  24.7 2.5 %pack_qd.1 = (bf16[3,272,128]{2,1,0:T(8,128)(2,1)}, bf16[3,272,128]{2,1,0:T(8,128)(2,1)}, bf16[3,272,128]{2,1,0:T(8,128)(2,1)}, bf16[3,272,128]{2,1,0:T(8,128)(2,1)}) custom-call(s32[4]{0:T(128)} %pad_add_fusion.where, bf16[128,1536]{1,0:T(8,128)(2,1)} %bitcast.41, bf16[128,1536]{1,0:T(8,128)(2,1)} %bitcast.42, f32[128,12]{1,0:T(8,128)} %bitcast.54, ...), custom_call_target="tpu_custom_call" | custom-call | tf_op jit(solution)/shard_map/pack_qd/pallas_call | solution.py:105
  27.3 1.6 collective-permute-start
  28.9 2.3 %collective-permute-start.1 = (bf16[3,272,128]{2,1,0:T(8,128)(2,1)}, bf16[3,272,128]{2,1,0:T(8,128)(2,1)S(1)}, u32[]{:S(2)}, u32[]{:S(2)}) collective-permute-start(bf16[3,272,128]{2,1,0:T(8,128)(2,1)} %get-tuple-element.14), channel_id=1, source_target_pairs={{0,2},{1,0},{2,6},{3,4},{4,3},{5,1},{6,7},{7,5},{8,10},{9,8},{10,1... | collective-permute-start | bytes 626696 | tf_op jit(solution)/shard_map/ppermute | solution.py:274
  31.2 3.3 %collective-permute-start.2 = (bf16[3,272,128]{2,1,0:T(8,128)(2,1)}, bf16[3,272,128]{2,1,0:T(8,128)(2,1)S(1)}, u32[]{:S(2)}, u32[]{:S(2)}) collective-permute-start(bf16[3,272,128]{2,1,0:T(8,128)(2,1)} %get-tuple-element.15), channel_id=1, source_target_pairs={{0,4},{1,6},{2,0},{3,2},{4,5},{5,7},{6,1},{7,3},{8,12},{9,14},{10,... | collective-permute-start | bytes 626696 | tf_op jit(solution)/shard_map/ppermute | solution.py:274
  34.5 1.9 collective-permute-start.3
  36.5 0.0 collective-permute-done
  36.5 8.4 %collective-permute-start.13 = (bf16[4,3,256,128]{3,2,1,0:T(8,128)(2,1)S(1)}, bf16[4,3,256,128]{3,2,1,0:T(8,128)(2,1)S(1)}, u32[]{:S(2)}, u32[]{:S(2)}) collective-permute-start(bf16[4,3,256,128]{3,2,1,0:T(8,128)(2,1)S(1)} %pad_maximum_fusion.1.rest_0_.own), channel_id=1, source_target_pairs={{32,0},{64,32},{96,64},{128,96},{160,128},{192,160},{224,192},{33,... | collective-permute-start | bytes 2359304 | tf_op jit(solution)/shard_map/ppermute | solution.py:287
  44.9 0.0 collective-permute-done.1
  44.9 0.1 pad_maximum_fusion.own.rest_0_
  45.0 1.9 collective-permute-start.22
  46.9 9.9 %collective-permute-start.25 = (bf16[4,3,272,128]{3,2,1,0:T(8,128)(2,1)S(1)}, bf16[4,3,272,128]{3,2,1,0:T(8,128)(2,1)}, u32[]{:S(2)}, u32[]{:S(2)}) collective-permute-start(bf16[4,3,272,128]{3,2,1,0:T(8,128)(2,1)S(1)} %pad_maximum_fusion.own.rest_0_), channel_id=1, source_target_pairs={{32,0},{64,32},{96,64},{128,96},{160,128},{192,160},{224,192},{33,... | collective-permute-start | bytes 2506760 | tf_op jit(solution)/shard_map/ppermute | solution.py:287
  56.9 0.6 collective-permute-start.8
  57.5 26.8 %collective-permute-done.10.rest_3_ = bf16[4,3,256,128]{3,2,1,0:T(8,128)(2,1)S(1)} collective-permute-done((bf16[4,3,256,128]{3,2,1,0:T(8,128)(2,1)S(1)}, bf16[4,3,256,128]{3,2,1,0:T(8,128)(2,1)S(1)}, u32[]{:S(2)}, u32[]{:S(2)}) %collective-permute-start.10) | collective-permute-done | bytes 786464 | tf_op jit(solution)/shard_map/ppermute | solution.py:287
  84.3 1.9 collective-permute-start.9
  86.2 11.1 %collective-permute-done.13.rest_6_ = bf16[4,3,256,128]{3,2,1,0:T(8,128)(2,1)S(1)} collective-permute-done((bf16[4,3,256,128]{3,2,1,0:T(8,128)(2,1)S(1)}, bf16[4,3,256,128]{3,2,1,0:T(8,128)(2,1)S(1)}, u32[]{:S(2)}, u32[]{:S(2)}) %collective-permute-start.13) | collective-permute-done | bytes 786464 | tf_op jit(solution)/shard_map/ppermute | solution.py:287
  97.3 0.6 collective-permute-start.20
  97.9 0.1 collective-permute-start.11
  98.0 2.9 %collective-permute-start.12 = (bf16[4,3,256,128]{3,2,1,0:T(8,128)(2,1)S(1)}, bf16[4,3,256,128]{3,2,1,0:T(8,128)(2,1)S(1)}, u32[]{:S(2)}, u32[]{:S(2)}) collective-permute-start(bf16[4,3,256,128]{3,2,1,0:T(8,128)(2,1)S(1)} %collective-permute-done.10.rest_3_), channel_id=1, source_target_pairs={{1,8},{8,1},{3,10},{10,3},{5,12},{12,5},{7,14},{14,7},{9,16},{16,9... | collective-permute-start | bytes 2359304 | tf_op jit(solution)/shard_map/ppermute | solution.py:294
  100.9 1.1 collective-permute-done.22.rest_3_
  102.0 26.4 %collective-permute-start.14 = (bf16[4,3,256,128]{3,2,1,0:T(8,128)(2,1)S(1)}, bf16[4,3,256,128]{3,2,1,0:T(8,128)(2,1)S(1)}, u32[]{:S(2)}, u32[]{:S(2)}) collective-permute-start(bf16[4,3,256,128]{3,2,1,0:T(8,128)(2,1)S(1)} %collective-permute-done.13.rest_6_), channel_id=1, source_target_pairs={{0,1},{1,0},{2,3},{3,2},{4,5},{5,4},{6,7},{7,6},{8,9},{9,8},{10,11... | collective-permute-start | bytes 2359304 | tf_op jit(solution)/shard_map/ppermute | solution.py:293
  128.5 0.0 collective-permute-done.25.rest_6_
  128.5 2.3 %collective-permute-start.15 = (bf16[4,3,256,128]{3,2,1,0:T(8,128)(2,1)S(1)}, bf16[4,3,256,128]{3,2,1,0:T(8,128)(2,1)S(1)}, u32[]{:S(2)}, u32[]{:S(2)}) collective-permute-start(bf16[4,3,256,128]{3,2,1,0:T(8,128)(2,1)S(1)} %collective-permute-done.13.rest_6_), channel_id=1, source_target_pairs={{1,8},{8,1},{3,10},{10,3},{5,12},{12,5},{7,14},{14,7},{9,16},{16,9... | collective-permute-start | bytes 2359304 | tf_op jit(solution)/shard_map/ppermute | solution.py:294
  130.8 3.2 %collective-permute-start.21 = (bf16[4,3,272,128]{3,2,1,0:T(8,128)(2,1)S(1)}, bf16[4,3,272,128]{3,2,1,0:T(8,128)(2,1)}, u32[]{:S(2)}, u32[]{:S(2)}) collective-permute-start(bf16[4,3,272,128]{3,2,1,0:T(8,128)(2,1)S(1)} %pad_maximum_fusion.own.rest_0_), channel_id=1, source_target_pairs={{1,8},{8,1},{3,10},{10,3},{5,12},{12,5},{7,14},{14,7},{9,16},{16,9... | collective-permute-start | bytes 2506760 | tf_op jit(solution)/shard_map/ppermute | solution.py:294
  134.1 0.1 collective-permute-start.23
  134.2 0.0 collective-permute-done.12.rest_5_
  134.2 2.3 %collective-permute-start.24 = (bf16[4,3,272,128]{3,2,1,0:T(8,128)(2,1)S(1)}, bf16[4,3,272,128]{3,2,1,0:T(8,128)(2,1)}, u32[]{:S(2)}, u32[]{:S(2)}) collective-permute-start(bf16[4,3,272,128]{3,2,1,0:T(8,128)(2,1)S(1)} %collective-permute-done.22.rest_3_), channel_id=1, source_target_pairs={{1,8},{8,1},{3,10},{10,3},{5,12},{12,5},{7,14},{14,7},{9,16},{16,9... | collective-permute-start | bytes 2506760 | tf_op jit(solution)/shard_map/ppermute | solution.py:294
  136.5 0.0 collective-permute-done.14.rest_7_
  136.6 5.2 %collective-permute-start.26 = (bf16[4,3,272,128]{3,2,1,0:T(8,128)(2,1)}, bf16[4,3,272,128]{3,2,1,0:T(8,128)(2,1)}, u32[]{:S(2)}, u32[]{:S(2)}) collective-permute-start(bf16[4,3,272,128]{3,2,1,0:T(8,128)(2,1)} %collective-permute-done.25.rest_6_), channel_id=1, source_target_pairs={{0,1},{1,0},{2,3},{3,2},{4,5},{5,4},{6,7},{7,6},{8,9},{9,8},{10,11... | collective-permute-start | bytes 2506760 | tf_op jit(solution)/shard_map/ppermute | solution.py:293
  141.8 0.0 collective-permute-done.15.rest_8_
  141.8 2.8 %collective-permute-start.27 = (bf16[4,3,272,128]{3,2,1,0:T(8,128)(2,1)}, bf16[4,3,272,128]{3,2,1,0:T(8,128)(2,1)}, u32[]{:S(2)}, u32[]{:S(2)}) collective-permute-start(bf16[4,3,272,128]{3,2,1,0:T(8,128)(2,1)} %collective-permute-done.25.rest_6_), channel_id=1, source_target_pairs={{1,8},{8,1},{3,10},{10,3},{5,12},{12,5},{7,14},{14,7},{9,16},{16,9... | collective-permute-start | bytes 2506760 | tf_op jit(solution)/shard_map/ppermute | solution.py:294
  144.7 18.0 %query_side.1 = bf16[4,3,128,128]{3,2,1,0:T(8,128)(2,1)} custom-call(s32[4]{0:T(128)} %pad_add_fusion.where, bf16[4,3,272,128]{3,2,1,0:T(8,128)(2,1)} %copy-done, bf16[4,3,256,128]{3,2,1,0:T(8,128)(2,1)} %copy-done.1, bf16[4,3,256,128]{3,2,1,0:T(8,128)(2,1)} %copy-done.4, bf16[4,3,256,128]{3,2,1,0:T(8,128)(2,1)} %copy-done.5, ...), custom_call_target="tpu_custom_call" | custom-call | flops 2038431744 | bytes 8388608 | tf_op jit(solution)/shard_map/query_side/pallas_call | solution.py:207
  162.7 1.1 slice_bitcast_fusion.4
  163.8 0.0 collective-permute-done.21.rest_2_
  163.8 0.7 collective-permute-start.16
  164.5 0.0 collective-permute-done.23.rest_4_
  164.5 7.0 %collective-permute-start.17 = (bf16[3,128,128]{2,1,0:T(8,128)(2,1)S(1)}, bf16[3,128,128]{2,1,0:T(8,128)(2,1)S(1)}, u32[]{:S(2)}, u32[]{:S(2)}) collective-permute-start(bf16[3,128,128]{2,1,0:T(8,128)(2,1)S(1)} %get-tuple-element.32), channel_id=1, source_target_pairs={{2,0},{0,1},{6,2},{4,3},{3,4},{1,5},{7,6},{5,7},{10,8},{8,9},{14,1... | collective-permute-start | bytes 294920 | tf_op jit(solution)/shard_map/ppermute | solution.py:281
  171.5 1.7 collective-permute-start.18
  173.2 14.8 %key_side.1 = bf16[4,3,256,128]{3,2,1,0:T(8,128)(2,1)} custom-call(s32[4]{0:T(128)} %pad_add_fusion.where, bf16[4,3,256,128]{3,2,1,0:T(8,128)(2,1)} %copy-done.1, bf16[4,3,272,128]{3,2,1,0:T(8,128)(2,1)} %copy-done, bf16[4,3,272,128]{3,2,1,0:T(8,128)(2,1)} %copy-done.20, bf16[4,3,272,128]{3,2,1,0:T(8,128)(2,1)} %collective-permute-done.21.rest_2_, ...), custom_call_target="tpu_custom_call" | custom-call | flops 2717908992 | bytes 8388608 | tf_op jit(solution)/shard_map/key_side/pallas_call | solution.py:207
  188.0 1.3 slice_bitcast_fusion
  189.3 0.7 collective-permute-start.28
  190.0 4.0 %collective-permute-start.29 = (bf16[3,256,128]{2,1,0:T(8,128)(2,1)S(1)}, bf16[3,256,128]{2,1,0:T(8,128)(2,1)S(1)}, u32[]{:S(2)}, u32[]{:S(2)}) collective-permute-start(bf16[3,256,128]{2,1,0:T(8,128)(2,1)S(1)} %get-tuple-element.28), channel_id=1, source_target_pairs={{2,0},{0,1},{6,2},{4,3},{3,4},{1,5},{7,6},{5,7},{10,8},{8,9},{14,1... | collective-permute-start | bytes 589832 | tf_op jit(solution)/shard_map/ppermute | solution.py:281
  194.0 1.7 collective-permute-start.30
  195.7 1.9 collective-permute-start.31
  197.7 5.1 %collective-permute-start.19 = (bf16[3,128,128]{2,1,0:T(8,128)(2,1)S(1)}, bf16[3,128,128]{2,1,0:T(8,128)(2,1)S(1)}, u32[]{:S(2)}, u32[]{:S(2)}) collective-permute-start(bf16[3,128,128]{2,1,0:T(8,128)(2,1)S(1)} %get-tuple-element.30), channel_id=1, source_target_pairs={{6,0},{4,1},{2,2},{0,3},{7,4},{5,5},{3,6},{1,7},{14,8},{12,9},{10,... | collective-permute-start | bytes 294920 | tf_op jit(solution)/shard_map/ppermute | solution.py:281
  202.7 7.3 %collective-permute-done.19.rest_3_ = bf16[3,128,128]{2,1,0:T(8,128)(2,1)S(1)} collective-permute-done((bf16[3,128,128]{2,1,0:T(8,128)(2,1)S(1)}, bf16[3,128,128]{2,1,0:T(8,128)(2,1)S(1)}, u32[]{:S(2)}, u32[]{:S(2)}) %collective-permute-start.19) | collective-permute-done | bytes 98336 | tf_op jit(solution)/shard_map/ppermute | solution.py:281
  210.0 0.6 copy-done.17
  210.6 2.0 unpack_q.1
  212.7 0.6 copy-done.10
  213.4 0.1 copy-done.11
  213.5 0.1 copy-done.12
  213.5 0.7 copy-done.13
  214.2 2.4 %unpack_kv.1 = (bf16[128,1536]{1,0:T(8,128)(2,1)}, bf16[128,1536]{1,0:T(8,128)(2,1)}) custom-call(s32[4]{0:T(128)} %pad_add_fusion.where, bf16[3,256,128]{2,1,0:T(8,128)(2,1)} %copy-done.10, bf16[3,256,128]{2,1,0:T(8,128)(2,1)} %copy-done.11, bf16[3,256,128]{2,1,0:T(8,128)(2,1)} %copy-done.12, bf16[3,256,128]{2,1,0:T(8,128)(2,1)} %copy-done.13), custom_call_target="tpu_custom_call" | custom-call | tf_op jit(solution)/shard_map/unpack_kv/pallas_call | solution.py:239
  (54 shorter events, 0.1 us)
Async XLA Ops:
  0.7 0.7 copy-start.18
  6.0 9.3 %collective-permute-start.4 = (bf16[3,256,128]{2,1,0:T(8,128)(2,1)}, bf16[3,256,128]{2,1,0:T(8,128)(2,1)S(1)}, u32[]{:S(2)}, u32[]{:S(2)}) collective-permute-start(bf16[3,256,128]{2,1,0:T(8,128)(2,1)} %get-tuple-element.17), channel_id=1, source_target_pairs={{0,0},{1,2},{2,4},{3,6},{4,1},{5,3},{6,5},{7,7},{8,8},{9,10},{10,1... | collective-permute-start | bytes 589832 | tf_op jit(solution)/shard_map/ppermute | solution.py:274
  7.6 7.7 %collective-permute-start.5 = (bf16[3,256,128]{2,1,0:T(8,128)(2,1)}, bf16[3,256,128]{2,1,0:T(8,128)(2,1)S(1)}, u32[]{:S(2)}, u32[]{:S(2)}) collective-permute-start(bf16[3,256,128]{2,1,0:T(8,128)(2,1)} %get-tuple-element.18), channel_id=1, source_target_pairs={{0,2},{1,0},{2,6},{3,4},{4,3},{5,1},{6,7},{7,5},{8,10},{9,8},{10,1... | collective-permute-start | bytes 589832 | tf_op jit(solution)/shard_map/ppermute | solution.py:274
  11.0 8.6 %collective-permute-start.6 = (bf16[3,256,128]{2,1,0:T(8,128)(2,1)}, bf16[3,256,128]{2,1,0:T(8,128)(2,1)S(1)}, u32[]{:S(2)}, u32[]{:S(2)}) collective-permute-start(bf16[3,256,128]{2,1,0:T(8,128)(2,1)} %get-tuple-element.19), channel_id=1, source_target_pairs={{0,4},{1,6},{2,0},{3,2},{4,5},{5,7},{6,1},{7,3},{8,12},{9,14},{10,... | collective-permute-start | bytes 589832 | tf_op jit(solution)/shard_map/ppermute | solution.py:274
  13.4 7.7 %collective-permute-start.7 = (bf16[3,256,128]{2,1,0:T(8,128)(2,1)}, bf16[3,256,128]{2,1,0:T(8,128)(2,1)S(1)}, u32[]{:S(2)}, u32[]{:S(2)}) collective-permute-start(bf16[3,256,128]{2,1,0:T(8,128)(2,1)} %get-tuple-element.20), channel_id=1, source_target_pairs={{0,6},{1,4},{2,2},{3,0},{4,7},{5,5},{6,3},{7,1},{8,14},{9,12},{10,... | collective-permute-start | bytes 589832 | tf_op jit(solution)/shard_map/ppermute | solution.py:274
  21.2 63.1 %copy-start.1 = (bf16[4,3,256,128]{3,2,1,0:T(8,128)(2,1)}, bf16[4,3,256,128]{3,2,1,0:T(8,128)(2,1)S(1)}, u32[]{:S(2)}) copy-start(bf16[4,3,256,128]{3,2,1,0:T(8,128)(2,1)S(1)} %pad_maximum_fusion.1.rest_0_.own) | copy-start | bytes 2359300
  21.2 63.1 %collective-permute-start.10 = (bf16[4,3,256,128]{3,2,1,0:T(8,128)(2,1)S(1)}, bf16[4,3,256,128]{3,2,1,0:T(8,128)(2,1)S(1)}, u32[]{:S(2)}, u32[]{:S(2)}) collective-permute-start(bf16[4,3,256,128]{3,2,1,0:T(8,128)(2,1)S(1)} %pad_maximum_fusion.1.rest_0_.own), channel_id=1, source_target_pairs={{0,32},{32,64},{64,96},{96,128},{128,160},{160,192},{192,224},{1,3... | collective-permute-start | bytes 2359304 | tf_op jit(solution)/shard_map/ppermute | solution.py:287
  27.3 9.2 %collective-permute-start = (bf16[3,272,128]{2,1,0:T(8,128)(2,1)}, bf16[3,272,128]{2,1,0:T(8,128)(2,1)S(1)}, u32[]{:S(2)}, u32[]{:S(2)}) collective-permute-start(bf16[3,272,128]{2,1,0:T(8,128)(2,1)} %get-tuple-element.13), channel_id=1, source_target_pairs={{0,0},{1,2},{2,4},{3,6},{4,1},{5,3},{6,5},{7,7},{8,8},{9,10},{10,1... | collective-permute-start | bytes 626696 | tf_op jit(solution)/shard_map/ppermute | solution.py:274
  28.9 16.0 %collective-permute-start.1 = (bf16[3,272,128]{2,1,0:T(8,128)(2,1)}, bf16[3,272,128]{2,1,0:T(8,128)(2,1)S(1)}, u32[]{:S(2)}, u32[]{:S(2)}) collective-permute-start(bf16[3,272,128]{2,1,0:T(8,128)(2,1)} %get-tuple-element.14), channel_id=1, source_target_pairs={{0,2},{1,0},{2,6},{3,4},{4,3},{5,1},{6,7},{7,5},{8,10},{9,8},{10,1... | collective-permute-start | bytes 626696 | tf_op jit(solution)/shard_map/ppermute | solution.py:274
  31.2 13.7 %collective-permute-start.2 = (bf16[3,272,128]{2,1,0:T(8,128)(2,1)}, bf16[3,272,128]{2,1,0:T(8,128)(2,1)S(1)}, u32[]{:S(2)}, u32[]{:S(2)}) collective-permute-start(bf16[3,272,128]{2,1,0:T(8,128)(2,1)} %get-tuple-element.15), channel_id=1, source_target_pairs={{0,4},{1,6},{2,0},{3,2},{4,5},{5,7},{6,1},{7,3},{8,12},{9,14},{10,... | collective-permute-start | bytes 626696 | tf_op jit(solution)/shard_map/ppermute | solution.py:274
  34.5 10.3 %collective-permute-start.3 = (bf16[3,272,128]{2,1,0:T(8,128)(2,1)}, bf16[3,272,128]{2,1,0:T(8,128)(2,1)S(1)}, u32[]{:S(2)}, u32[]{:S(2)}) collective-permute-start(bf16[3,272,128]{2,1,0:T(8,128)(2,1)} %get-tuple-element.16), channel_id=1, source_target_pairs={{0,6},{1,4},{2,2},{3,0},{4,7},{5,5},{6,3},{7,1},{8,14},{9,12},{10,... | collective-permute-start | bytes 626696 | tf_op jit(solution)/shard_map/ppermute | solution.py:274
  36.5 60.8 %collective-permute-start.13 = (bf16[4,3,256,128]{3,2,1,0:T(8,128)(2,1)S(1)}, bf16[4,3,256,128]{3,2,1,0:T(8,128)(2,1)S(1)}, u32[]{:S(2)}, u32[]{:S(2)}) collective-permute-start(bf16[4,3,256,128]{3,2,1,0:T(8,128)(2,1)S(1)} %pad_maximum_fusion.1.rest_0_.own), channel_id=1, source_target_pairs={{32,0},{64,32},{96,64},{128,96},{160,128},{192,160},{224,192},{33,... | collective-permute-start | bytes 2359304 | tf_op jit(solution)/shard_map/ppermute | solution.py:287
  45.0 99.6 %copy-start = (bf16[4,3,272,128]{3,2,1,0:T(8,128)(2,1)}, bf16[4,3,272,128]{3,2,1,0:T(8,128)(2,1)S(1)}, u32[]{:S(2)}) copy-start(bf16[4,3,272,128]{3,2,1,0:T(8,128)(2,1)S(1)} %pad_maximum_fusion.own.rest_0_) | copy-start | bytes 2506756
  45.0 57.0 %collective-permute-start.22 = (bf16[4,3,272,128]{3,2,1,0:T(8,128)(2,1)S(1)}, bf16[4,3,272,128]{3,2,1,0:T(8,128)(2,1)S(1)}, u32[]{:S(2)}, u32[]{:S(2)}) collective-permute-start(bf16[4,3,272,128]{3,2,1,0:T(8,128)(2,1)S(1)} %pad_maximum_fusion.own.rest_0_), channel_id=1, source_target_pairs={{0,32},{32,64},{64,96},{96,128},{128,160},{160,192},{192,224},{1,3... | collective-permute-start | bytes 2506760 | tf_op jit(solution)/shard_map/ppermute | solution.py:287
  46.9 81.5 %collective-permute-start.25 = (bf16[4,3,272,128]{3,2,1,0:T(8,128)(2,1)S(1)}, bf16[4,3,272,128]{3,2,1,0:T(8,128)(2,1)}, u32[]{:S(2)}, u32[]{:S(2)}) collective-permute-start(bf16[4,3,272,128]{3,2,1,0:T(8,128)(2,1)S(1)} %pad_maximum_fusion.own.rest_0_), channel_id=1, source_target_pairs={{32,0},{64,32},{96,64},{128,96},{160,128},{192,160},{224,192},{33,... | collective-permute-start | bytes 2506760 | tf_op jit(solution)/shard_map/ppermute | solution.py:287
  56.9 41.0 %collective-permute-start.8 = (bf16[4,3,256,128]{3,2,1,0:T(8,128)(2,1)S(1)}, bf16[4,3,256,128]{3,2,1,0:T(8,128)(2,1)S(1)}, u32[]{:S(2)}, u32[]{:S(2)}) collective-permute-start(bf16[4,3,256,128]{3,2,1,0:T(8,128)(2,1)S(1)} %pad_maximum_fusion.1.rest_0_.own), channel_id=1, source_target_pairs={{0,1},{1,0},{2,3},{3,2},{4,5},{5,4},{6,7},{7,6},{8,9},{9,8},{10,11... | collective-permute-start | bytes 2359304 | tf_op jit(solution)/shard_map/ppermute | solution.py:293
  84.3 60.3 %copy-start.2 = (bf16[4,3,256,128]{3,2,1,0:T(8,128)(2,1)}, bf16[4,3,256,128]{3,2,1,0:T(8,128)(2,1)S(1)}, u32[]{:S(2)}) copy-start(bf16[4,3,256,128]{3,2,1,0:T(8,128)(2,1)S(1)} %collective-permute-done.10.rest_3_) | copy-start | bytes 2359300
  84.3 13.7 %collective-permute-start.9 = (bf16[4,3,256,128]{3,2,1,0:T(8,128)(2,1)S(1)}, bf16[4,3,256,128]{3,2,1,0:T(8,128)(2,1)S(1)}, u32[]{:S(2)}, u32[]{:S(2)}) collective-permute-start(bf16[4,3,256,128]{3,2,1,0:T(8,128)(2,1)S(1)} %pad_maximum_fusion.1.rest_0_.own), channel_id=1, source_target_pairs={{1,8},{8,1},{3,10},{10,3},{5,12},{12,5},{7,14},{14,7},{9,16},{16,9... | collective-permute-start | bytes 2359304 | tf_op jit(solution)/shard_map/ppermute | solution.py:294
  97.3 47.3 %copy-start.3 = (bf16[4,3,256,128]{3,2,1,0:T(8,128)(2,1)}, bf16[4,3,256,128]{3,2,1,0:T(8,128)(2,1)S(1)}, u32[]{:S(2)}) copy-start(bf16[4,3,256,128]{3,2,1,0:T(8,128)(2,1)S(1)} %collective-permute-done.13.rest_6_) | copy-start | bytes 2359300
  97.3 33.5 %collective-permute-start.20 = (bf16[4,3,272,128]{3,2,1,0:T(8,128)(2,1)S(1)}, bf16[4,3,272,128]{3,2,1,0:T(8,128)(2,1)S(1)}, u32[]{:S(2)}, u32[]{:S(2)}) collective-permute-start(bf16[4,3,272,128]{3,2,1,0:T(8,128)(2,1)S(1)} %pad_maximum_fusion.own.rest_0_), channel_id=1, source_target_pairs={{0,1},{1,0},{2,3},{3,2},{4,5},{5,4},{6,7},{7,6},{8,9},{9,8},{10,11... | collective-permute-start | bytes 2506760 | tf_op jit(solution)/shard_map/ppermute | solution.py:293
  97.9 46.7 %copy-start.4 = (bf16[4,3,256,128]{3,2,1,0:T(8,128)(2,1)}, bf16[4,3,256,128]{3,2,1,0:T(8,128)(2,1)S(1)}, u32[]{:S(2)}) copy-start(bf16[4,3,256,128]{3,2,1,0:T(8,128)(2,1)S(1)} %collective-permute-done.8.rest_1_) | copy-start | bytes 2359300
  97.9 36.2 %collective-permute-start.11 = (bf16[4,3,256,128]{3,2,1,0:T(8,128)(2,1)S(1)}, bf16[4,3,256,128]{3,2,1,0:T(8,128)(2,1)S(1)}, u32[]{:S(2)}, u32[]{:S(2)}) collective-permute-start(bf16[4,3,256,128]{3,2,1,0:T(8,128)(2,1)S(1)} %collective-permute-done.10.rest_3_), channel_id=1, source_target_pairs={{0,1},{1,0},{2,3},{3,2},{4,5},{5,4},{6,7},{7,6},{8,9},{9,8},{10,11... | collective-permute-start | bytes 2359304 | tf_op jit(solution)/shard_map/ppermute | solution.py:293
  98.0 46.6 %copy-start.5 = (bf16[4,3,256,128]{3,2,1,0:T(8,128)(2,1)}, bf16[4,3,256,128]{3,2,1,0:T(8,128)(2,1)S(1)}, u32[]{:S(2)}) copy-start(bf16[4,3,256,128]{3,2,1,0:T(8,128)(2,1)S(1)} %collective-permute-done.9.rest_2_) | copy-start | bytes 2359300
  98.0 36.2 %collective-permute-start.12 = (bf16[4,3,256,128]{3,2,1,0:T(8,128)(2,1)S(1)}, bf16[4,3,256,128]{3,2,1,0:T(8,128)(2,1)S(1)}, u32[]{:S(2)}, u32[]{:S(2)}) collective-permute-start(bf16[4,3,256,128]{3,2,1,0:T(8,128)(2,1)S(1)} %collective-permute-done.10.rest_3_), channel_id=1, source_target_pairs={{1,8},{8,1},{3,10},{10,3},{5,12},{12,5},{7,14},{14,7},{9,16},{16,9... | collective-permute-start | bytes 2359304 | tf_op jit(solution)/shard_map/ppermute | solution.py:294
  102.0 60.7 %copy-start.19 = (bf16[4,3,272,128]{3,2,1,0:T(8,128)(2,1)}, bf16[4,3,272,128]{3,2,1,0:T(8,128)(2,1)S(1)}, u32[]{:S(2)}) copy-start(bf16[4,3,272,128]{3,2,1,0:T(8,128)(2,1)S(1)} %collective-permute-done.22.rest_3_) | copy-start | bytes 2506756
  102.0 34.5 %collective-permute-start.14 = (bf16[4,3,256,128]{3,2,1,0:T(8,128)(2,1)S(1)}, bf16[4,3,256,128]{3,2,1,0:T(8,128)(2,1)S(1)}, u32[]{:S(2)}, u32[]{:S(2)}) collective-permute-start(bf16[4,3,256,128]{3,2,1,0:T(8,128)(2,1)S(1)} %collective-permute-done.13.rest_6_), channel_id=1, source_target_pairs={{0,1},{1,0},{2,3},{3,2},{4,5},{5,4},{6,7},{7,6},{8,9},{9,8},{10,11... | collective-permute-start | bytes 2359304 | tf_op jit(solution)/shard_map/ppermute | solution.py:293
  128.5 13.3 %collective-permute-start.15 = (bf16[4,3,256,128]{3,2,1,0:T(8,128)(2,1)S(1)}, bf16[4,3,256,128]{3,2,1,0:T(8,128)(2,1)S(1)}, u32[]{:S(2)}, u32[]{:S(2)}) collective-permute-start(bf16[4,3,256,128]{3,2,1,0:T(8,128)(2,1)S(1)} %collective-permute-done.13.rest_6_), channel_id=1, source_target_pairs={{1,8},{8,1},{3,10},{10,3},{5,12},{12,5},{7,14},{14,7},{9,16},{16,9... | collective-permute-start | bytes 2359304 | tf_op jit(solution)/shard_map/ppermute | solution.py:294
  130.8 11.0 %copy-start.20 = (bf16[4,3,272,128]{3,2,1,0:T(8,128)(2,1)}, bf16[4,3,272,128]{3,2,1,0:T(8,128)(2,1)S(1)}, u32[]{:S(2)}) copy-start(bf16[4,3,272,128]{3,2,1,0:T(8,128)(2,1)S(1)} %collective-permute-done.20.rest_1_) | copy-start | bytes 2506756
  130.8 32.9 %collective-permute-start.21 = (bf16[4,3,272,128]{3,2,1,0:T(8,128)(2,1)S(1)}, bf16[4,3,272,128]{3,2,1,0:T(8,128)(2,1)}, u32[]{:S(2)}, u32[]{:S(2)}) collective-permute-start(bf16[4,3,272,128]{3,2,1,0:T(8,128)(2,1)S(1)} %pad_maximum_fusion.own.rest_0_), channel_id=1, source_target_pairs={{1,8},{8,1},{3,10},{10,3},{5,12},{12,5},{7,14},{14,7},{9,16},{16,9... | collective-permute-start | bytes 2506760 | tf_op jit(solution)/shard_map/ppermute | solution.py:294
  134.1 10.6 %copy-start.6 = (bf16[4,3,256,128]{3,2,1,0:T(8,128)(2,1)}, bf16[4,3,256,128]{3,2,1,0:T(8,128)(2,1)S(1)}, u32[]{:S(2)}) copy-start(bf16[4,3,256,128]{3,2,1,0:T(8,128)(2,1)S(1)} %collective-permute-done.11.rest_4_) | copy-start | bytes 2359300
  134.1 30.4 %collective-permute-start.23 = (bf16[4,3,272,128]{3,2,1,0:T(8,128)(2,1)S(1)}, bf16[4,3,272,128]{3,2,1,0:T(8,128)(2,1)}, u32[]{:S(2)}, u32[]{:S(2)}) collective-permute-start(bf16[4,3,272,128]{3,2,1,0:T(8,128)(2,1)S(1)} %collective-permute-done.22.rest_3_), channel_id=1, source_target_pairs={{0,1},{1,0},{2,3},{3,2},{4,5},{5,4},{6,7},{7,6},{8,9},{9,8},{10,11... | collective-permute-start | bytes 2506760 | tf_op jit(solution)/shard_map/ppermute | solution.py:293
  134.2 10.4 %copy-start.7 = (bf16[4,3,256,128]{3,2,1,0:T(8,128)(2,1)}, bf16[4,3,256,128]{3,2,1,0:T(8,128)(2,1)S(1)}, u32[]{:S(2)}) copy-start(bf16[4,3,256,128]{3,2,1,0:T(8,128)(2,1)S(1)} %collective-permute-done.12.rest_5_) | copy-start | bytes 2359300
  134.2 37.3 %collective-permute-start.24 = (bf16[4,3,272,128]{3,2,1,0:T(8,128)(2,1)S(1)}, bf16[4,3,272,128]{3,2,1,0:T(8,128)(2,1)}, u32[]{:S(2)}, u32[]{:S(2)}) collective-permute-start(bf16[4,3,272,128]{3,2,1,0:T(8,128)(2,1)S(1)} %collective-permute-done.22.rest_3_), channel_id=1, source_target_pairs={{1,8},{8,1},{3,10},{10,3},{5,12},{12,5},{7,14},{14,7},{9,16},{16,9... | collective-permute-start | bytes 2506760 | tf_op jit(solution)/shard_map/ppermute | solution.py:294
  136.6 8.1 %copy-start.8 = (bf16[4,3,256,128]{3,2,1,0:T(8,128)(2,1)}, bf16[4,3,256,128]{3,2,1,0:T(8,128)(2,1)S(1)}, u32[]{:S(2)}) copy-start(bf16[4,3,256,128]{3,2,1,0:T(8,128)(2,1)S(1)} %collective-permute-done.14.rest_7_) | copy-start | bytes 2359300
  136.6 36.6 %collective-permute-start.26 = (bf16[4,3,272,128]{3,2,1,0:T(8,128)(2,1)}, bf16[4,3,272,128]{3,2,1,0:T(8,128)(2,1)}, u32[]{:S(2)}, u32[]{:S(2)}) collective-permute-start(bf16[4,3,272,128]{3,2,1,0:T(8,128)(2,1)} %collective-permute-done.25.rest_6_), channel_id=1, source_target_pairs={{0,1},{1,0},{2,3},{3,2},{4,5},{5,4},{6,7},{7,6},{8,9},{9,8},{10,11... | collective-permute-start | bytes 2506760 | tf_op jit(solution)/shard_map/ppermute | solution.py:293
  141.8 2.9 %copy-start.9 = (bf16[4,3,256,128]{3,2,1,0:T(8,128)(2,1)}, bf16[4,3,256,128]{3,2,1,0:T(8,128)(2,1)S(1)}, u32[]{:S(2)}) copy-start(bf16[4,3,256,128]{3,2,1,0:T(8,128)(2,1)S(1)} %collective-permute-done.15.rest_8_) | copy-start | bytes 2359300
  141.8 31.4 %collective-permute-start.27 = (bf16[4,3,272,128]{3,2,1,0:T(8,128)(2,1)}, bf16[4,3,272,128]{3,2,1,0:T(8,128)(2,1)}, u32[]{:S(2)}, u32[]{:S(2)}) collective-permute-start(bf16[4,3,272,128]{3,2,1,0:T(8,128)(2,1)} %collective-permute-done.25.rest_6_), channel_id=1, source_target_pairs={{1,8},{8,1},{3,10},{10,3},{5,12},{12,5},{7,14},{14,7},{9,16},{16,9... | collective-permute-start | bytes 2506760 | tf_op jit(solution)/shard_map/ppermute | solution.py:294
  163.8 30.2 %collective-permute-start.16 = (bf16[3,128,128]{2,1,0:T(8,128)(2,1)S(1)}, bf16[3,128,128]{2,1,0:T(8,128)(2,1)S(1)}, u32[]{:S(2)}, u32[]{:S(2)}) collective-permute-start(bf16[3,128,128]{2,1,0:T(8,128)(2,1)S(1)} %get-tuple-element.33), channel_id=1, source_target_pairs={{0,0},{2,1},{4,2},{6,3},{1,4},{3,5},{5,6},{7,7},{8,8},{10,9},{12,1... | collective-permute-start | bytes 294920 | tf_op jit(solution)/shard_map/ppermute | solution.py:281
  164.5 31.3 %collective-permute-start.17 = (bf16[3,128,128]{2,1,0:T(8,128)(2,1)S(1)}, bf16[3,128,128]{2,1,0:T(8,128)(2,1)S(1)}, u32[]{:S(2)}, u32[]{:S(2)}) collective-permute-start(bf16[3,128,128]{2,1,0:T(8,128)(2,1)S(1)} %get-tuple-element.32), channel_id=1, source_target_pairs={{2,0},{0,1},{6,2},{4,3},{3,4},{1,5},{7,6},{5,7},{10,8},{8,9},{14,1... | collective-permute-start | bytes 294920 | tf_op jit(solution)/shard_map/ppermute | solution.py:281
  171.5 26.2 %collective-permute-start.18 = (bf16[3,128,128]{2,1,0:T(8,128)(2,1)S(1)}, bf16[3,128,128]{2,1,0:T(8,128)(2,1)S(1)}, u32[]{:S(2)}, u32[]{:S(2)}) collective-permute-start(bf16[3,128,128]{2,1,0:T(8,128)(2,1)S(1)} %get-tuple-element.31), channel_id=1, source_target_pairs={{4,0},{6,1},{0,2},{2,3},{5,4},{7,5},{1,6},{3,7},{12,8},{14,9},{8,1... | collective-permute-start | bytes 294920 | tf_op jit(solution)/shard_map/ppermute | solution.py:281
  189.3 23.4 %collective-permute-start.28 = (bf16[3,256,128]{2,1,0:T(8,128)(2,1)S(1)}, bf16[3,256,128]{2,1,0:T(8,128)(2,1)S(1)}, u32[]{:S(2)}, u32[]{:S(2)}) collective-permute-start(bf16[3,256,128]{2,1,0:T(8,128)(2,1)S(1)} %get-tuple-element.29), channel_id=1, source_target_pairs={{0,0},{2,1},{4,2},{6,3},{1,4},{3,5},{5,6},{7,7},{8,8},{10,9},{12,1... | collective-permute-start | bytes 589832 | tf_op jit(solution)/shard_map/ppermute | solution.py:281
  190.0 22.7 %collective-permute-start.29 = (bf16[3,256,128]{2,1,0:T(8,128)(2,1)S(1)}, bf16[3,256,128]{2,1,0:T(8,128)(2,1)S(1)}, u32[]{:S(2)}, u32[]{:S(2)}) collective-permute-start(bf16[3,256,128]{2,1,0:T(8,128)(2,1)S(1)} %get-tuple-element.28), channel_id=1, source_target_pairs={{2,0},{0,1},{6,2},{4,3},{3,4},{1,5},{7,6},{5,7},{10,8},{8,9},{14,1... | collective-permute-start | bytes 589832 | tf_op jit(solution)/shard_map/ppermute | solution.py:281
  194.0 16.0 %copy-start.14 = (bf16[3,128,128]{2,1,0:T(8,128)(2,1)}, bf16[3,128,128]{2,1,0:T(8,128)(2,1)S(1)}, u32[]{:S(2)}) copy-start(bf16[3,128,128]{2,1,0:T(8,128)(2,1)S(1)} %collective-permute-done.16.rest_0_) | copy-start | bytes 294916
  194.0 18.7 %collective-permute-start.30 = (bf16[3,256,128]{2,1,0:T(8,128)(2,1)S(1)}, bf16[3,256,128]{2,1,0:T(8,128)(2,1)S(1)}, u32[]{:S(2)}, u32[]{:S(2)}) collective-permute-start(bf16[3,256,128]{2,1,0:T(8,128)(2,1)S(1)} %get-tuple-element.27), channel_id=1, source_target_pairs={{4,0},{6,1},{0,2},{2,3},{5,4},{7,5},{1,6},{3,7},{12,8},{14,9},{8,1... | collective-permute-start | bytes 589832 | tf_op jit(solution)/shard_map/ppermute | solution.py:281
  195.7 14.3 %copy-start.15 = (bf16[3,128,128]{2,1,0:T(8,128)(2,1)}, bf16[3,128,128]{2,1,0:T(8,128)(2,1)S(1)}, u32[]{:S(2)}) copy-start(bf16[3,128,128]{2,1,0:T(8,128)(2,1)S(1)} %collective-permute-done.17.rest_1_) | copy-start | bytes 294916
  195.7 17.0 %collective-permute-start.31 = (bf16[3,256,128]{2,1,0:T(8,128)(2,1)S(1)}, bf16[3,256,128]{2,1,0:T(8,128)(2,1)S(1)}, u32[]{:S(2)}, u32[]{:S(2)}) collective-permute-start(bf16[3,256,128]{2,1,0:T(8,128)(2,1)S(1)} %get-tuple-element.26), channel_id=1, source_target_pairs={{6,0},{4,1},{2,2},{0,3},{7,4},{5,5},{3,6},{1,7},{14,8},{12,9},{10,... | collective-permute-start | bytes 589832 | tf_op jit(solution)/shard_map/ppermute | solution.py:281
  197.6 12.4 %copy-start.16 = (bf16[3,128,128]{2,1,0:T(8,128)(2,1)}, bf16[3,128,128]{2,1,0:T(8,128)(2,1)S(1)}, u32[]{:S(2)}) copy-start(bf16[3,128,128]{2,1,0:T(8,128)(2,1)S(1)} %collective-permute-done.18.rest_2_) | copy-start | bytes 294916
  197.7 12.3 %collective-permute-start.19 = (bf16[3,128,128]{2,1,0:T(8,128)(2,1)S(1)}, bf16[3,128,128]{2,1,0:T(8,128)(2,1)S(1)}, u32[]{:S(2)}, u32[]{:S(2)}) collective-permute-start(bf16[3,128,128]{2,1,0:T(8,128)(2,1)S(1)} %get-tuple-element.30), channel_id=1, source_target_pairs={{6,0},{4,1},{2,2},{0,3},{7,4},{5,5},{3,6},{1,7},{14,8},{12,9},{10,... | collective-permute-start | bytes 294920 | tf_op jit(solution)/shard_map/ppermute | solution.py:281
  210.0 0.6 copy-start.17
  212.7 0.7 copy-start.10
  212.7 0.8 copy-start.11
  212.7 0.8 copy-start.12
  213.5 0.7 copy-start.13

commit v2 on v1

v2 whole, which is shorter than its diff:
```python
import functools
import math

import jax
import jax.numpy as jnp
from jax import lax
from jax.experimental import pallas as pl
from jax.experimental.pallas import tpu as pltpu
from jax.sharding import PartitionSpec as P

HEADS = 12
HEAD_DIM = 128
CHIPS = 16
BLOCKS = 4
FRAMES = 4
TOKENS = 128
HALF = 64
STAT_ROWS = 16
KV_ROWS = 2 * TOKENS
QD_ROWS = 2 * TOKENS + STAT_ROWS
SCALE = 1.0 / math.sqrt(HEAD_DIM)
LOG2E = math.log2(math.e)
VMEM_LIMIT = 56 * 1024 * 1024
AXES = ("frame", "space")

SMEM_SPEC = pl.BlockSpec(memory_space=pltpu.SMEM)


def vmem_specs(count):
    return [pl.BlockSpec(memory_space=pltpu.VMEM)] * count


def params():
    return pltpu.CompilerParams(vmem_limit_bytes=VMEM_LIMIT)


def keep_matrix(tile_valid, stored_dim):
    frame_valid = tile_valid[lax.axis_index("frame")]
    row_valid = tile_valid[lax.axis_size("frame") + lax.axis_index("space") // 4]
    tiled = lax.broadcasted_iota(jnp.int32, (TOKENS, TOKENS), 1 - stored_dim)
    stored = lax.broadcasted_iota(jnp.int32, (TOKENS, TOKENS), stored_dim)
    tile, frame = tiled >> 6, (tiled >> 4) & 3
    row, col = (tiled >> 2) & 3, tiled & 3
    same = stored == frame * 32 + row * 8 + tile * 4 + col
    keep = same & (frame < frame_valid) & (row < row_valid)
    return jnp.where(keep, 1.0, 0.0).astype(jnp.bfloat16)


def dot_t(a, b):
    return lax.dot_general(a, b, (((1,), (1,)), ((), ())), preferred_element_type=jnp.float32)


def dot(a, b):
    return jnp.dot(a, b, preferred_element_type=jnp.float32)


def pack_pair(matrix, first, second, out):
    for part, ref in enumerate((first, second)):
        moved = dot(matrix, ref[...]).astype(jnp.bfloat16)
        for head in range(HEADS):
            out[head, part * TOKENS : (part + 1) * TOKENS, :] = moved[
                :, head * HEAD_DIM : (head + 1) * HEAD_DIM
            ]
    out[HEADS:] = jnp.zeros((CHIPS - HEADS,) + out.shape[1:], jnp.bfloat16)


def pack_kv_kernel(tile_valid, first, second, out):
    pack_pair(keep_matrix(tile_valid, 1), first, second, out)


def pack_qd_kernel(tile_valid, first, second, log_norm, delta, out, table):
    matrix = keep_matrix(tile_valid, 1)
    pack_pair(matrix, first, second, out)
    table[...] = jnp.zeros_like(table)
    for base, stat in ((0, log_norm[...] * LOG2E), (3, delta[...])):
        left = stat
        for step in range(3):
            piece = left.astype(jnp.bfloat16)
            left = left - piece.astype(jnp.float32)
            turned = dot(matrix, piece).T
            for head in range(HEADS):
                table[head, base + step : base + step + 1, :] = turned[head : head + 1, :]
    out[:HEADS, 2 * TOKENS :, :] = table[...].astype(jnp.bfloat16)


def pack_kv(tile_valid, first, second):
    return pl.pallas_call(
        pack_kv_kernel,
        out_shape=jax.ShapeDtypeStruct((CHIPS, KV_ROWS, HEAD_DIM), jnp.bfloat16),
        in_specs=[SMEM_SPEC] + vmem_specs(2),
        out_specs=vmem_specs(1)[0],
        compiler_params=params(),
        name="pack_kv",
    )(tile_valid, first, second)


def pack_qd(tile_valid, first, second, log_norm, delta):
    return pl.pallas_call(
        pack_qd_kernel,
        out_shape=jax.ShapeDtypeStruct((CHIPS, QD_ROWS, HEAD_DIM), jnp.bfloat16),
        in_specs=[SMEM_SPEC] + vmem_specs(4),
        out_specs=vmem_specs(1)[0],
        scratch_shapes=[pltpu.VMEM((HEADS, STAT_ROWS, TOKENS), jnp.float32)],
        compiler_params=params(),
        name="pack_qd",
    )(tile_valid, first, second, log_norm, delta)


def window(column):
    pieces = []
    if column > 0:
        pieces.append((column - 1, HALF, TOKENS))
    pieces.append((column, 0, TOKENS))
    if column < BLOCKS - 1:
        pieces.append((column + 1, 0, HALF))
    return pieces


def near_rows(near, column, offset):
    parts = [near(b, offset + lo, offset + hi) for b, lo, hi in window(column)]
    return jnp.concatenate(parts, axis=0)


def near_stat(near, column, offset, base):
    parts = []
    for b, lo, hi in window(column):
        rows = near(b, offset, offset + STAT_ROWS).astype(jnp.float32)
        total = rows[base : base + 1] + rows[base + 1 : base + 2] + rows[base + 2 : base + 3]
        parts.append(total[:, lo:hi])
    return jnp.concatenate(parts, axis=1)


def tile_mask(column):
    extent = sum(hi - lo for _, lo, hi in window(column))
    skip = 1 if column > 0 else 0
    own = lax.broadcasted_iota(jnp.int32, (TOKENS, extent), 0) >> 6
    near = (lax.broadcasted_iota(jnp.int32, (TOKENS, extent), 1) >> 6) - skip
    return (own - near <= 1) & (near - own <= 1)


def reader(ref, *index):
    return lambda block, lo, hi: ref[(*index, block, slice(lo, hi), slice(None))]


def query_step(own, own_frame, nears, offset, totals):
    for column in range(BLOCKS):
        query = own[own_frame, column, :TOKENS, :]
        grad = own[own_frame, column, TOKENS : 2 * TOKENS, :]
        stat = own[own_frame, column, 2 * TOKENS :, :].astype(jnp.float32).T
        mask = tile_mask(column)
        norm = jnp.broadcast_to(stat[:, 0:1] + stat[:, 1:2] + stat[:, 2:3], mask.shape)
        delta = jnp.broadcast_to(stat[:, 3:4] + stat[:, 4:5] + stat[:, 5:6], mask.shape)
        total = totals[own_frame, column]
        for near in nears:
            keys = near_rows(near, column, offset)
            values = near_rows(near, column, offset + TOKENS)
            probs = jnp.exp2(dot_t(query, keys) * (SCALE * LOG2E) - norm)
            probs = jnp.where(mask, probs, 0.0)
            slope = probs * (dot_t(grad, values) - delta)
            total = total + dot(slope.astype(jnp.bfloat16), keys)
        totals[own_frame, column] = total


def key_step(own, own_frame, nears, offset, key_totals, value_totals):
    for column in range(BLOCKS):
        key = own[own_frame, column, :TOKENS, :]
        value = own[own_frame, column, TOKENS : 2 * TOKENS, :]
        mask = tile_mask(column)
        key_total = key_totals[own_frame, column]
        value_total = value_totals[own_frame, column]
        for near in nears:
            queries = near_rows(near, column, offset)
            grads = near_rows(near, column, offset + TOKENS)
            norm = near_stat(near, column, offset + 2 * TOKENS, 0)
            delta = near_stat(near, column, offset + 2 * TOKENS, 3)
            probs = jnp.exp2(dot_t(key, queries) * (SCALE * LOG2E) - norm)
            probs = jnp.where(mask, probs, 0.0)
            value_total = value_total + dot(probs.astype(jnp.bfloat16), grads)
            slope = probs * (dot_t(value, grads) - delta)
            key_total = key_total + dot(slope.astype(jnp.bfloat16), queries)
        key_totals[own_frame, column] = key_total
        value_totals[own_frame, column] = value_total


def frame_pairs(step):
    def body(t, carry):
        own_frame = (t + 1) // 3
        step(own_frame, t - 2 * own_frame)
        return carry

    lax.fori_loop(0, 3 * FRAMES - 2, body, 0)


def query_kernel(own, *rest):
    nears, totals = rest[:-1], rest[-1]
    totals[...] = jnp.zeros_like(totals)
    frame_pairs(
        lambda a, b: query_step(own, a, [reader(near, b) for near in nears], 0, totals)
    )


def key_kernel(own, *rest):
    nears, (key_totals, value_totals) = rest[:-2], rest[-2:]
    key_totals[...] = jnp.zeros_like(key_totals)
    value_totals[...] = jnp.zeros_like(value_totals)
    frame_pairs(
        lambda a, b: key_step(
            own, a, [reader(near, b) for near in nears], 0, key_totals, value_totals
        )
    )


def last_kernel(own_kv, own_qd, row_qd, jump_own, jump_core, jump_row, *rest):
    query_in, key_in, value_in, out, query_totals, key_totals, value_totals = rest
    query_totals[...] = query_in[...]
    key_totals[...] = key_in[...]
    value_totals[...] = value_in[...]
    frame_pairs(
        lambda a, b: key_step(own_kv, a, [reader(row_qd, b)], 0, key_totals, value_totals)
    )
    edge = jnp.where(lax.axis_index("frame") < FRAMES, FRAMES - 1, 0)
    jumped = [reader(jump_own), reader(jump_core), reader(jump_row)]
    query_step(own_qd, edge, jumped, 0, query_totals)
    key_step(own_kv, edge, jumped, KV_ROWS, key_totals, value_totals)
    for frame in range(FRAMES):
        for column in range(BLOCKS):
            high, core = column // 2, column % 2
            parts = (
                query_totals[frame, column] * SCALE,
                key_totals[frame, column] * SCALE,
                value_totals[frame, column],
            )
            for part, total in enumerate(parts):
                out[core, frame, high, part * TOKENS : (part + 1) * TOKENS, :] = total.astype(
                    jnp.bfloat16
                )


TOTALS = jax.ShapeDtypeStruct((FRAMES, BLOCKS, TOKENS, HEAD_DIM), jnp.float32)


def attend(kernel, name, args, out_shape, pairs, scratch=()):
    flops = pairs * 2 * TOKENS * HEAD_DIM * 256
    return pl.pallas_call(
        kernel,
        out_shape=out_shape,
        in_specs=vmem_specs(len(args)),
        out_specs=jax.tree.map(lambda _: vmem_specs(1)[0], out_shape),
        scratch_shapes=scratch,
        compiler_params=params(),
        cost_estimate=pl.CostEstimate(
            flops=flops * 8, bytes_accessed=6 << 20, transcendentals=pairs << 15
        ),
        name=name,
    )(*args)


def unpack_kernel(tile_valid, blocks, *outs):
    matrix = keep_matrix(tile_valid, 0)
    for part, out in enumerate(outs):
        rows = slice(part * TOKENS, (part + 1) * TOKENS)
        joined = jnp.concatenate([blocks[head, rows, :] for head in range(HEADS)], axis=1)
        out[...] = dot(matrix, joined).astype(jnp.bfloat16)


def unpack(tile_valid, blocks):
    shape = jax.ShapeDtypeStruct((TOKENS, HEADS * HEAD_DIM), jnp.bfloat16)
    return pl.pallas_call(
        unpack_kernel,
        out_shape=[shape] * 3,
        in_specs=[SMEM_SPEC] + vmem_specs(1),
        out_specs=vmem_specs(3),
        compiler_params=params(),
        name="unpack",
    )(tile_valid, blocks)


def plane_exchange(array):
    spaces = lax.axis_size("space")
    groups = []
    for half in range(lax.axis_size("frame") // FRAMES):
        for z in range(spaces // 8):
            for core in range(2):
                groups.append(
                    [
                        (half * FRAMES + j // 4) * spaces + z * 8 + (j % 4) * 2 + core
                        for j in range(CHIPS)
                    ]
                )
    return lax.all_to_all(array, AXES, 0, 0, axis_index_groups=groups)


def core_swap(array):
    return lax.ppermute(array, "space", [(s, s ^ 1) for s in range(lax.axis_size("space"))])


def row_swap(array):
    route = []
    for s in range(1, lax.axis_size("space") - 8, 2):
        if s % 2 == 1:
            route += [(s, s + 7), (s + 7, s)]
    return lax.ppermute(array, "space", route)


def half_swap(array):
    count = lax.axis_size("frame")
    return lax.ppermute(array, "frame", [(f, (f + FRAMES) % count) for f in range(count)])


def two_ways(core, mine, other, axis):
    first = jnp.where(core == 0, mine, other)
    second = jnp.where(core == 0, other, mine)
    return jnp.stack([first, second], axis=axis)


def spread(packed, core):
    arrived = plane_exchange(packed).reshape(FRAMES, 2, 2, *packed.shape[1:])
    mine = lax.dynamic_index_in_dim(arrived, core, 1, keepdims=False)
    other = lax.dynamic_index_in_dim(arrived, 1 - core, 1, keepdims=False)
    whole = two_ways(core, mine, core_swap(other), 2)
    return whole.reshape(FRAMES, BLOCKS, *packed.shape[1:])


def shards(query, key, value, grad_out, log_norm, delta, tile_valid):
    core = lax.axis_index("space") % 2
    edge = jnp.where(lax.axis_index("frame") < FRAMES, FRAMES - 1, 0)
    shape = query.shape

    def flat(array):
        return array.reshape(TOKENS, array.shape[-1])

    own_kv = spread(pack_kv(tile_valid, flat(key), flat(value)), core)
    own_qd = spread(
        pack_qd(tile_valid, flat(query), flat(grad_out), flat(log_norm), flat(delta)), core
    )
    row_kv = row_swap(own_kv)
    core_kv = core_swap(own_kv)
    border = jnp.concatenate(
        [
            lax.dynamic_index_in_dim(own_kv, edge, 0, keepdims=False),
            lax.dynamic_index_in_dim(own_qd, edge, 0, keepdims=False),
        ],
        axis=1,
    )
    jump_own = half_swap(border)
    core_qd = core_swap(own_qd)
    row_qd = row_swap(own_qd)
    jump_core = core_swap(jump_own)
    jump_row = row_swap(jump_own)

    query_part = attend(
        query_kernel, "query_side", (own_qd, own_kv, core_kv, row_kv), TOTALS, 360
    )
    key_part, value_part = attend(
        key_kernel, "key_side", (own_kv, own_qd, core_qd), [TOTALS] * 2, 320
    )
    grads = attend(
        last_kernel,
        "last_part",
        (own_kv, own_qd, row_qd, jump_own, jump_core, jump_row, query_part, key_part, value_part),
        jax.ShapeDtypeStruct((2, FRAMES, 2, 3 * TOKENS, HEAD_DIM), jnp.bfloat16),
        240,
        [pltpu.VMEM(TOTALS.shape, TOTALS.dtype)] * 3,
    )
    mine = lax.dynamic_index_in_dim(grads, core, 0, keepdims=False)
    other = lax.dynamic_index_in_dim(grads, 1 - core, 0, keepdims=False)
    whole = two_ways(core, mine, core_swap(other), 1)
    blocks = plane_exchange(whole.reshape(CHIPS, 3 * TOKENS, HEAD_DIM))
    return tuple(out.reshape(shape) for out in unpack(tile_valid, blocks))


def solution(mesh):
    blocks = P("frame", "space", None, None, None)
    return jax.shard_map(
        shards,
        mesh=mesh,
        in_specs=(blocks,) * 6 + (P(),),
        out_specs=(blocks,) * 3,
        check_vma=False,
    )
```

time: 217 us -> 196 us (0.903)
  the two profiles are of different devices: /device:TPU:192 before, /device:TPU:1 now
where the time goes in v2:
time: 196 us; the launch traced here: 193 us
  Pallas kernels  69.1 us (35%)
  waiting for transfers between devices  53.6 us (27%)
  starting transfers between devices  36.5 us (19%)
  blocking collectives  25.9 us (13%)
  local copies, waits for them, and re-layouts  5.37 us (3%)
    pallas_call x3, Pallas kernels, attend(): pl.pallas_call(kernel, out_shape=out_shape, in_specs=vmem_specs(len(args)...  61.3 us
    all_to_all x2, waiting for transfers between devices, plane_exchange(): return lax.all_to_all(array, AXES, 0, 0, axis_index_groups=groups)  26.1 us
    all_to_all x1, blocking collectives, plane_exchange(): return lax.all_to_all(array, AXES, 0, 0, axis_index_groups=groups)  25.9 us
    ppermute x1, waiting for transfers between devices, half_swap(): lax.ppermute(array, 'frame', [(f, (f + FRAMES) % count) for f in range(co...  25.2 us
    ppermute x3, starting transfers between devices, row_swap(): return lax.ppermute(array, 'space', route)  11.8 us
    all_to_all x2, starting transfers between devices, plane_exchange(): return lax.all_to_all(array, AXES, 0, 0, axis_index_groups=groups)  11.8 us
    ppermute x6, starting transfers between devices, core_swap(): lax.ppermute(array, 'space', [(s, s ^ 1) for s in range(lax.axis_size('sp...  6.82 us
    ppermute x1, starting transfers between devices, half_swap(): lax.ppermute(array, 'frame', [(f, (f + FRAMES) % count) for f in range(co...  6.1 us
  transfers between devices with their start and end apart: 12, of which 4 were waited for; matrix products, arithmetic and copies ran while one was open for 1% of the time, Pallas kernels for 24%

profile of v2, /device:TPU:1, one launch (start us, length us, event | category | flops | bytes accessed | tf_op | source)
XLA Modules:
  0.0 193.0 jit_solution(14740895755570343928)
XLA Ops:
  0.6 2.5 %pack_kv.1 = bf16[16,256,128]{2,1,0:T(8,128)(2,1)} custom-call(s32[16]{0:T(128)} %tile_valid.5, bf16[128,1536]{1,0:T(8,128)(2,1)} %bitcast.88, bf16[128,1536]{1,0:T(8,128)(2,1)} %bitcast.89), custom_call_target="tpu_custom_call" | custom-call | tf_op jit(solution)/shard_map/pack_kv/pallas_call | solution.py:87
  3.1 7.6 %all-to-all-start = ((bf16[16,256,128]{2,1,0:T(8,128)(2,1)}), bf16[16,256,128]{2,1,0:T(8,128)(2,1)S(1)}, u32[]{:S(2)}, u32[]{:S(2)}) async-start(bf16[16,256,128]{2,1,0:T(8,128)(2,1)} %pack_kv.1), calls=%async_computation | async-start | bytes 2097152 | tf_op jit(solution)/shard_map/all_to_all | solution.py:290
  10.7 2.7 %pack_qd.1 = bf16[16,272,128]{2,1,0:T(8,128)(2,1)} custom-call(s32[16]{0:T(128)} %tile_valid.5, bf16[128,1536]{1,0:T(8,128)(2,1)} %bitcast.86, bf16[128,1536]{1,0:T(8,128)(2,1)} %bitcast.87, f32[128,12]{1,0:T(8,128)} %bitcast.90, f32[128,12]{1,0:T(8,128)} %bitcast.91), custom_call_target="tpu_custom_call" | custom-call | tf_op jit(solution)/shard_map/pack_qd/pallas_call | solution.py:98
  13.4 13.3 %all-to-all-done = bf16[16,256,128]{2,1,0:T(8,128)(2,1)S(1)} async-done(((bf16[16,256,128]{2,1,0:T(8,128)(2,1)}), bf16[16,256,128]{2,1,0:T(8,128)(2,1)S(1)}, u32[]{:S(2)}, u32[]{:S(2)}) %all-to-all-start) | async-done | bytes 1048608 | tf_op jit(solution)/shard_map/all_to_all | solution.py:290
  26.7 4.2 %all-to-all-start.1 = ((bf16[16,272,128]{2,1,0:T(8,128)(2,1)}), bf16[16,272,128]{2,1,0:T(8,128)(2,1)S(1)}, u32[]{:S(2)}, u32[]{:S(2)}) async-start(bf16[16,272,128]{2,1,0:T(8,128)(2,1)} %pack_qd.1), calls=%async_computation.1 | async-start | bytes 2228224 | tf_op jit(solution)/shard_map/all_to_all | solution.py:290
  30.9 0.9 dynamic-slice_bitcast_fusion.2
  31.7 2.1 %collective-permute-start = (bf16[4,2,256,128]{3,2,1,0:T(8,128)(2,1)}, bf16[4,2,256,128]{3,2,1,0:T(8,128)(2,1)}, u32[]{:S(2)}, u32[]{:S(2)}) collective-permute-start(bf16[4,2,256,128]{3,2,1,0:T(8,128)(2,1)} %dynamic-slice_bitcast_fusion.2), channel_id=1, source_target_pairs={{0,1},{1,0},{2,3},{3,2},{4,5},{5,4},{6,7},{7,6},{8,9},{9,8},{10,11... | collective-permute-start | bytes 1572872 | tf_op jit(solution)/shard_map/ppermute | solution.py:294
  33.9 12.7 %all-to-all-done.1 = bf16[16,272,128]{2,1,0:T(8,128)(2,1)S(1)} async-done(((bf16[16,272,128]{2,1,0:T(8,128)(2,1)}), bf16[16,272,128]{2,1,0:T(8,128)(2,1)S(1)}, u32[]{:S(2)}, u32[]{:S(2)}) %all-to-all-start.1) | async-done | bytes 1114144 | tf_op jit(solution)/shard_map/all_to_all | solution.py:290
  46.6 3.5 %collective-permute-start.1 = (bf16[4,2,272,128]{3,2,1,0:T(8,128)(2,1)S(1)}, bf16[4,2,272,128]{3,2,1,0:T(8,128)(2,1)S(1)}, u32[]{:S(2)}, u32[]{:S(2)}) collective-permute-start(bf16[4,2,272,128]{3,2,1,0:T(8,128)(2,1)S(1)} %dynamic-slice_bitcast_fusion.1), channel_id=1, source_target_pairs={{0,1},{1,0},{2,3},{3,2},{4,5},{5,4},{6,7},{7,6},{8,9},{9,8},{10,11... | collective-permute-start | bytes 1671176 | tf_op jit(solution)/shard_map/ppermute | solution.py:294
  50.1 0.0 collective-permute-done
  50.1 1.1 fusion.4
  51.3 0.1 pad_maximum_fusion.2
  51.4 0.0 copy-start.1
  51.4 3.5 %collective-permute-start.7 = (bf16[4,4,256,128]{3,2,1,0:T(8,128)(2,1)S(1)}, bf16[4,4,256,128]{3,2,1,0:T(8,128)(2,1)S(1)}, u32[]{:S(2)}, u32[]{:S(2)}) collective-permute-start(bf16[4,4,256,128]{3,2,1,0:T(8,128)(2,1)S(1)} %bitcast.80), channel_id=1, source_target_pairs={{1,8},{8,1},{3,10},{10,3},{5,12},{12,5},{7,14},{14,7},{9,16},{16,9... | collective-permute-start | bytes 3145736 | tf_op jit(solution)/shard_map/ppermute | solution.py:302
  54.9 0.1 collective-permute-start.6
  55.0 0.0 collective-permute-done.1
  55.0 0.1 fusion.2
  55.1 0.0 copy-done.1
  55.1 0.1 pad_maximum_fusion.1
  55.2 0.0 copy-start
  55.3 6.1 %collective-permute-start.3 = (bf16[4,528,128]{2,1,0:T(8,128)(2,1)S(1)}, bf16[4,528,128]{2,1,0:T(8,128)(2,1)S(1)}, u32[]{:S(2)}, u32[]{:S(2)}) collective-permute-start(bf16[4,528,128]{2,1,0:T(8,128)(2,1)S(1)} %pad_maximum_fusion.3), channel_id=1, source_target_pairs={{0,128},{32,160},{64,192},{96,224},{128,0},{160,32},{192,64},{224,... | collective-permute-start | bytes 1622024 | tf_op jit(solution)/shard_map/ppermute | solution.py:307
  61.4 0.7 collective-permute-start.8
  62.2 2.7 %collective-permute-start.2 = (bf16[4,4,272,128]{3,2,1,0:T(8,128)(2,1)S(1)}, bf16[4,4,272,128]{3,2,1,0:T(8,128)(2,1)S(1)}, u32[]{:S(2)}, u32[]{:S(2)}) collective-permute-start(bf16[4,4,272,128]{3,2,1,0:T(8,128)(2,1)S(1)} %bitcast.76), channel_id=1, source_target_pairs={{1,8},{8,1},{3,10},{10,3},{5,12},{12,5},{7,14},{14,7},{9,16},{16,9... | collective-permute-start | bytes 3342344 | tf_op jit(solution)/shard_map/ppermute | solution.py:302
  64.9 25.2 %collective-permute-done.3.jump_own = bf16[4,528,128]{2,1,0:T(8,128)(2,1)S(1)} collective-permute-done((bf16[4,528,128]{2,1,0:T(8,128)(2,1)S(1)}, bf16[4,528,128]{2,1,0:T(8,128)(2,1)S(1)}, u32[]{:S(2)}, u32[]{:S(2)}) %collective-permute-start.3) | collective-permute-done | bytes 540704 | tf_op jit(solution)/shard_map/ppermute | solution.py:307
  90.1 0.0 copy-start.6
  90.1 5.6 %collective-permute-start.5 = (bf16[4,528,128]{2,1,0:T(8,128)(2,1)S(1)}, bf16[4,528,128]{2,1,0:T(8,128)(2,1)S(1)}, u32[]{:S(2)}, u32[]{:S(2)}) collective-permute-start(bf16[4,528,128]{2,1,0:T(8,128)(2,1)S(1)} %collective-permute-done.3.jump_own), channel_id=1, source_target_pairs={{1,8},{8,1},{3,10},{10,3},{5,12},{12,5},{7,14},{14,7},{9,16},{16,9... | collective-permute-start | bytes 1622024 | tf_op jit(solution)/shard_map/ppermute | solution.py:302
  95.8 0.0 collective-permute-done.7.rest_2_
  95.8 0.0 copy-start.5
  95.8 0.3 collective-permute-start.4
  96.1 0.0 collective-permute-done.6.rest_1_
  96.1 0.0 copy-done
  96.1 0.7 copy-done.5
  96.8 23.8 %query_side.1.rest_0_ = f32[4,4,128,128]{3,2,1,0:T(8,128)} custom-call(bf16[4,4,272,128]{3,2,1,0:T(8,128)(2,1)} %bitcast.77, bf16[4,4,256,128]{3,2,1,0:T(8,128)(2,1)} %bitcast.83, bf16[4,4,256,128]{3,2,1,0:T(8,128)(2,1)} %collective-permute-done.6.rest_1_, bf16[4,4,256,128]{3,2,1,0:T(8,128)(2,1)} %copy-done.5), custom_call_target="tpu_custom_call" | custom-call | flops 24159191040 | bytes 6291456 | tf_op jit(solution)/shard_map/query_side/pallas_call | solution.py:244
  120.6 0.0 copy-done.6
  120.6 0.0 collective-permute-done.8.rest_1_
  120.6 0.0 copy-start.4
  120.6 1.0 copy-done.4
  121.6 18.9 %key_side.1 = (f32[4,4,128,128]{3,2,1,0:T(8,128)}, f32[4,4,128,128]{3,2,1,0:T(8,128)}) custom-call(bf16[4,4,256,128]{3,2,1,0:T(8,128)(2,1)} %bitcast.84, bf16[4,4,272,128]{3,2,1,0:T(8,128)(2,1)} %bitcast.78, bf16[4,4,272,128]{3,2,1,0:T(8,128)(2,1)} %copy-done.4), custom_call_target="tpu_custom_call" | custom-call | flops 21474836480 | bytes 6291456 | tf_op jit(solution)/shard_map/key_side/pallas_call | solution.py:244
  140.5 0.0 collective-permute-done.5.jump_row
  140.5 0.0 copy-start.7
  140.5 0.0 collective-permute-done.4.jump_core
  140.5 0.0 copy-start.8
  140.5 0.0 collective-permute-done.2.row_qd
  140.6 0.0 copy-start.3
  140.6 0.8 copy-done.7
  141.3 0.2 copy-done.8
  141.5 0.4 copy-done.3
  142.0 18.6 %last_part.1 = bf16[2,4,2,384,128]{4,3,2,1,0:T(8,128)(2,1)} custom-call(bf16[4,4,256,128]{3,2,1,0:T(8,128)(2,1)} %bitcast.85, bf16[4,4,272,128]{3,2,1,0:T(8,128)(2,1)} %bitcast.79, bf16[4,4,272,128]{3,2,1,0:T(8,128)(2,1)} %copy-done.3, bf16[4,528,128]{2,1,0:T(8,128)(2,1)} %copy-done.6, bf16[4,528,128]{2,1,0:T(8,128)(2,1)} %copy-done.8, ...), custom_call_target="tpu_custom_call" | custom-call | flops 16106127360 | bytes 6291456 | tf_op jit(solution)/shard_map/last_part/pallas_call | solution.py:244
  160.5 0.0 copy-start.2
  160.5 1.3 dynamic-slice_bitcast_fusion
  161.8 0.1 collective-permute-start.9
  161.9 2.3 %collective-permute-done.9 = bf16[4,2,384,128]{3,2,1,0:T(8,128)(2,1)S(1)} collective-permute-done((bf16[4,2,384,128]{3,2,1,0:T(8,128)(2,1)S(1)}, bf16[4,2,384,128]{3,2,1,0:T(8,128)(2,1)S(1)}, u32[]{:S(2)}, u32[]{:S(2)}) %collective-permute-start.9) | collective-permute-done | bytes 786464 | tf_op jit(solution)/shard_map/ppermute | solution.py:294
  164.2 0.0 copy-done.2
  164.2 0.1 fusion
  164.3 0.1 pad_maximum_fusion
  164.5 25.9 %all_to_all.15.blocks = bf16[16,384,128]{2,1,0:T(8,128)(2,1)} all-to-all(bf16[16,384,128]{2,1,0:T(8,128)(2,1)S(1)} %bitcast.69), channel_id=1, replica_groups={{0,2,4,6,32,34,36,38,64,66,68,70,96,98,100,102},{1,3,5,7,33,35,37,39,65..., dimensions={0} | all-to-all | bytes 3145728 | tf_op jit(solution)/shard_map/all_to_all | solution.py:290
  190.3 2.7 %unpack.1 = (bf16[128,1536]{1,0:T(8,128)(2,1)}, bf16[128,1536]{1,0:T(8,128)(2,1)}, bf16[128,1536]{1,0:T(8,128)(2,1)}) custom-call(s32[16]{0:T(128)} %tile_valid.5, bf16[16,384,128]{2,1,0:T(8,128)(2,1)} %all_to_all.15.blocks), custom_call_target="tpu_custom_call" | custom-call | tf_op jit(solution)/shard_map/unpack/pallas_call | solution.py:268
  (4 shorter events, 0.1 us)
Async XLA Ops:
  3.1 23.6 %all-to-all-start = ((bf16[16,256,128]{2,1,0:T(8,128)(2,1)}), bf16[16,256,128]{2,1,0:T(8,128)(2,1)S(1)}, u32[]{:S(2)}, u32[]{:S(2)}) async-start(bf16[16,256,128]{2,1,0:T(8,128)(2,1)} %pack_kv.1), calls=%async_computation | async-start | bytes 2097152 | tf_op jit(solution)/shard_map/all_to_all | solution.py:290
  26.7 19.9 %all-to-all-start.1 = ((bf16[16,272,128]{2,1,0:T(8,128)(2,1)}), bf16[16,272,128]{2,1,0:T(8,128)(2,1)S(1)}, u32[]{:S(2)}, u32[]{:S(2)}) async-start(bf16[16,272,128]{2,1,0:T(8,128)(2,1)} %pack_qd.1), calls=%async_computation.1 | async-start | bytes 2228224 | tf_op jit(solution)/shard_map/all_to_all | solution.py:290
  31.7 18.4 %collective-permute-start = (bf16[4,2,256,128]{3,2,1,0:T(8,128)(2,1)}, bf16[4,2,256,128]{3,2,1,0:T(8,128)(2,1)}, u32[]{:S(2)}, u32[]{:S(2)}) collective-permute-start(bf16[4,2,256,128]{3,2,1,0:T(8,128)(2,1)} %dynamic-slice_bitcast_fusion.2), channel_id=1, source_target_pairs={{0,1},{1,0},{2,3},{3,2},{4,5},{5,4},{6,7},{7,6},{8,9},{9,8},{10,11... | collective-permute-start | bytes 1572872 | tf_op jit(solution)/shard_map/ppermute | solution.py:294
  46.6 8.4 %collective-permute-start.1 = (bf16[4,2,272,128]{3,2,1,0:T(8,128)(2,1)S(1)}, bf16[4,2,272,128]{3,2,1,0:T(8,128)(2,1)S(1)}, u32[]{:S(2)}, u32[]{:S(2)}) collective-permute-start(bf16[4,2,272,128]{3,2,1,0:T(8,128)(2,1)S(1)} %dynamic-slice_bitcast_fusion.1), channel_id=1, source_target_pairs={{0,1},{1,0},{2,3},{3,2},{4,5},{5,4},{6,7},{7,6},{8,9},{9,8},{10,11... | collective-permute-start | bytes 1671176 | tf_op jit(solution)/shard_map/ppermute | solution.py:294
  51.4 3.8 %copy-start.1 = (bf16[4,2,2,256,128]{4,3,2,1,0:T(8,128)(2,1)}, bf16[4,2,2,256,128]{4,3,2,1,0:T(8,128)(2,1)S(1)}, u32[]{:S(2)}) copy-start(bf16[4,2,2,256,128]{4,3,2,1,0:T(8,128)(2,1)S(1)} %pad_maximum_fusion.2) | copy-start | bytes 3145732
  51.4 44.4 %collective-permute-start.7 = (bf16[4,4,256,128]{3,2,1,0:T(8,128)(2,1)S(1)}, bf16[4,4,256,128]{3,2,1,0:T(8,128)(2,1)S(1)}, u32[]{:S(2)}, u32[]{:S(2)}) collective-permute-start(bf16[4,4,256,128]{3,2,1,0:T(8,128)(2,1)S(1)} %bitcast.80), channel_id=1, source_target_pairs={{1,8},{8,1},{3,10},{10,3},{5,12},{12,5},{7,14},{14,7},{9,16},{16,9... | collective-permute-start | bytes 3145736 | tf_op jit(solution)/shard_map/ppermute | solution.py:302
  54.9 41.2 %collective-permute-start.6 = (bf16[4,4,256,128]{3,2,1,0:T(8,128)(2,1)S(1)}, bf16[4,4,256,128]{3,2,1,0:T(8,128)(2,1)}, u32[]{:S(2)}, u32[]{:S(2)}) collective-permute-start(bf16[4,4,256,128]{3,2,1,0:T(8,128)(2,1)S(1)} %bitcast.81), channel_id=1, source_target_pairs={{0,1},{1,0},{2,3},{3,2},{4,5},{5,4},{6,7},{7,6},{8,9},{9,8},{10,11... | collective-permute-start | bytes 3145736 | tf_op jit(solution)/shard_map/ppermute | solution.py:294
  55.2 40.8 %copy-start = (bf16[4,2,2,272,128]{4,3,2,1,0:T(8,128)(2,1)}, bf16[4,2,2,272,128]{4,3,2,1,0:T(8,128)(2,1)S(1)}, u32[]{:S(2)}) copy-start(bf16[4,2,2,272,128]{4,3,2,1,0:T(8,128)(2,1)S(1)} %pad_maximum_fusion.1) | copy-start | bytes 3342340
  55.3 34.8 %collective-permute-start.3 = (bf16[4,528,128]{2,1,0:T(8,128)(2,1)S(1)}, bf16[4,528,128]{2,1,0:T(8,128)(2,1)S(1)}, u32[]{:S(2)}, u32[]{:S(2)}) collective-permute-start(bf16[4,528,128]{2,1,0:T(8,128)(2,1)S(1)} %pad_maximum_fusion.3), channel_id=1, source_target_pairs={{0,128},{32,160},{64,192},{96,224},{128,0},{160,32},{192,64},{224,... | collective-permute-start | bytes 1622024 | tf_op jit(solution)/shard_map/ppermute | solution.py:307
  61.4 59.2 %collective-permute-start.8 = (bf16[4,4,272,128]{3,2,1,0:T(8,128)(2,1)S(1)}, bf16[4,4,272,128]{3,2,1,0:T(8,128)(2,1)S(1)}, u32[]{:S(2)}, u32[]{:S(2)}) collective-permute-start(bf16[4,4,272,128]{3,2,1,0:T(8,128)(2,1)S(1)} %bitcast.75), channel_id=1, source_target_pairs={{0,1},{1,0},{2,3},{3,2},{4,5},{5,4},{6,7},{7,6},{8,9},{9,8},{10,11... | collective-permute-start | bytes 3342344 | tf_op jit(solution)/shard_map/ppermute | solution.py:294
  62.2 78.4 %collective-permute-start.2 = (bf16[4,4,272,128]{3,2,1,0:T(8,128)(2,1)S(1)}, bf16[4,4,272,128]{3,2,1,0:T(8,128)(2,1)S(1)}, u32[]{:S(2)}, u32[]{:S(2)}) collective-permute-start(bf16[4,4,272,128]{3,2,1,0:T(8,128)(2,1)S(1)} %bitcast.76), channel_id=1, source_target_pairs={{1,8},{8,1},{3,10},{10,3},{5,12},{12,5},{7,14},{14,7},{9,16},{16,9... | collective-permute-start | bytes 3342344 | tf_op jit(solution)/shard_map/ppermute | solution.py:302
  90.1 30.4 %copy-start.6 = (bf16[4,528,128]{2,1,0:T(8,128)(2,1)}, bf16[4,528,128]{2,1,0:T(8,128)(2,1)S(1)}, u32[]{:S(2)}) copy-start(bf16[4,528,128]{2,1,0:T(8,128)(2,1)S(1)} %collective-permute-done.3.jump_own) | copy-start | bytes 1622020
  90.1 50.4 %collective-permute-start.5 = (bf16[4,528,128]{2,1,0:T(8,128)(2,1)S(1)}, bf16[4,528,128]{2,1,0:T(8,128)(2,1)S(1)}, u32[]{:S(2)}, u32[]{:S(2)}) collective-permute-start(bf16[4,528,128]{2,1,0:T(8,128)(2,1)S(1)} %collective-permute-done.3.jump_own), channel_id=1, source_target_pairs={{1,8},{8,1},{3,10},{10,3},{5,12},{12,5},{7,14},{14,7},{9,16},{16,9... | collective-permute-start | bytes 1622024 | tf_op jit(solution)/shard_map/ppermute | solution.py:302
  95.8 1.0 copy-start.5
  95.8 44.8 %collective-permute-start.4 = (bf16[4,528,128]{2,1,0:T(8,128)(2,1)S(1)}, bf16[4,528,128]{2,1,0:T(8,128)(2,1)S(1)}, u32[]{:S(2)}, u32[]{:S(2)}) collective-permute-start(bf16[4,528,128]{2,1,0:T(8,128)(2,1)S(1)} %collective-permute-done.3.jump_own), channel_id=1, source_target_pairs={{0,1},{1,0},{2,3},{3,2},{4,5},{5,4},{6,7},{7,6},{8,9},{9,8},{10,11... | collective-permute-start | bytes 1622024 | tf_op jit(solution)/shard_map/ppermute | solution.py:294
  120.6 1.0 copy-start.4
  140.5 0.8 copy-start.7
  140.5 1.0 copy-start.8
  140.6 1.4 copy-start.3
  160.5 3.7 %copy-start.2 = (bf16[2,4,2,384,128]{4,3,2,1,0:T(8,128)(2,1)S(1)}, bf16[2,4,2,384,128]{4,3,2,1,0:T(8,128)(2,1)}, u32[]{:S(2)}) copy-start(bf16[2,4,2,384,128]{4,3,2,1,0:T(8,128)(2,1)} %last_part.1) | copy-start | bytes 4718596
  161.8 2.4 %collective-permute-start.9 = (bf16[4,2,384,128]{3,2,1,0:T(8,128)(2,1)S(1)}, bf16[4,2,384,128]{3,2,1,0:T(8,128)(2,1)S(1)}, u32[]{:S(2)}, u32[]{:S(2)}) collective-permute-start(bf16[4,2,384,128]{3,2,1,0:T(8,128)(2,1)S(1)} %dynamic-slice_bitcast_fusion), channel_id=1, source_target_pairs={{0,1},{1,0},{2,3},{3,2},{4,5},{5,4},{6,7},{7,6},{8,9},{9,8},{10,11... | collective-permute-start | bytes 2359304 | tf_op jit(solution)/shard_map/ppermute | solution.py:294

commit v3 on v2

v3 whole, which is shorter than its diff:
```python
import functools
import math

import jax
import jax.numpy as jnp
from jax import lax
from jax.experimental import pallas as pl
from jax.experimental.pallas import tpu as pltpu
from jax.sharding import PartitionSpec as P

HEADS = 12
HEAD_DIM = 128
CHIPS = 16
BLOCKS = 4
FRAMES = 4
TOKENS = 128
HALF = 64
STAT_ROWS = 16
KEY, VALUE, QUERY, GRAD, STAT = (part * TOKENS for part in range(5))
ROWS = STAT + STAT_ROWS
SCALE = 1.0 / math.sqrt(HEAD_DIM)
LOG2E = math.log2(math.e)
VMEM_LIMIT = 56 * 1024 * 1024
FILL_FLOPS = 1 << 34
AXES = ("frame", "space")

SMEM_SPEC = pl.BlockSpec(memory_space=pltpu.SMEM)


def vmem_specs(count):
    return [pl.BlockSpec(memory_space=pltpu.VMEM)] * count


def params():
    return pltpu.CompilerParams(vmem_limit_bytes=VMEM_LIMIT)


def keep_matrix(tile_valid, stored_dim):
    frame_valid = tile_valid[lax.axis_index("frame")]
    row_valid = tile_valid[lax.axis_size("frame") + lax.axis_index("space") // 4]
    tiled = lax.broadcasted_iota(jnp.int32, (TOKENS, TOKENS), 1 - stored_dim)
    stored = lax.broadcasted_iota(jnp.int32, (TOKENS, TOKENS), stored_dim)
    tile, frame = tiled >> 6, (tiled >> 4) & 3
    row, col = (tiled >> 2) & 3, tiled & 3
    same = stored == frame * 32 + row * 8 + tile * 4 + col
    keep = same & (frame < frame_valid) & (row < row_valid)
    return jnp.where(keep, 1.0, 0.0).astype(jnp.bfloat16)


def dot_t(a, b):
    return lax.dot_general(a, b, (((1,), (1,)), ((), ())), preferred_element_type=jnp.float32)


def dot(a, b):
    return jnp.dot(a, b, preferred_element_type=jnp.float32)


def pack_part(matrix, start, ref, out):
    moved = dot(matrix, ref[...]).astype(jnp.bfloat16)
    for head in range(HEADS):
        out[head, start : start + TOKENS, :] = moved[:, head * HEAD_DIM : (head + 1) * HEAD_DIM]


def fill(heads, out):
    out[:HEADS] = heads[...]
    out[HEADS:] = jnp.zeros((CHIPS - HEADS,) + out.shape[1:], jnp.bfloat16)


def pack_kernel(tile_valid, key, value, query, grad, log_norm, delta, out, filled, table):
    matrix = keep_matrix(tile_valid, 1)
    for start, ref in ((KEY, key), (VALUE, value), (QUERY, query), (GRAD, grad)):
        pack_part(matrix, start, ref, out)
    table[...] = jnp.zeros_like(table)
    for base, stat in ((0, log_norm[...] * LOG2E), (3, delta[...])):
        left = stat
        for step in range(3):
            piece = left.astype(jnp.bfloat16)
            left = left - piece.astype(jnp.float32)
            turned = dot(matrix, piece).T
            for head in range(HEADS):
                table[head, base + step : base + step + 1, :] = turned[head : head + 1, :]
    out[:, STAT:, :] = table[...].astype(jnp.bfloat16)
    fill(out, filled)


HEADS_SHAPE = jax.ShapeDtypeStruct((HEADS, ROWS, HEAD_DIM), jnp.bfloat16)
FILLED_SHAPE = jax.ShapeDtypeStruct((CHIPS, ROWS, HEAD_DIM), jnp.bfloat16)


def pack(tile_valid, *arrays):
    return pl.pallas_call(
        pack_kernel,
        out_shape=[HEADS_SHAPE, FILLED_SHAPE],
        in_specs=[SMEM_SPEC] + vmem_specs(len(arrays)),
        out_specs=vmem_specs(2),
        scratch_shapes=[pltpu.VMEM((HEADS, STAT_ROWS, TOKENS), jnp.float32)],
        compiler_params=params(),
        name="pack",
    )(tile_valid, *arrays)


def refill(heads):
    return pl.pallas_call(
        fill,
        out_shape=FILLED_SHAPE,
        in_specs=vmem_specs(1),
        out_specs=vmem_specs(1)[0],
        compiler_params=params(),
        cost_estimate=pl.CostEstimate(
            flops=FILL_FLOPS, bytes_accessed=FILL_FLOPS >> 8, transcendentals=0
        ),
        name="refill",
    )(heads)


def window(column):
    pieces = []
    if column > 0:
        pieces.append((column - 1, HALF, TOKENS))
    pieces.append((column, 0, TOKENS))
    if column < BLOCKS - 1:
        pieces.append((column + 1, 0, HALF))
    return pieces


def near_rows(near, column, offset):
    parts = [near(b, offset + lo, offset + hi) for b, lo, hi in window(column)]
    return jnp.concatenate(parts, axis=0)


def near_stat(near, column, base):
    parts = []
    for b, lo, hi in window(column):
        rows = near(b, STAT, ROWS).astype(jnp.float32)
        total = rows[base : base + 1] + rows[base + 1 : base + 2] + rows[base + 2 : base + 3]
        parts.append(total[:, lo:hi])
    return jnp.concatenate(parts, axis=1)


def tile_mask(column):
    extent = sum(hi - lo for _, lo, hi in window(column))
    skip = 1 if column > 0 else 0
    own = lax.broadcasted_iota(jnp.int32, (TOKENS, extent), 0) >> 6
    near = (lax.broadcasted_iota(jnp.int32, (TOKENS, extent), 1) >> 6) - skip
    return (own - near <= 1) & (near - own <= 1)


def reader(ref, *index):
    return lambda block, lo, hi: ref[(*index, block, slice(lo, hi), slice(None))]


def near_all(nears, column, offset):
    return jnp.concatenate([near_rows(near, column, offset) for near in nears], axis=0)


def near_all_stat(nears, column, base):
    return jnp.concatenate([near_stat(near, column, base) for near in nears], axis=1)


def tile_masks(column, own_count, near_count):
    one = jnp.where(tile_mask(column), 1.0, 0.0)
    line = jnp.concatenate([one] * near_count, axis=1)
    return jnp.concatenate([line] * own_count, axis=0) > 0.5


def query_sum(own, nears, column):
    query = own(column, QUERY, QUERY + TOKENS)
    grad = own(column, GRAD, GRAD + TOKENS)
    stat = own(column, STAT, ROWS).astype(jnp.float32).T
    norm = stat[:, 0:1] + stat[:, 1:2] + stat[:, 2:3]
    delta = stat[:, 3:4] + stat[:, 4:5] + stat[:, 5:6]
    keys = near_all(nears, column, KEY)
    values = near_all(nears, column, VALUE)
    probs = jnp.exp2(dot_t(query, keys) * (SCALE * LOG2E) - norm)
    probs = jnp.where(tile_masks(column, 1, len(nears)), probs, 0.0)
    slope = probs * (dot_t(grad, values) - delta)
    return dot(slope.astype(jnp.bfloat16), keys)


def key_sum(owns, nears, column):
    key = jnp.concatenate([own(column, KEY, KEY + TOKENS) for own in owns], axis=0)
    value = jnp.concatenate([own(column, VALUE, VALUE + TOKENS) for own in owns], axis=0)
    queries = near_all(nears, column, QUERY)
    grads = near_all(nears, column, GRAD)
    norm = near_all_stat(nears, column, 0)
    delta = near_all_stat(nears, column, 3)
    probs = jnp.exp2(dot_t(key, queries) * (SCALE * LOG2E) - norm)
    probs = jnp.where(tile_masks(column, len(owns), len(nears)), probs, 0.0)
    value_sum = dot(probs.astype(jnp.bfloat16), grads)
    slope = probs * (dot_t(value, grads) - delta)
    return dot(slope.astype(jnp.bfloat16), queries), value_sum


def add_key_sums(totals, frames, column, parts):
    for i, frame in enumerate(frames):
        for total, part in zip(totals, parts):
            total[frame, column] += part[i * TOKENS : (i + 1) * TOKENS]


def by_core(ref, *index):
    return lambda block, lo, hi: ref[(block % 2, *index, block // 2, slice(lo, hi))]


def by_column(ref, *index):
    return lambda block, lo, hi: ref[(*index, block // 2, block % 2, slice(lo, hi))]


def frames_near(frame):
    return [f for f in range(FRAMES) if abs(f - frame) <= 1]


def edge_frame():
    return jnp.where(lax.axis_index("frame") < FRAMES, FRAMES - 1, 0)


def place(scratch, core, arrived, swapped):
    scratch[core] = arrived
    scratch[1 - core] = swapped


def first_query_kernel(arrived, swapped, total, blocks):
    core = lax.axis_index("space") % 2
    place(blocks, core, arrived[...], swapped[...])
    for frame in range(FRAMES):
        nears = [by_core(blocks, f, row) for f in frames_near(frame) for row in range(2)]
        for column in range(BLOCKS):
            total[frame, column] = query_sum(by_core(blocks, frame, core), nears, column)


def first_key_kernel(arrived, swapped, key_total, value_total, blocks):
    core = lax.axis_index("space") % 2
    place(blocks, core, arrived[...], swapped[...])
    key_total[...] = jnp.zeros_like(key_total)
    value_total[...] = jnp.zeros_like(value_total)
    for column in range(BLOCKS):
        for f in range(FRAMES):
            frames = frames_near(f)
            owns = [by_core(blocks, frame, core) for frame in frames]
            parts = key_sum(owns, [by_core(blocks, f, 0), by_core(blocks, f, 1)], column)
            add_key_sums((key_total, value_total), frames, column, parts)


def last_kernel(arrived, swapped, row, row_swapped, jump, jump_swapped, jump_row, *rest):
    firsts, (mine, other), rest = rest[:3], rest[3:5], rest[5:]
    own, near, jumped, jumped_row, done, first_totals, *totals, sems = rest
    core = lax.axis_index("space") % 2
    lower = lax.axis_index("frame") < FRAMES
    moves = [
        (arrived.at[:, core], own.at[core]),
        (swapped.at[:, core], own.at[1 - core]),
        (row.at[:, 1 - core], near.at[core]),
        (row_swapped, near.at[1 - core]),
        (jump, jumped.at[core]),
        (jump_swapped, jumped.at[1 - core]),
        (jump_row, jumped_row),
    ] + [(first, first_totals.at[i]) for i, first in enumerate(firsts)]
    copies = [pltpu.make_async_copy(*move, sems.at[i]) for i, move in enumerate(moves)]
    for copy in copies:
        copy.start()
    for total in totals[1:]:
        total[...] = jnp.zeros_like(total)
    for copy in copies[:4]:
        copy.wait()
    for column in range(BLOCKS):
        for f in range(FRAMES):
            frames = frames_near(f)
            owns = [by_core(own, frame) for frame in frames]
            parts = key_sum(owns, [by_core(near, f)], column)
            add_key_sums(totals[1:], frames, column, parts)
    for copy in copies[4:7]:
        copy.wait()
    frames = [jnp.where(lower, FRAMES - 1 - d, d) for d in range(FRAMES)]
    jumps = [by_core(jumped, 0), by_core(jumped, 1), by_column(jumped_row)]
    for column in range(BLOCKS):
        parts = key_sum([by_core(own, frames[0])], jumps, column)
        add_key_sums(totals[1:], frames[:1], column, parts)
    for d in range(FRAMES):
        nears = [by_core(near, frames[e]) for e in frames_near(d)] + (jumps if d == 0 else [])
        for column in range(BLOCKS):
            totals[0][frames[d], column] = query_sum(by_core(own, frames[d]), nears, column)
    for copy in copies[7:]:
        copy.wait()
    for part, (total, scale) in enumerate(zip(totals, (SCALE, SCALE, 1.0))):
        rows = slice(part * TOKENS, (part + 1) * TOKENS)
        for column in range(BLOCKS):
            both = (total[:, column] + first_totals[part, :, column]) * scale
            done[column % 2, :, column // 2, rows, :] = both.astype(jnp.bfloat16)
    mine[...] = done[core]
    other[...] = done[1 - core]


KEY_FLOPS = 1 << 33
TOTALS = (FRAMES, BLOCKS, TOKENS, HEAD_DIM)
DONE = (FRAMES, 2, 3 * TOKENS, HEAD_DIM)


def attend(kernel, name, flops, args, in_specs, out_shape, scratch):
    return pl.pallas_call(
        kernel,
        out_shape=out_shape,
        in_specs=in_specs,
        out_specs=vmem_specs(len(out_shape)),
        scratch_shapes=scratch,
        compiler_params=params(),
        cost_estimate=pl.CostEstimate(flops=flops, bytes_accessed=flops >> 8, transcendentals=0),
        name=name,
    )(*args)


def first_part(kernel, name, parts, flops, *args):
    return attend(
        kernel,
        name,
        flops,
        args,
        vmem_specs(len(args)),
        [jax.ShapeDtypeStruct(TOTALS, jnp.float32)] * parts,
        [pltpu.VMEM((2, FRAMES, 2, 2, ROWS, HEAD_DIM), jnp.bfloat16)],
    )


def last_part(*args):
    return attend(
        last_kernel,
        "last_part",
        1 << 30,
        args,
        [pl.BlockSpec(memory_space=pl.ANY)] * len(args),
        [jax.ShapeDtypeStruct(DONE, jnp.bfloat16)] * 2,
        [
            pltpu.VMEM((2, FRAMES, 2, ROWS, HEAD_DIM), jnp.bfloat16),
            pltpu.VMEM((2, FRAMES, 2, ROWS, HEAD_DIM), jnp.bfloat16),
            pltpu.VMEM((2, 2, 2, ROWS, HEAD_DIM), jnp.bfloat16),
            pltpu.VMEM((2, 2, ROWS, HEAD_DIM), jnp.bfloat16),
            pltpu.VMEM((2, *DONE), jnp.bfloat16),
            pltpu.VMEM((3, *TOTALS), jnp.float32),
        ]
        + [pltpu.VMEM(TOTALS, jnp.float32)] * 3
        + [pltpu.SemaphoreType.DMA((len(args),))],
    )


def unpack_kernel(tile_valid, blocks, *outs):
    matrix = keep_matrix(tile_valid, 0)
    for part, out in enumerate(outs):
        rows = slice(part * TOKENS, (part + 1) * TOKENS)
        joined = jnp.concatenate([blocks[head, rows, :] for head in range(HEADS)], axis=1)
        out[...] = dot(matrix, joined).astype(jnp.bfloat16)


def unpack(tile_valid, blocks):
    shape = jax.ShapeDtypeStruct((TOKENS, HEADS * HEAD_DIM), jnp.bfloat16)
    return pl.pallas_call(
        unpack_kernel,
        out_shape=[shape] * 3,
        in_specs=[SMEM_SPEC] + vmem_specs(1),
        out_specs=vmem_specs(3),
        compiler_params=params(),
        name="unpack",
    )(tile_valid, blocks)


def plane_exchange(array):
    spaces = lax.axis_size("space")
    groups = []
    for half in range(lax.axis_size("frame") // FRAMES):
        for z in range(spaces // 8):
            for core in range(2):
                groups.append(
                    [
                        (half * FRAMES + j // 4) * spaces + z * 8 + (j % 4) * 2 + core
                        for j in range(CHIPS)
                    ]
                )
    return lax.all_to_all(array, AXES, 0, 0, axis_index_groups=groups)


def with_idle(array):
    return jnp.pad(array, ((0, CHIPS - HEADS), (0, 0), (0, 0)))


def core_swap(array):
    return lax.ppermute(array, "space", [(s, s ^ 1) for s in range(lax.axis_size("space"))])


def row_swap(array):
    route = []
    for s in range(1, lax.axis_size("space") - 8, 2):
        route += [(s, s + 7), (s + 7, s)]
    return lax.ppermute(array, "space", route)


def row_shift(array):
    count = lax.axis_size("space")
    route = [(s, s + (8 if s // 4 % 2 else -8)) for s in range(count)]
    return lax.ppermute(array, "space", [(a, b) for a, b in route if 0 <= b < count])


def half_swap(array):
    count = lax.axis_size("frame")
    return lax.ppermute(array, "frame", [(f, (f + FRAMES) % count) for f in range(count)])


def two_ways(core, mine, other, axis):
    first = jnp.where(core == 0, mine, other)
    second = jnp.where(core == 0, other, mine)
    return jnp.stack([first, second], axis=axis)


def own_row(core, arrived, swapped, axis):
    mine = lax.dynamic_index_in_dim(arrived, core, axis, keepdims=False)
    other = lax.dynamic_index_in_dim(swapped, core, axis, keepdims=False)
    return two_ways(core, mine, other, axis + 1)


def shards(query, key, value, grad_out, log_norm, delta, tile_valid):
    core = lax.axis_index("space") % 2
    shape = query.shape

    def flat(array):
        return array.reshape(TOKENS, array.shape[-1])

    heads, packed = pack(
        tile_valid, *(flat(v) for v in (key, value, query, grad_out, log_norm, delta))
    )
    shifted = refill(row_shift(heads))
    arrived = plane_exchange(packed)
    arrived, shifted = lax.optimization_barrier((arrived, shifted))
    arrived = arrived.reshape(FRAMES, 2, 2, ROWS, HEAD_DIM)
    jump = half_swap(lax.dynamic_index_in_dim(arrived, edge_frame(), 0, keepdims=False))
    swapped = core_swap(arrived)
    row = plane_exchange(shifted).reshape(FRAMES, 2, 2, ROWS, HEAD_DIM)
    first_q = first_part(first_query_kernel, "first_query", 1, 1 << 10, arrived, swapped)
    jump, first_q = lax.optimization_barrier((jump, first_q))
    jump_swapped = core_swap(jump)
    key_args, jump_swapped = lax.optimization_barrier(((arrived, swapped), jump_swapped))
    first_kv = first_part(first_key_kernel, "first_key", 2, KEY_FLOPS, *key_args)
    jump_row = row_swap(own_row(core, jump, jump_swapped, 0))
    row, first_kv, jump_row = lax.optimization_barrier((row, first_kv, jump_row))
    row_swapped = core_swap(lax.dynamic_index_in_dim(row, core, 1, keepdims=False))
    firsts = (*first_q, *first_kv)
    mine, other = last_part(
        arrived, swapped, row, row_swapped, jump, jump_swapped, jump_row, *firsts
    )
    whole = two_ways(core, mine, core_swap(other), 1)
    blocks = plane_exchange(whole.reshape(CHIPS, *mine.shape[2:]))
    return tuple(out.reshape(shape) for out in unpack(tile_valid, blocks))


def solution(mesh):
    blocks = P("frame", "space", None, None, None)
    return jax.shard_map(
        shards,
        mesh=mesh,
        in_specs=(blocks,) * 6 + (P(),),
        out_specs=(blocks,) * 3,
        check_vma=False,
    )
```

time: 196 us -> 151 us (0.77); the launches traced: 193 us -> 150 us
  Pallas kernels: 69.1 us -> 42.4 us
  waiting for transfers between devices: 53.6 us -> 37.7 us
  blocking collectives: 25.9 us -> 29 us
  local copies, waits for them, and re-layouts: 5.37 us -> 2.69 us
    pallas_call x5, Pallas kernels: 66.4 us -> 39.8 us  [the longest x3 32.7 us: attend(): pl.pallas_call(kernel, out_shape=out_shape, in_specs=in_specs, out_specs=...]
    ppermute x0 -> x1, waiting for transfers between devices: none -> 25.6 us  [row_shift(): lax.ppermute(array, 'space', [(a, b) for a, b in route if 0 <= b < count])]
    all_to_all x2, waiting for transfers between devices: 26.1 us -> 2.02 us  [plane_exchange(): return lax.all_to_all(array, AXES, 0, 0, axis_index_groups=groups)]
    ppermute x1, waiting for transfers between devices: 25.2 us -> 3.68 us  [half_swap(): lax.ppermute(array, 'frame', [(f, (f + FRAMES) % count) for f in range(co...]
    ppermute x6 -> x4, waiting for transfers between devices: 2.29 us -> 6.35 us  [core_swap(): lax.ppermute(array, 'space', [(s, s ^ 1) for s in range(lax.axis_size('sp...]
    all_to_all x2, starting transfers between devices: 11.8 us -> 15.8 us  [plane_exchange(): return lax.all_to_all(array, AXES, 0, 0, axis_index_groups=groups)]
    all_to_all x1, blocking collectives: 25.9 us -> 29 us  [plane_exchange(): return lax.all_to_all(array, AXES, 0, 0, axis_index_groups=groups)]
    ppermute x6 -> x4, starting transfers between devices: 6.82 us -> 3.96 us  [core_swap(): lax.ppermute(array, 'space', [(s, s ^ 1) for s in range(lax.axis_size('sp...]
  transfers between devices with their start and end apart: 12 -> 9, of which waited for: 4 -> 6; matrix products, arithmetic and copies ran while one was open for 1% -> 0% of each run, Pallas kernels for 24% -> 15%
where the time goes in v3:
time: 151 us; the launch traced here: 150 us
  Pallas kernels  42.4 us (28%)
  waiting for transfers between devices  37.7 us (25%)
  starting transfers between devices  36.1 us (24%)
  blocking collectives  29 us (19%)
  local copies, waits for them, and re-layouts  2.69 us (2%)
    pallas_call x3, Pallas kernels, attend(): pl.pallas_call(kernel, out_shape=out_shape, in_specs=in_specs, out_specs=...  32.7 us
    all_to_all x1, blocking collectives, plane_exchange(): return lax.all_to_all(array, AXES, 0, 0, axis_index_groups=groups)  29 us
    ppermute x1, waiting for transfers between devices, row_shift(): lax.ppermute(array, 'space', [(a, b) for a, b in route if 0 <= b < count])  25.6 us
    all_to_all x2, starting transfers between devices, plane_exchange(): return lax.all_to_all(array, AXES, 0, 0, axis_index_groups=groups)  15.8 us
    ppermute x1, starting transfers between devices, row_swap(): return lax.ppermute(array, 'space', route)  8.96 us
    ppermute x4, waiting for transfers between devices, core_swap(): lax.ppermute(array, 'space', [(s, s ^ 1) for s in range(lax.axis_size('sp...  6.35 us
    ppermute x1, starting transfers between devices, half_swap(): lax.ppermute(array, 'frame', [(f, (f + FRAMES) % count) for f in range(co...  6.09 us
    pallas_call x1, Pallas kernels, pack(): pl.pallas_call(pack_kernel, out_shape=[HEADS_SHAPE, FILLED_SHAPE], in_spe...  4.12 us
  transfers between devices with their start and end apart: 9, of which 6 were waited for; matrix products, arithmetic and copies ran while one was open for 0% of the time, Pallas kernels for 15%

profile of v3, /device:TPU:1, one launch (start us, length us, event | category | flops | bytes accessed | tf_op | source)
XLA Modules:
  0.0 150.1 jit_solution(16149401737088138518)
XLA Ops:
  0.6 4.1 %pack.1 = (bf16[12,528,128]{2,1,0:T(8,128)(2,1)}, bf16[16,528,128]{2,1,0:T(8,128)(2,1)}) custom-call(s32[16]{0:T(128)} %tile_valid.3, bf16[128,1536]{1,0:T(8,128)(2,1)} %bitcast.38, bf16[128,1536]{1,0:T(8,128)(2,1)} %bitcast.39, bf16[128,1536]{1,0:T(8,128)(2,1)} %bitcast.40, bf16[128,1536]{1,0:T(8,128)(2,1)} %bitcast.41, f32[128,12]{1,0:T(8,128)} %bitcast.42, ...), custom_call_target="tpu_custom_call" | custom-call | tf_op jit(solution)/shard_map/pack/pallas_call | solution.py:91
  4.7 1.3 collective-permute-start
  6.0 11.0 %all-to-all-start = ((bf16[16,528,128]{2,1,0:T(8,128)(2,1)}), bf16[16,528,128]{2,1,0:T(8,128)(2,1)S(1)}, u32[]{:S(2)}, u32[]{:S(2)}) async-start(bf16[16,528,128]{2,1,0:T(8,128)(2,1)} %get-tuple-element.23), calls=%async_computation | async-start | bytes 4325376 | tf_op jit(solution)/shard_map/all_to_all | solution.py:375
  17.1 25.6 %collective-permute-done.heads = bf16[12,528,128]{2,1,0:T(8,128)(2,1)} collective-permute-done((bf16[12,528,128]{2,1,0:T(8,128)(2,1)}, bf16[12,528,128]{2,1,0:T(8,128)(2,1)}, u32[]{:S(2)}, u32[]{:S(2)}) %collective-permute-start) | collective-permute-done | bytes 1622048 | tf_op jit(solution)/shard_map/ppermute | solution.py:396
  42.7 3.0 %refill.1 = bf16[16,528,128]{2,1,0:T(8,128)(2,1)} custom-call(bf16[12,528,128]{2,1,0:T(8,128)(2,1)} %collective-permute-done.heads), custom_call_target="tpu_custom_call" | custom-call | flops 17179869184 | bytes 67108864 | tf_op jit(solution)/shard_map/refill/pallas_call | solution.py:103
  45.7 2.0 %all-to-all-done = bf16[16,528,128]{2,1,0:T(8,128)(2,1)S(1)} async-done(((bf16[16,528,128]{2,1,0:T(8,128)(2,1)}), bf16[16,528,128]{2,1,0:T(8,128)(2,1)S(1)}, u32[]{:S(2)}, u32[]{:S(2)}) %all-to-all-start) | async-done | bytes 2162720 | tf_op jit(solution)/shard_map/all_to_all | solution.py:375
  47.7 0.0 copy-start
  47.7 2.4 %collective-permute-start.1 = (bf16[4,2,2,528,128]{4,3,2,1,0:T(8,128)(2,1)S(1)}, bf16[4,2,2,528,128]{4,3,2,1,0:T(8,128)(2,1)}, u32[]{:S(2)}, u32[]{:S(2)}) collective-permute-start(bf16[4,2,2,528,128]{4,3,2,1,0:T(8,128)(2,1)S(1)} %bitcast.32), channel_id=1, source_target_pairs={{0,1},{1,0},{2,3},{3,2},{4,5},{5,4},{6,7},{7,6},{8,9},{9,8},{10,11... | collective-permute-start | bytes 6488072 | tf_op jit(solution)/shard_map/ppermute | solution.py:383
  50.1 6.1 %collective-permute-start.2 = (bf16[2,2,528,128]{3,2,1,0:T(8,128)(2,1)S(1)}, bf16[2,2,528,128]{3,2,1,0:T(8,128)(2,1)S(1)}, u32[]{:S(2)}, u32[]{:S(2)}) collective-permute-start(bf16[2,2,528,128]{3,2,1,0:T(8,128)(2,1)S(1)} %dynamic-slice_bitcast_fusion.1), channel_id=1, source_target_pairs={{0,128},{32,160},{64,192},{96,224},{128,0},{160,32},{192,64},{224,... | collective-permute-start | bytes 1622024 | tf_op jit(solution)/shard_map/ppermute | solution.py:401
  56.2 0.0 copy-done
  56.2 4.8 %all-to-all-start.1 = ((bf16[16,528,128]{2,1,0:T(8,128)(2,1)}), bf16[16,528,128]{2,1,0:T(8,128)(2,1)}, u32[]{:S(2)}, u32[]{:S(2)}) async-start(bf16[16,528,128]{2,1,0:T(8,128)(2,1)} %refill.1), calls=%async_computation.1 | async-start | bytes 4325376 | tf_op jit(solution)/shard_map/all_to_all | solution.py:375
  61.0 0.0 collective-permute-done.1.swapped
  61.0 9.2 %first_query.1.rest_0_ = f32[4,4,128,128]{3,2,1,0:T(8,128)} custom-call(bf16[4,2,2,528,128]{4,3,2,1,0:T(8,128)(2,1)} %bitcast.34, bf16[4,2,2,528,128]{4,3,2,1,0:T(8,128)(2,1)} %collective-permute-done.1.swapped), custom_call_target="tpu_custom_call" | custom-call | flops 1024 | bytes 4 | tf_op jit(solution)/shard_map/first_query/pallas_call | solution.py:298
  70.2 3.7 %collective-permute-done.2.jump = bf16[2,2,528,128]{3,2,1,0:T(8,128)(2,1)S(1)} collective-permute-done((bf16[2,2,528,128]{3,2,1,0:T(8,128)(2,1)S(1)}, bf16[2,2,528,128]{3,2,1,0:T(8,128)(2,1)S(1)}, u32[]{:S(2)}, u32[]{:S(2)}) %collective-permute-start.2) | collective-permute-done | bytes 540704 | tf_op jit(solution)/shard_map/ppermute | solution.py:401
  73.9 0.0 copy-start.1
  73.9 0.7 collective-permute-start.3
  74.6 1.6 %collective-permute-done.3.jump_swapped = bf16[2,2,528,128]{3,2,1,0:T(8,128)(2,1)S(1)} collective-permute-done((bf16[2,2,528,128]{3,2,1,0:T(8,128)(2,1)S(1)}, bf16[2,2,528,128]{3,2,1,0:T(8,128)(2,1)S(1)}, u32[]{:S(2)}, u32[]{:S(2)}) %collective-permute-start.3) | collective-permute-done | bytes 540704 | tf_op jit(solution)/shard_map/ppermute | solution.py:383
  76.2 0.0 copy-start.2
  76.2 0.1 pad_maximum_fusion.1
  76.3 9.0 %collective-permute-start.4 = (bf16[2,2,528,128]{3,2,1,0:T(8,128)(2,1)S(1)}, bf16[2,2,528,128]{3,2,1,0:T(8,128)(2,1)S(1)}, u32[]{:S(2)}, u32[]{:S(2)}) collective-permute-start(bf16[2,2,528,128]{3,2,1,0:T(8,128)(2,1)S(1)} %pad_maximum_fusion.1), channel_id=1, source_target_pairs={{1,8},{8,1},{3,10},{10,3},{5,12},{12,5},{7,14},{14,7},{9,16},{16,9... | collective-permute-start | bytes 1622024 | tf_op jit(solution)/shard_map/ppermute | solution.py:390
  85.3 10.4 %first_key.1 = (f32[4,4,128,128]{3,2,1,0:T(8,128)}, f32[4,4,128,128]{3,2,1,0:T(8,128)}) custom-call(bf16[4,2,2,528,128]{4,3,2,1,0:T(8,128)(2,1)} %bitcast.35, bf16[4,2,2,528,128]{4,3,2,1,0:T(8,128)(2,1)} %collective-permute-done.1.swapped), custom_call_target="tpu_custom_call" | custom-call | flops 8589934592 | bytes 33554432 | tf_op jit(solution)/shard_map/first_key/pallas_call | solution.py:298
  95.7 0.0 copy-done.1
  95.7 0.0 copy-done.2
  95.7 0.0 all-to-all-done.1
  95.7 0.0 collective-permute-done.4.jump_row
  95.7 0.0 copy-start.4
  95.7 1.5 %dynamic-slice_bitcast_fusion = bf16[4,2,528,128]{3,2,1,0:T(8,128)(2,1)S(1)} fusion(bf16[4,2,2,528,128]{4,3,2,1,0:T(8,128)(2,1)} %bitcast.7.row, s32[]{:T(128)S(6)} %select_n.68), kind=kLoop, calls=%fused_computation.1 | loop fusion | bytes 2162692 | tf_op jit(solution)/shard_map/jit(dynamic_index_in_dim)/squeeze | solution.py:440
  97.2 0.5 collective-permute-start.5
  97.7 2.5 %collective-permute-done.5.row_swapped = bf16[4,2,528,128]{3,2,1,0:T(8,128)(2,1)S(1)} collective-permute-done((bf16[4,2,528,128]{3,2,1,0:T(8,128)(2,1)S(1)}, bf16[4,2,528,128]{3,2,1,0:T(8,128)(2,1)S(1)}, u32[]{:S(2)}, u32[]{:S(2)}) %collective-permute-start.5) | collective-permute-done | bytes 1081376 | tf_op jit(solution)/shard_map/ppermute | solution.py:383
  100.2 0.0 copy-done.4
  100.2 0.0 copy-start.3
  100.2 1.0 copy-done.3
  101.2 13.1 %last_part.1 = (bf16[4,2,384,128]{3,2,1,0:T(8,128)(2,1)}, bf16[4,2,384,128]{3,2,1,0:T(8,128)(2,1)}) custom-call(bf16[4,2,2,528,128]{4,3,2,1,0:T(8,128)(2,1)} %bitcast.36, bf16[4,2,2,528,128]{4,3,2,1,0:T(8,128)(2,1)} %collective-permute-done.1.swapped, bf16[4,2,2,528,128]{4,3,2,1,0:T(8,128)(2,1)} %bitcast.7.row, bf16[4,2,528,128]{3,2,1,0:T(8,128)(2,1)} %copy-done.3, ...), custom_call_target="tpu_custom_call" | custom-call | flops 1073741824 | bytes 4194304 | tf_op jit(solution)/shard_map/last_part/pallas_call | solution.py:298
  114.3 0.3 collective-permute-start.6
  114.6 2.3 %collective-permute-done.6 = bf16[4,2,384,128]{3,2,1,0:T(8,128)(2,1)S(1)} collective-permute-done((bf16[4,2,384,128]{3,2,1,0:T(8,128)(2,1)}, bf16[4,2,384,128]{3,2,1,0:T(8,128)(2,1)S(1)}, u32[]{:S(2)}, u32[]{:S(2)}) %collective-permute-start.6) | collective-permute-done | bytes 786464 | tf_op jit(solution)/shard_map/ppermute | solution.py:383
  116.9 1.2 select_bitcast_fusion.1
  118.1 0.1 pad_maximum_fusion
  118.3 0.1 copy.11
  118.4 29.0 %all_to_all.15.blocks = bf16[16,384,128]{2,1,0:T(8,128)(2,1)} all-to-all(bf16[16,384,128]{2,1,0:T(8,128)(2,1)S(1)} %bitcast.37), channel_id=1, replica_groups={{0,2,4,6,32,34,36,38,64,66,68,70,96,98,100,102},{1,3,5,7,33,35,37,39,65..., dimensions={0} | all-to-all | bytes 3145728 | tf_op jit(solution)/shard_map/all_to_all | solution.py:375
  147.5 2.7 %unpack.1 = (bf16[128,1536]{1,0:T(8,128)(2,1)}, bf16[128,1536]{1,0:T(8,128)(2,1)}, bf16[128,1536]{1,0:T(8,128)(2,1)}) custom-call(s32[16]{0:T(128)} %tile_valid.3, bf16[16,384,128]{2,1,0:T(8,128)(2,1)} %all_to_all.15.blocks), custom_call_target="tpu_custom_call" | custom-call | tf_op jit(solution)/shard_map/unpack/pallas_call | solution.py:353
  (2 shorter events, 0.1 us)
Async XLA Ops:
  4.7 37.9 %collective-permute-start = (bf16[12,528,128]{2,1,0:T(8,128)(2,1)}, bf16[12,528,128]{2,1,0:T(8,128)(2,1)}, u32[]{:S(2)}, u32[]{:S(2)}) collective-permute-start(bf16[12,528,128]{2,1,0:T(8,128)(2,1)} %get-tuple-element.24), channel_id=1, source_target_pairs={{4,12},{5,13},{6,14},{7,15},{8,0},{9,1},{10,2},{11,3},{12,20},{13,... | collective-permute-start | bytes 4866056 | tf_op jit(solution)/shard_map/ppermute | solution.py:396
  6.0 41.6 %all-to-all-start = ((bf16[16,528,128]{2,1,0:T(8,128)(2,1)}), bf16[16,528,128]{2,1,0:T(8,128)(2,1)S(1)}, u32[]{:S(2)}, u32[]{:S(2)}) async-start(bf16[16,528,128]{2,1,0:T(8,128)(2,1)} %get-tuple-element.23), calls=%async_computation | async-start | bytes 4325376 | tf_op jit(solution)/shard_map/all_to_all | solution.py:375
  47.7 8.6 %copy-start = (bf16[16,528,128]{2,1,0:T(8,128)(2,1)}, bf16[16,528,128]{2,1,0:T(8,128)(2,1)S(1)}, u32[]{:S(2)}) copy-start(bf16[16,528,128]{2,1,0:T(8,128)(2,1)S(1)} %all-to-all-done) | copy-start | bytes 6488068
  47.7 13.3 %collective-permute-start.1 = (bf16[4,2,2,528,128]{4,3,2,1,0:T(8,128)(2,1)S(1)}, bf16[4,2,2,528,128]{4,3,2,1,0:T(8,128)(2,1)}, u32[]{:S(2)}, u32[]{:S(2)}) collective-permute-start(bf16[4,2,2,528,128]{4,3,2,1,0:T(8,128)(2,1)S(1)} %bitcast.32), channel_id=1, source_target_pairs={{0,1},{1,0},{2,3},{3,2},{4,5},{5,4},{6,7},{7,6},{8,9},{9,8},{10,11... | collective-permute-start | bytes 6488072 | tf_op jit(solution)/shard_map/ppermute | solution.py:383
  50.1 23.7 %collective-permute-start.2 = (bf16[2,2,528,128]{3,2,1,0:T(8,128)(2,1)S(1)}, bf16[2,2,528,128]{3,2,1,0:T(8,128)(2,1)S(1)}, u32[]{:S(2)}, u32[]{:S(2)}) collective-permute-start(bf16[2,2,528,128]{3,2,1,0:T(8,128)(2,1)S(1)} %dynamic-slice_bitcast_fusion.1), channel_id=1, source_target_pairs={{0,128},{32,160},{64,192},{96,224},{128,0},{160,32},{192,64},{224,... | collective-permute-start | bytes 1622024 | tf_op jit(solution)/shard_map/ppermute | solution.py:401
  56.2 39.4 %all-to-all-start.1 = ((bf16[16,528,128]{2,1,0:T(8,128)(2,1)}), bf16[16,528,128]{2,1,0:T(8,128)(2,1)}, u32[]{:S(2)}, u32[]{:S(2)}) async-start(bf16[16,528,128]{2,1,0:T(8,128)(2,1)} %refill.1), calls=%async_computation.1 | async-start | bytes 4325376 | tf_op jit(solution)/shard_map/all_to_all | solution.py:375
  73.9 21.8 %copy-start.1 = (bf16[2,2,528,128]{3,2,1,0:T(8,128)(2,1)}, bf16[2,2,528,128]{3,2,1,0:T(8,128)(2,1)S(1)}, u32[]{:S(2)}) copy-start(bf16[2,2,528,128]{3,2,1,0:T(8,128)(2,1)S(1)} %collective-permute-done.2.jump) | copy-start | bytes 1622020
  73.9 2.3 %collective-permute-start.3 = (bf16[2,2,528,128]{3,2,1,0:T(8,128)(2,1)S(1)}, bf16[2,2,528,128]{3,2,1,0:T(8,128)(2,1)S(1)}, u32[]{:S(2)}, u32[]{:S(2)}) collective-permute-start(bf16[2,2,528,128]{3,2,1,0:T(8,128)(2,1)S(1)} %collective-permute-done.2.jump), channel_id=1, source_target_pairs={{0,1},{1,0},{2,3},{3,2},{4,5},{5,4},{6,7},{7,6},{8,9},{9,8},{10,11... | collective-permute-start | bytes 1622024 | tf_op jit(solution)/shard_map/ppermute | solution.py:383
  76.2 19.5 %copy-start.2 = (bf16[2,2,528,128]{3,2,1,0:T(8,128)(2,1)}, bf16[2,2,528,128]{3,2,1,0:T(8,128)(2,1)S(1)}, u32[]{:S(2)}) copy-start(bf16[2,2,528,128]{3,2,1,0:T(8,128)(2,1)S(1)} %collective-permute-done.3.jump_swapped) | copy-start | bytes 1622020
  76.3 19.4 %collective-permute-start.4 = (bf16[2,2,528,128]{3,2,1,0:T(8,128)(2,1)S(1)}, bf16[2,2,528,128]{3,2,1,0:T(8,128)(2,1)S(1)}, u32[]{:S(2)}, u32[]{:S(2)}) collective-permute-start(bf16[2,2,528,128]{3,2,1,0:T(8,128)(2,1)S(1)} %pad_maximum_fusion.1), channel_id=1, source_target_pairs={{1,8},{8,1},{3,10},{10,3},{5,12},{12,5},{7,14},{14,7},{9,16},{16,9... | collective-permute-start | bytes 1622024 | tf_op jit(solution)/shard_map/ppermute | solution.py:390
  95.7 4.5 %copy-start.4 = (bf16[2,2,528,128]{3,2,1,0:T(8,128)(2,1)}, bf16[2,2,528,128]{3,2,1,0:T(8,128)(2,1)S(1)}, u32[]{:S(2)}) copy-start(bf16[2,2,528,128]{3,2,1,0:T(8,128)(2,1)S(1)} %collective-permute-done.4.jump_row) | copy-start | bytes 1622020
  97.2 3.0 %collective-permute-start.5 = (bf16[4,2,528,128]{3,2,1,0:T(8,128)(2,1)S(1)}, bf16[4,2,528,128]{3,2,1,0:T(8,128)(2,1)S(1)}, u32[]{:S(2)}, u32[]{:S(2)}) collective-permute-start(bf16[4,2,528,128]{3,2,1,0:T(8,128)(2,1)S(1)} %dynamic-slice_bitcast_fusion), channel_id=1, source_target_pairs={{0,1},{1,0},{2,3},{3,2},{4,5},{5,4},{6,7},{7,6},{8,9},{9,8},{10,11... | collective-permute-start | bytes 3244040 | tf_op jit(solution)/shard_map/ppermute | solution.py:383
  100.2 1.0 copy-start.3
  114.3 2.6 %collective-permute-start.6 = (bf16[4,2,384,128]{3,2,1,0:T(8,128)(2,1)}, bf16[4,2,384,128]{3,2,1,0:T(8,128)(2,1)S(1)}, u32[]{:S(2)}, u32[]{:S(2)}) collective-permute-start(bf16[4,2,384,128]{3,2,1,0:T(8,128)(2,1)} %get-tuple-element.39), channel_id=1, source_target_pairs={{0,1},{1,0},{2,3},{3,2},{4,5},{5,4},{6,7},{7,6},{8,9},{9,8},{10,11... | collective-permute-start | bytes 2359304 | tf_op jit(solution)/shard_map/ppermute | solution.py:383

commit v4 on v3

--- a/solution.py
+++ b/solution.py
@@ -99,12 +99,38 @@
     )(tile_valid, *arrays)
 
 
+def refill_kernel(heads, out, scratch, sems):
+    pieces = [pl.ds(i * 3, 3) for i in range(HEADS // 3)]
+    ins = [
+        pltpu.make_async_copy(heads.at[piece], scratch.at[piece], sems.at[i])
+        for i, piece in enumerate(pieces)
+    ]
+    for copy in ins:
+        copy.start()
+    scratch[HEADS:] = jnp.zeros((CHIPS - HEADS,) + out.shape[1:], jnp.bfloat16)
+    pieces.append(pl.ds(HEADS, CHIPS - HEADS))
+    outs = [
+        pltpu.make_async_copy(scratch.at[piece], out.at[piece], sems.at[len(ins) + i])
+        for i, piece in enumerate(pieces)
+    ]
+    outs[-1].start()
+    for copy_in, copy_out in zip(ins, outs):
+        copy_in.wait()
+        copy_out.start()
+    for copy in outs:
+        copy.wait()
+
+
 def refill(heads):
     return pl.pallas_call(
-        fill,
+        refill_kernel,
         out_shape=FILLED_SHAPE,
-        in_specs=vmem_specs(1),
-        out_specs=vmem_specs(1)[0],
+        in_specs=[pl.BlockSpec(memory_space=pl.ANY)],
+        out_specs=pl.BlockSpec(memory_space=pl.ANY),
+        scratch_shapes=[
+            pltpu.VMEM(FILLED_SHAPE.shape, jnp.bfloat16),
+            pltpu.SemaphoreType.DMA((2 * (HEADS // 3) + 1,)),
+        ],
         compiler_params=params(),
         cost_estimate=pl.CostEstimate(
             flops=FILL_FLOPS, bytes_accessed=FILL_FLOPS >> 8, transcendentals=0
@@ -240,103 +266,159 @@
             add_key_sums((key_total, value_total), frames, column, parts)
 
 
-def last_kernel(arrived, swapped, row, row_swapped, jump, jump_swapped, jump_row, *rest):
-    firsts, (mine, other), rest = rest[:3], rest[3:5], rest[5:]
-    own, near, jumped, jumped_row, done, first_totals, *totals, sems = rest
-    core = lax.axis_index("space") % 2
-    lower = lax.axis_index("frame") < FRAMES
-    moves = [
-        (arrived.at[:, core], own.at[core]),
-        (swapped.at[:, core], own.at[1 - core]),
-        (row.at[:, 1 - core], near.at[core]),
-        (row_swapped, near.at[1 - core]),
-        (jump, jumped.at[core]),
-        (jump_swapped, jumped.at[1 - core]),
-        (jump_row, jumped_row),
-    ] + [(first, first_totals.at[i]) for i, first in enumerate(firsts)]
+def start_all(moves, sems):
     copies = [pltpu.make_async_copy(*move, sems.at[i]) for i, move in enumerate(moves)]
     for copy in copies:
         copy.start()
+    return copies
+
+
+def wait_all(copies):
+    for copy in copies:
+        copy.wait()
+
+
+def finish(totals, firsts, column, done):
+    for part, (total, first, scale) in enumerate(zip(totals, firsts, (SCALE, SCALE, 1.0))):
+        rows = slice(part * TOKENS, (part + 1) * TOKENS)
+        done[column % 2, ..., column // 2, rows, :] = ((total + first) * scale).astype(jnp.bfloat16)
+
+
+def row_kernel(arrived, swapped, row, row_swapped, *rest):
+    firsts, (mine, other, edges), rest = rest[:3], rest[3:6], rest[6:]
+    own, near, done, first_totals, *totals, sems = rest
+    core = lax.axis_index("space") % 2
+    copies = start_all(
+        [
+            (arrived.at[:, core], own.at[core]),
+            (swapped.at[:, core], own.at[1 - core]),
+            (row.at[:, 1 - core], near.at[core]),
+            (row_swapped, near.at[1 - core]),
+        ]
+        + [(first, first_totals.at[i]) for i, first in enumerate(firsts)],
+        sems,
+    )
     for total in totals[1:]:
         total[...] = jnp.zeros_like(total)
-    for copy in copies[:4]:
-        copy.wait()
+    wait_all(copies[:4])
     for column in range(BLOCKS):
         for f in range(FRAMES):
             frames = frames_near(f)
             owns = [by_core(own, frame) for frame in frames]
             parts = key_sum(owns, [by_core(near, f)], column)
             add_key_sums(totals[1:], frames, column, parts)
-    for copy in copies[4:7]:
-        copy.wait()
-    frames = [jnp.where(lower, FRAMES - 1 - d, d) for d in range(FRAMES)]
+    for frame in range(FRAMES):
+        nears = [by_core(near, f) for f in frames_near(frame)]
+        for column in range(BLOCKS):
+            totals[0][frame, column] = query_sum(by_core(own, frame), nears, column)
+    wait_all(copies[4:])
+    for column in range(BLOCKS):
+        sums = [total[:, column] for total in totals]
+        finish(sums, [first_totals[part, :, column] for part in range(3)], column, done)
+    mine[...] = done[core]
+    other[...] = done[1 - core]
+    edge = edge_frame()
+    for part, total in enumerate(totals):
+        edges[part] = total[edge] + first_totals[part, edge]
+
+
+def jump_kernel(arrived, swapped, jump, jump_swapped, jump_row, edges, mine_in, other_in, *rest):
+    mine, other, own, jumped, jumped_row, sums, done, sems = rest
+    core = lax.axis_index("space") % 2
+    edge = edge_frame()
+    copies = start_all(
+        [
+            (arrived.at[edge, core], own.at[core]),
+            (swapped.at[edge, core], own.at[1 - core]),
+            (jump, jumped.at[core]),
+            (jump_swapped, jumped.at[1 - core]),
+            (jump_row, jumped_row),
+            (edges, sums),
+        ],
+        sems,
+    )
+    wait_all(copies)
     jumps = [by_core(jumped, 0), by_core(jumped, 1), by_column(jumped_row)]
     for column in range(BLOCKS):
-        parts = key_sum([by_core(own, frames[0])], jumps, column)
-        add_key_sums(totals[1:], frames[:1], column, parts)
-    for d in range(FRAMES):
-        nears = [by_core(near, frames[e]) for e in frames_near(d)] + (jumps if d == 0 else [])
-        for column in range(BLOCKS):
-            totals[0][frames[d], column] = query_sum(by_core(own, frames[d]), nears, column)
-    for copy in copies[7:]:
-        copy.wait()
-    for part, (total, scale) in enumerate(zip(totals, (SCALE, SCALE, 1.0))):
-        rows = slice(part * TOKENS, (part + 1) * TOKENS)
-        for column in range(BLOCKS):
-            both = (total[:, column] + first_totals[part, :, column]) * scale
-            done[column % 2, :, column // 2, rows, :] = both.astype(jnp.bfloat16)
-    mine[...] = done[core]
-    other[...] = done[1 - core]
-
-
-KEY_FLOPS = 1 << 33
+        parts = (query_sum(by_core(own), jumps, column), *key_sum([by_core(own)], jumps, column))
+        finish(parts, [sums[part, column] for part in range(3)], column, done)
+    wait_all(start_all([(done.at[core], mine.at[edge]), (done.at[1 - core], other.at[edge])], sems))
+
+
+KERNEL_FLOPS = 1 << 10
 TOTALS = (FRAMES, BLOCKS, TOKENS, HEAD_DIM)
 DONE = (FRAMES, 2, 3 * TOKENS, HEAD_DIM)
 
 
-def attend(kernel, name, flops, args, in_specs, out_shape, scratch):
+def attend(kernel, name, args, in_specs, out_specs, out_shape, scratch, aliases=None):
     return pl.pallas_call(
         kernel,
         out_shape=out_shape,
         in_specs=in_specs,
-        out_specs=vmem_specs(len(out_shape)),
+        out_specs=out_specs,
         scratch_shapes=scratch,
+        input_output_aliases=aliases or {},
         compiler_params=params(),
-        cost_estimate=pl.CostEstimate(flops=flops, bytes_accessed=flops >> 8, transcendentals=0),
+        cost_estimate=pl.CostEstimate(
+            flops=KERNEL_FLOPS, bytes_accessed=KERNEL_FLOPS, transcendentals=0
+        ),
         name=name,
     )(*args)
 
 
-def first_part(kernel, name, parts, flops, *args):
+def any_specs(count):
+    return [pl.BlockSpec(memory_space=pl.ANY)] * count
+
+
+def first_part(kernel, name, parts, *args):
     return attend(
         kernel,
         name,
-        flops,
         args,
         vmem_specs(len(args)),
+        vmem_specs(parts),
         [jax.ShapeDtypeStruct(TOTALS, jnp.float32)] * parts,
         [pltpu.VMEM((2, FRAMES, 2, 2, ROWS, HEAD_DIM), jnp.bfloat16)],
     )
 
 
-def last_part(*args):
+def row_part(*args):
     return attend(
-        last_kernel,
-        "last_part",
-        1 << 30,
+        row_kernel,
+        "row_part",
         args,
-        [pl.BlockSpec(memory_space=pl.ANY)] * len(args),
-        [jax.ShapeDtypeStruct(DONE, jnp.bfloat16)] * 2,
+        any_specs(len(args)),
+        vmem_specs(3),
+        [jax.ShapeDtypeStruct(DONE, jnp.bfloat16)] * 2
+        + [jax.ShapeDtypeStruct((3, *TOTALS[1:]), jnp.float32)],
         [
             pltpu.VMEM((2, FRAMES, 2, ROWS, HEAD_DIM), jnp.bfloat16),
             pltpu.VMEM((2, FRAMES, 2, ROWS, HEAD_DIM), jnp.bfloat16),
-            pltpu.VMEM((2, 2, 2, ROWS, HEAD_DIM), jnp.bfloat16),
-            pltpu.VMEM((2, 2, ROWS, HEAD_DIM), jnp.bfloat16),
             pltpu.VMEM((2, *DONE), jnp.bfloat16),
             pltpu.VMEM((3, *TOTALS), jnp.float32),
         ]
         + [pltpu.VMEM(TOTALS, jnp.float32)] * 3
         + [pltpu.SemaphoreType.DMA((len(args),))],
+    )
+
+
+def jump_part(*args):
+    return attend(
+        jump_kernel,
+        "jump_part",
+        args,
+        any_specs(len(args)),
+        any_specs(2),
+        [jax.ShapeDtypeStruct(DONE, jnp.bfloat16)] * 2,
+        [
+            pltpu.VMEM((2, 2, ROWS, HEAD_DIM), jnp.bfloat16),
+            pltpu.VMEM((2, 2, 2, ROWS, HEAD_DIM), jnp.bfloat16),
+            pltpu.VMEM((2, 2, ROWS, HEAD_DIM), jnp.bfloat16),
+            pltpu.VMEM((3, *TOTALS[1:]), jnp.float32),
+            pltpu.VMEM((2, *DONE[1:]), jnp.bfloat16),
+            pltpu.SemaphoreType.DMA((len(args),)),
+        ],
+        {6: 0, 7: 1},
     )
 
 
@@ -355,7 +437,7 @@
         out_shape=[shape] * 3,
         in_specs=[SMEM_SPEC] + vmem_specs(1),
         out_specs=vmem_specs(3),
-        compiler_params=params(),
+        compiler_params=pltpu.CompilerParams(vmem_limit_bytes=VMEM_LIMIT // 3),
         name="unpack",
     )(tile_valid, blocks)
 
@@ -430,17 +512,18 @@
     jump = half_swap(lax.dynamic_index_in_dim(arrived, edge_frame(), 0, keepdims=False))
     swapped = core_swap(arrived)
     row = plane_exchange(shifted).reshape(FRAMES, 2, 2, ROWS, HEAD_DIM)
-    first_q = first_part(first_query_kernel, "first_query", 1, 1 << 10, arrived, swapped)
-    jump, first_q = lax.optimization_barrier((jump, first_q))
+    firsts = [
+        *first_part(first_query_kernel, "first_query", 1, arrived, swapped),
+        *first_part(first_key_kernel, "first_key", 2, arrived, swapped),
+    ]
+    jump, firsts = lax.optimization_barrier((jump, firsts))
     jump_swapped = core_swap(jump)
-    key_args, jump_swapped = lax.optimization_barrier(((arrived, swapped), jump_swapped))
-    first_kv = first_part(first_key_kernel, "first_key", 2, KEY_FLOPS, *key_args)
     jump_row = row_swap(own_row(core, jump, jump_swapped, 0))
-    row, first_kv, jump_row = lax.optimization_barrier((row, first_kv, jump_row))
     row_swapped = core_swap(lax.dynamic_index_in_dim(row, core, 1, keepdims=False))
-    firsts = (*first_q, *first_kv)
-    mine, other = last_part(
-        arrived, swapped, row, row_swapped, jump, jump_swapped, jump_row, *firsts
+    mine, other, edges = row_part(arrived, swapped, row, row_swapped, *firsts)
+    jump_row, edges = lax.optimization_barrier((jump_row, edges))
+    mine, other = jump_part(
+        arrived, swapped, jump, jump_swapped, jump_row, edges, mine, other
     )
     whole = two_ways(core, mine, core_swap(other), 1)
     blocks = plane_exchange(whole.reshape(CHIPS, *mine.shape[2:]))

time: 151 us -> 144 us (0.954)
  starting transfers between devices: 36.1 us -> 31.4 us
  blocking collectives: 29 us -> 25.4 us
    all_to_all x2, waiting for transfers between devices: 2.02 us -> 10.3 us  [plane_exchange(): return lax.all_to_all(array, AXES, 0, 0, axis_index_groups=groups)]
    ppermute x1, starting transfers between devices: 8.96 us -> 3.95 us  [row_swap(): return lax.ppermute(array, 'space', route)]
    ppermute x4, waiting for transfers between devices: 6.35 us -> 2.49 us  [core_swap(): lax.ppermute(array, 'space', [(s, s ^ 1) for s in range(lax.axis_size('sp...]
    ppermute x1, waiting for transfers between devices: 3.68 us -> 0.01 us  [half_swap(): lax.ppermute(array, 'frame', [(f, (f + FRAMES) % count) for f in range(co...]
    all_to_all x1, blocking collectives: 29 us -> 25.4 us  [plane_exchange(): return lax.all_to_all(array, AXES, 0, 0, axis_index_groups=groups)]
    pallas_call x3 -> x4, Pallas kernels: 32.7 us -> 35.1 us  [attend(): pl.pallas_call(kernel, out_shape=out_shape, in_specs=in_specs, out_specs=...]
  transfers between devices with their start and end apart: 9 -> 9, of which waited for: 6 -> 4; matrix products, arithmetic and copies ran while one was open for 0% -> 1% of each run, Pallas kernels for 15% -> 23%
where the time goes in v4:
time: 144 us; the launch traced here: 143 us
  Pallas kernels  43.5 us (30%)
  waiting for transfers between devices  38.4 us (27%)
  starting transfers between devices  31.4 us (22%)
  blocking collectives  25.4 us (18%)
  local copies, waits for them, and re-layouts  2.32 us (2%)
  other arithmetic  1.48 us (1%)
    pallas_call x4, Pallas kernels, attend(): pl.pallas_call(kernel, out_shape=out_shape, in_specs=in_specs, out_specs=...  35.1 us
    ppermute x1, waiting for transfers between devices, row_shift(): lax.ppermute(array, 'space', [(a, b) for a, b in route if 0 <= b < count])  25.6 us
    all_to_all x1, blocking collectives, plane_exchange(): return lax.all_to_all(array, AXES, 0, 0, axis_index_groups=groups)  25.4 us
    all_to_all x2, starting transfers between devices, plane_exchange(): return lax.all_to_all(array, AXES, 0, 0, axis_index_groups=groups)  15.5 us
    all_to_all x2, waiting for transfers between devices, plane_exchange(): return lax.all_to_all(array, AXES, 0, 0, axis_index_groups=groups)  10.3 us
    ppermute x1, starting transfers between devices, half_swap(): lax.ppermute(array, 'frame', [(f, (f + FRAMES) % count) for f in range(co...  6.27 us
    ppermute x4, starting transfers between devices, core_swap(): lax.ppermute(array, 'space', [(s, s ^ 1) for s in range(lax.axis_size('sp...  4.41 us
    pallas_call x1, Pallas kernels, pack(): pl.pallas_call(pack_kernel, out_shape=[HEADS_SHAPE, FILLED_SHAPE], in_spe...  4.11 us
  transfers between devices with their start and end apart: 9, of which 4 were waited for; matrix products, arithmetic and copies ran while one was open for 1% of the time, Pallas kernels for 23%

profile of v4, /device:TPU:1, one launch (start us, length us, event | category | flops | bytes accessed | tf_op | source)
XLA Modules:
  0.0 143.3 jit_solution(1616424714982155503)
XLA Ops:
  0.6 4.1 %pack.1 = (bf16[12,528,128]{2,1,0:T(8,128)(2,1)}, bf16[16,528,128]{2,1,0:T(8,128)(2,1)}) custom-call(s32[16]{0:T(128)} %tile_valid.3, bf16[128,1536]{1,0:T(8,128)(2,1)} %bitcast.39, bf16[128,1536]{1,0:T(8,128)(2,1)} %bitcast.40, bf16[128,1536]{1,0:T(8,128)(2,1)} %bitcast.41, bf16[128,1536]{1,0:T(8,128)(2,1)} %bitcast.42, f32[128,12]{1,0:T(8,128)} %bitcast.43, ...), custom_call_target="tpu_custom_call" | custom-call | tf_op jit(solution)/shard_map/pack/pallas_call | solution.py:91
  4.7 1.3 collective-permute-start
  6.0 11.0 %all-to-all-start = ((bf16[16,528,128]{2,1,0:T(8,128)(2,1)}), bf16[16,528,128]{2,1,0:T(8,128)(2,1)S(1)}, u32[]{:S(2)}, u32[]{:S(2)}) async-start(bf16[16,528,128]{2,1,0:T(8,128)(2,1)} %get-tuple-element.23), calls=%async_computation | async-start | bytes 4325376 | tf_op jit(solution)/shard_map/all_to_all | solution.py:457
  17.1 25.6 %collective-permute-done.heads = bf16[12,528,128]{2,1,0:T(8,128)(2,1)} collective-permute-done((bf16[12,528,128]{2,1,0:T(8,128)(2,1)}, bf16[12,528,128]{2,1,0:T(8,128)(2,1)}, u32[]{:S(2)}, u32[]{:S(2)}) %collective-permute-start) | collective-permute-done | bytes 1622048 | tf_op jit(solution)/shard_map/ppermute | solution.py:478
  42.7 2.5 %refill.1 = bf16[16,528,128]{2,1,0:T(8,128)(2,1)} custom-call(bf16[12,528,128]{2,1,0:T(8,128)(2,1)} %collective-permute-done.heads), custom_call_target="tpu_custom_call" | custom-call | flops 17179869184 | bytes 67108864 | tf_op jit(solution)/shard_map/refill/pallas_call | solution.py:125
  45.1 2.5 %all-to-all-done = bf16[16,528,128]{2,1,0:T(8,128)(2,1)S(1)} async-done(((bf16[16,528,128]{2,1,0:T(8,128)(2,1)}), bf16[16,528,128]{2,1,0:T(8,128)(2,1)S(1)}, u32[]{:S(2)}, u32[]{:S(2)}) %all-to-all-start) | async-done | bytes 2162720 | tf_op jit(solution)/shard_map/all_to_all | solution.py:457
  47.7 0.0 copy-start.1
  47.7 2.4 %collective-permute-start.1 = (bf16[4,2,2,528,128]{4,3,2,1,0:T(8,128)(2,1)S(1)}, bf16[4,2,2,528,128]{4,3,2,1,0:T(8,128)(2,1)}, u32[]{:S(2)}, u32[]{:S(2)}) collective-permute-start(bf16[4,2,2,528,128]{4,3,2,1,0:T(8,128)(2,1)S(1)} %bitcast.32), channel_id=1, source_target_pairs={{0,1},{1,0},{2,3},{3,2},{4,5},{5,4},{6,7},{7,6},{8,9},{9,8},{10,11... | collective-permute-start | bytes 6488072 | tf_op jit(solution)/shard_map/ppermute | solution.py:465
  50.1 4.4 %all-to-all-start.1 = ((bf16[16,528,128]{2,1,0:T(8,128)(2,1)}), bf16[16,528,128]{2,1,0:T(8,128)(2,1)}, u32[]{:S(2)}, u32[]{:S(2)}) async-start(bf16[16,528,128]{2,1,0:T(8,128)(2,1)} %refill.1), calls=%async_computation.1 | async-start | bytes 4325376 | tf_op jit(solution)/shard_map/all_to_all | solution.py:457
  54.6 0.0 copy-done.1
  54.6 6.3 %collective-permute-start.2 = (bf16[2,2,528,128]{3,2,1,0:T(8,128)(2,1)S(1)}, bf16[2,2,528,128]{3,2,1,0:T(8,128)(2,1)S(1)}, u32[]{:S(2)}, u32[]{:S(2)}) collective-permute-start(bf16[2,2,528,128]{3,2,1,0:T(8,128)(2,1)S(1)} %dynamic-slice_bitcast_fusion.1), channel_id=1, source_target_pairs={{0,128},{32,160},{64,192},{96,224},{128,0},{160,32},{192,64},{224,... | collective-permute-start | bytes 1622024 | tf_op jit(solution)/shard_map/ppermute | solution.py:483
  60.9 0.0 collective-permute-done.1.swapped
  60.9 9.2 %first_query.1.rest_0_ = f32[4,4,128,128]{3,2,1,0:T(8,128)} custom-call(bf16[4,2,2,528,128]{4,3,2,1,0:T(8,128)(2,1)} %bitcast.34, bf16[4,2,2,528,128]{4,3,2,1,0:T(8,128)(2,1)} %collective-permute-done.1.swapped), custom_call_target="tpu_custom_call" | custom-call | flops 1024 | bytes 1024 | tf_op jit(solution)/shard_map/first_query/pallas_call | solution.py:354
  70.1 10.3 %first_key.1 = (f32[4,4,128,128]{3,2,1,0:T(8,128)}, f32[4,4,128,128]{3,2,1,0:T(8,128)}) custom-call(bf16[4,2,2,528,128]{4,3,2,1,0:T(8,128)(2,1)} %bitcast.35, bf16[4,2,2,528,128]{4,3,2,1,0:T(8,128)(2,1)} %collective-permute-done.1.swapped), custom_call_target="tpu_custom_call" | custom-call | flops 1024 | bytes 1024 | tf_op jit(solution)/shard_map/first_key/pallas_call | solution.py:354
  80.4 0.0 collective-permute-done.2.jump
  80.5 0.0 copy-start.2
  80.5 0.7 collective-permute-start.3
  81.2 7.7 %all-to-all-done.1 = bf16[16,528,128]{2,1,0:T(8,128)(2,1)} async-done(((bf16[16,528,128]{2,1,0:T(8,128)(2,1)}), bf16[16,528,128]{2,1,0:T(8,128)(2,1)}, u32[]{:S(2)}, u32[]{:S(2)}) %all-to-all-start.1) | async-done | bytes 2162720 | tf_op jit(solution)/shard_map/all_to_all | solution.py:457
  88.9 1.3 dynamic-slice_bitcast_fusion
  90.2 1.2 collective-permute-start.5
  91.4 0.0 collective-permute-done.3.jump_swapped
  91.4 0.0 copy-start.3
  91.4 0.0 copy-done.2
  91.4 0.1 pad_maximum_fusion.1
  91.5 3.9 %collective-permute-start.4 = (bf16[2,2,528,128]{3,2,1,0:T(8,128)(2,1)S(1)}, bf16[2,2,528,128]{3,2,1,0:T(8,128)(2,1)S(1)}, u32[]{:S(2)}, u32[]{:S(2)}) collective-permute-start(bf16[2,2,528,128]{3,2,1,0:T(8,128)(2,1)S(1)} %pad_maximum_fusion.1), channel_id=1, source_target_pairs={{1,8},{8,1},{3,10},{10,3},{5,12},{12,5},{7,14},{14,7},{9,16},{16,9... | collective-permute-start | bytes 1622024 | tf_op jit(solution)/shard_map/ppermute | solution.py:472
  95.5 0.0 collective-permute-done.5.row_swapped
  95.5 11.1 %row_part.1 = (bf16[4,2,384,128]{3,2,1,0:T(8,128)(2,1)}, bf16[4,2,384,128]{3,2,1,0:T(8,128)(2,1)}, f32[3,4,128,128]{3,2,1,0:T(8,128)}) custom-call(bf16[4,2,2,528,128]{4,3,2,1,0:T(8,128)(2,1)} %bitcast.36, bf16[4,2,2,528,128]{4,3,2,1,0:T(8,128)(2,1)} %collective-permute-done.1.swapped, bf16[4,2,2,528,128]{4,3,2,1,0:T(8,128)(2,1)} %bitcast.11.row, ...), custom_call_target="tpu_custom_call" | custom-call | flops 1024 | bytes 1024 | tf_op jit(solution)/shard_map/row_part/pallas_call | solution.py:354
  106.6 0.0 copy-done.3
  106.6 0.0 collective-permute-done.4.jump_row
  106.6 0.0 copy-start.4
  106.6 0.8 copy-done.4
  107.4 4.5 %jump_part.1 = (bf16[4,2,384,128]{3,2,1,0:T(8,128)(2,1)}, bf16[4,2,384,128]{3,2,1,0:T(8,128)(2,1)}) custom-call(bf16[4,2,2,528,128]{4,3,2,1,0:T(8,128)(2,1)} %bitcast.37, bf16[4,2,2,528,128]{4,3,2,1,0:T(8,128)(2,1)} %collective-permute-done.1.swapped, bf16[2,2,528,128]{3,2,1,0:T(8,128)(2,1)} %copy-done.2, ...), custom_call_target="tpu_custom_call", output_to_operand_aliasing={{0}: (6, {}), {1}: (7, {})} | custom-call | flops 1024 | bytes 1024 | tf_op jit(solution)/shard_map/jump_part/pallas_call | solution.py:354
  111.9 0.1 collective-permute-start.6
  112.0 2.5 %collective-permute-done.6 = bf16[4,2,384,128]{3,2,1,0:T(8,128)(2,1)S(1)} collective-permute-done((bf16[4,2,384,128]{3,2,1,0:T(8,128)(2,1)}, bf16[4,2,384,128]{3,2,1,0:T(8,128)(2,1)S(1)}, u32[]{:S(2)}, u32[]{:S(2)}) %collective-permute-start.6) | collective-permute-done | bytes 786464 | tf_op jit(solution)/shard_map/ppermute | solution.py:465
  114.5 1.2 select_bitcast_fusion.1
  115.7 0.1 pad_maximum_fusion
  115.9 0.1 copy.13
  116.0 0.0 copy-start
  116.1 25.4 %all_to_all.15.blocks = bf16[16,384,128]{2,1,0:T(8,128)(2,1)S(1)} all-to-all(bf16[16,384,128]{2,1,0:T(8,128)(2,1)S(1)} %bitcast.38), channel_id=1, replica_groups={{0,2,4,6,32,34,36,38,64,66,68,70,96,98,100,102},{1,3,5,7,33,35,37,39,65..., dimensions={0} | all-to-all | bytes 3145728 | tf_op jit(solution)/shard_map/all_to_all | solution.py:457
  141.5 0.0 copy-done
  141.5 1.8 %unpack.1 = (bf16[128,1536]{1,0:T(8,128)(2,1)}, bf16[128,1536]{1,0:T(8,128)(2,1)}, bf16[128,1536]{1,0:T(8,128)(2,1)}) custom-call(s32[16]{0:T(128)S(1)} %copy-done, bf16[16,384,128]{2,1,0:T(8,128)(2,1)S(1)} %all_to_all.15.blocks), custom_call_target="tpu_custom_call" | custom-call | tf_op jit(solution)/shard_map/unpack/pallas_call | solution.py:435
  (2 shorter events, 0.1 us)
Async XLA Ops:
  4.7 37.9 %collective-permute-start = (bf16[12,528,128]{2,1,0:T(8,128)(2,1)}, bf16[12,528,128]{2,1,0:T(8,128)(2,1)}, u32[]{:S(2)}, u32[]{:S(2)}) collective-permute-start(bf16[12,528,128]{2,1,0:T(8,128)(2,1)} %get-tuple-element.24), channel_id=1, source_target_pairs={{4,12},{5,13},{6,14},{7,15},{8,0},{9,1},{10,2},{11,3},{12,20},{13,... | collective-permute-start | bytes 4866056 | tf_op jit(solution)/shard_map/ppermute | solution.py:478
  6.0 41.6 %all-to-all-start = ((bf16[16,528,128]{2,1,0:T(8,128)(2,1)}), bf16[16,528,128]{2,1,0:T(8,128)(2,1)S(1)}, u32[]{:S(2)}, u32[]{:S(2)}) async-start(bf16[16,528,128]{2,1,0:T(8,128)(2,1)} %get-tuple-element.23), calls=%async_computation | async-start | bytes 4325376 | tf_op jit(solution)/shard_map/all_to_all | solution.py:457
  47.7 6.9 %copy-start.1 = (bf16[16,528,128]{2,1,0:T(8,128)(2,1)}, bf16[16,528,128]{2,1,0:T(8,128)(2,1)S(1)}, u32[]{:S(2)}) copy-start(bf16[16,528,128]{2,1,0:T(8,128)(2,1)S(1)} %all-to-all-done) | copy-start | bytes 6488068
  47.7 13.2 %collective-permute-start.1 = (bf16[4,2,2,528,128]{4,3,2,1,0:T(8,128)(2,1)S(1)}, bf16[4,2,2,528,128]{4,3,2,1,0:T(8,128)(2,1)}, u32[]{:S(2)}, u32[]{:S(2)}) collective-permute-start(bf16[4,2,2,528,128]{4,3,2,1,0:T(8,128)(2,1)S(1)} %bitcast.32), channel_id=1, source_target_pairs={{0,1},{1,0},{2,3},{3,2},{4,5},{5,4},{6,7},{7,6},{8,9},{9,8},{10,11... | collective-permute-start | bytes 6488072 | tf_op jit(solution)/shard_map/ppermute | solution.py:465
  50.1 38.8 %all-to-all-start.1 = ((bf16[16,528,128]{2,1,0:T(8,128)(2,1)}), bf16[16,528,128]{2,1,0:T(8,128)(2,1)}, u32[]{:S(2)}, u32[]{:S(2)}) async-start(bf16[16,528,128]{2,1,0:T(8,128)(2,1)} %refill.1), calls=%async_computation.1 | async-start | bytes 4325376 | tf_op jit(solution)/shard_map/all_to_all | solution.py:457
  54.6 25.8 %collective-permute-start.2 = (bf16[2,2,528,128]{3,2,1,0:T(8,128)(2,1)S(1)}, bf16[2,2,528,128]{3,2,1,0:T(8,128)(2,1)S(1)}, u32[]{:S(2)}, u32[]{:S(2)}) collective-permute-start(bf16[2,2,528,128]{3,2,1,0:T(8,128)(2,1)S(1)} %dynamic-slice_bitcast_fusion.1), channel_id=1, source_target_pairs={{0,128},{32,160},{64,192},{96,224},{128,0},{160,32},{192,64},{224,... | collective-permute-start | bytes 1622024 | tf_op jit(solution)/shard_map/ppermute | solution.py:483
  80.5 11.0 %copy-start.2 = (bf16[2,2,528,128]{3,2,1,0:T(8,128)(2,1)}, bf16[2,2,528,128]{3,2,1,0:T(8,128)(2,1)S(1)}, u32[]{:S(2)}) copy-start(bf16[2,2,528,128]{3,2,1,0:T(8,128)(2,1)S(1)} %collective-permute-done.2.jump) | copy-start | bytes 1622020
  80.5 10.9 %collective-permute-start.3 = (bf16[2,2,528,128]{3,2,1,0:T(8,128)(2,1)S(1)}, bf16[2,2,528,128]{3,2,1,0:T(8,128)(2,1)S(1)}, u32[]{:S(2)}, u32[]{:S(2)}) collective-permute-start(bf16[2,2,528,128]{3,2,1,0:T(8,128)(2,1)S(1)} %collective-permute-done.2.jump), channel_id=1, source_target_pairs={{0,1},{1,0},{2,3},{3,2},{4,5},{5,4},{6,7},{7,6},{8,9},{9,8},{10,11... | collective-permute-start | bytes 1622024 | tf_op jit(solution)/shard_map/ppermute | solution.py:465
  90.2 5.2 %collective-permute-start.5 = (bf16[4,2,528,128]{3,2,1,0:T(8,128)(2,1)S(1)}, bf16[4,2,528,128]{3,2,1,0:T(8,128)(2,1)}, u32[]{:S(2)}, u32[]{:S(2)}) collective-permute-start(bf16[4,2,528,128]{3,2,1,0:T(8,128)(2,1)S(1)} %dynamic-slice_bitcast_fusion), channel_id=1, source_target_pairs={{0,1},{1,0},{2,3},{3,2},{4,5},{5,4},{6,7},{7,6},{8,9},{9,8},{10,11... | collective-permute-start | bytes 3244040 | tf_op jit(solution)/shard_map/ppermute | solution.py:465
  91.4 15.2 %copy-start.3 = (bf16[2,2,528,128]{3,2,1,0:T(8,128)(2,1)}, bf16[2,2,528,128]{3,2,1,0:T(8,128)(2,1)S(1)}, u32[]{:S(2)}) copy-start(bf16[2,2,528,128]{3,2,1,0:T(8,128)(2,1)S(1)} %collective-permute-done.3.jump_swapped) | copy-start | bytes 1622020
  91.5 15.1 %collective-permute-start.4 = (bf16[2,2,528,128]{3,2,1,0:T(8,128)(2,1)S(1)}, bf16[2,2,528,128]{3,2,1,0:T(8,128)(2,1)S(1)}, u32[]{:S(2)}, u32[]{:S(2)}) collective-permute-start(bf16[2,2,528,128]{3,2,1,0:T(8,128)(2,1)S(1)} %pad_maximum_fusion.1), channel_id=1, source_target_pairs={{1,8},{8,1},{3,10},{10,3},{5,12},{12,5},{7,14},{14,7},{9,16},{16,9... | collective-permute-start | bytes 1622024 | tf_op jit(solution)/shard_map/ppermute | solution.py:472
  106.6 0.8 copy-start.4
  111.9 2.6 %collective-permute-start.6 = (bf16[4,2,384,128]{3,2,1,0:T(8,128)(2,1)}, bf16[4,2,384,128]{3,2,1,0:T(8,128)(2,1)S(1)}, u32[]{:S(2)}, u32[]{:S(2)}) collective-permute-start(bf16[4,2,384,128]{3,2,1,0:T(8,128)(2,1)} %get-tuple-element.39), channel_id=1, source_target_pairs={{0,1},{1,0},{2,3},{3,2},{4,5},{5,4},{6,7},{7,6},{8,9},{9,8},{10,11... | collective-permute-start | bytes 2359304 | tf_op jit(solution)/shard_map/ppermute | solution.py:465
  116.0 25.5 %copy-start = (s32[16]{0:T(128)S(1)}, s32[16]{0:T(128)}, u32[]{:S(2)}) copy-start(s32[16]{0:T(128)} %tile_valid.3) | copy-start | bytes 196

commit v5 on v4

--- a/solution.py
+++ b/solution.py
@@ -18,6 +18,7 @@
 STAT_ROWS = 16
 KEY, VALUE, QUERY, GRAD, STAT = (part * TOKENS for part in range(5))
 ROWS = STAT + STAT_ROWS
+RAW = GRAD
 SCALE = 1.0 / math.sqrt(HEAD_DIM)
 LOG2E = math.log2(math.e)
 VMEM_LIMIT = 56 * 1024 * 1024
@@ -61,12 +62,7 @@
         out[head, start : start + TOKENS, :] = moved[:, head * HEAD_DIM : (head + 1) * HEAD_DIM]
 
 
-def fill(heads, out):
-    out[:HEADS] = heads[...]
-    out[HEADS:] = jnp.zeros((CHIPS - HEADS,) + out.shape[1:], jnp.bfloat16)
-
-
-def pack_kernel(tile_valid, key, value, query, grad, log_norm, delta, out, filled, table):
+def pack_kernel(tile_valid, key, value, query, grad, log_norm, delta, out, raw, table):
     matrix = keep_matrix(tile_valid, 1)
     for start, ref in ((KEY, key), (VALUE, value), (QUERY, query), (GRAD, grad)):
         pack_part(matrix, start, ref, out)
@@ -79,18 +75,20 @@
             turned = dot(matrix, piece).T
             for head in range(HEADS):
                 table[head, base + step : base + step + 1, :] = turned[head : head + 1, :]
-    out[:, STAT:, :] = table[...].astype(jnp.bfloat16)
-    fill(out, filled)
-
-
-HEADS_SHAPE = jax.ShapeDtypeStruct((HEADS, ROWS, HEAD_DIM), jnp.bfloat16)
-FILLED_SHAPE = jax.ShapeDtypeStruct((CHIPS, ROWS, HEAD_DIM), jnp.bfloat16)
+    out[:HEADS, STAT:, :] = table[...].astype(jnp.bfloat16)
+    out[HEADS:] = jnp.zeros((CHIPS - HEADS,) + out.shape[1:], jnp.bfloat16)
+    raw[...] = out[:HEADS, :RAW, :]
+
+
+PACKED_SHAPE = jax.ShapeDtypeStruct((CHIPS, ROWS, HEAD_DIM), jnp.bfloat16)
+RAW_SHAPE = jax.ShapeDtypeStruct((HEADS, RAW, HEAD_DIM), jnp.bfloat16)
+FILLED_SHAPE = jax.ShapeDtypeStruct((CHIPS, RAW, HEAD_DIM), jnp.bfloat16)
 
 
 def pack(tile_valid, *arrays):
     return pl.pallas_call(
         pack_kernel,
-        out_shape=[HEADS_SHAPE, FILLED_SHAPE],
+        out_shape=[PACKED_SHAPE, RAW_SHAPE],
         in_specs=[SMEM_SPEC] + vmem_specs(len(arrays)),
         out_specs=vmem_specs(2),
         scratch_shapes=[pltpu.VMEM((HEADS, STAT_ROWS, TOKENS), jnp.float32)],
@@ -227,8 +225,8 @@
     return lambda block, lo, hi: ref[(block % 2, *index, block // 2, slice(lo, hi))]
 
 
-def by_column(ref, *index):
-    return lambda block, lo, hi: ref[(*index, block // 2, block % 2, slice(lo, hi))]
+def by_either(raw, rest):
+    return lambda block, lo, hi: raw(block, lo, hi) if hi <= RAW else rest(block, lo - RAW, hi - RAW)
 
 
 def frames_near(frame):
@@ -244,18 +242,13 @@
     scratch[1 - core] = swapped
 
 
-def first_query_kernel(arrived, swapped, total, blocks):
+def first_kernel(arrived, swapped, query_total, key_total, value_total, blocks):
     core = lax.axis_index("space") % 2
     place(blocks, core, arrived[...], swapped[...])
     for frame in range(FRAMES):
         nears = [by_core(blocks, f, row) for f in frames_near(frame) for row in range(2)]
         for column in range(BLOCKS):
-            total[frame, column] = query_sum(by_core(blocks, frame, core), nears, column)
-
-
-def first_key_kernel(arrived, swapped, key_total, value_total, blocks):
-    core = lax.axis_index("space") % 2
-    place(blocks, core, arrived[...], swapped[...])
+            query_total[frame, column] = query_sum(by_core(blocks, frame, core), nears, column)
     key_total[...] = jnp.zeros_like(key_total)
     value_total[...] = jnp.zeros_like(value_total)
     for column in range(BLOCKS):
@@ -266,6 +259,20 @@
             add_key_sums((key_total, value_total), frames, column, parts)
 
 
+def rest_kernel(arrived, swapped, out, sems):
+    core = lax.axis_index("space") % 2
+    rows = pl.ds(RAW, ROWS - RAW)
+    wait_all(
+        start_all(
+            [
+                (arrived.at[:, core, :, rows], out.at[core]),
+                (swapped.at[:, core, :, rows], out.at[1 - core]),
+            ],
+            sems,
+        )
+    )
+
+
 def start_all(moves, sems):
     copies = [pltpu.make_async_copy(*move, sems.at[i]) for i, move in enumerate(moves)]
     for copy in copies:
@@ -284,42 +291,47 @@
         done[column % 2, ..., column // 2, rows, :] = ((total + first) * scale).astype(jnp.bfloat16)
 
 
-def row_kernel(arrived, swapped, row, row_swapped, *rest):
+def row_kernel(arrived, swapped, row, row_swapped, row_rest, *rest):
     firsts, (mine, other, edges), rest = rest[:3], rest[3:6], rest[6:]
-    own, near, done, first_totals, *totals, sems = rest
+    own, near_raw, near_rest, done, first_totals, *totals, sems = rest
     core = lax.axis_index("space") % 2
     copies = start_all(
         [
             (arrived.at[:, core], own.at[core]),
             (swapped.at[:, core], own.at[1 - core]),
-            (row.at[:, 1 - core], near.at[core]),
-            (row_swapped, near.at[1 - core]),
+            (row.at[:, 1 - core], near_raw.at[core]),
+            (row_swapped, near_raw.at[1 - core]),
+            (row_rest, near_rest),
         ]
         + [(first, first_totals.at[i]) for i, first in enumerate(firsts)],
         sems,
     )
+
+    def near(frame):
+        return by_either(by_core(near_raw, frame), by_core(near_rest, frame))
+
     for total in totals[1:]:
         total[...] = jnp.zeros_like(total)
-    wait_all(copies[:4])
+    wait_all(copies[:5])
     for column in range(BLOCKS):
         for f in range(FRAMES):
             frames = frames_near(f)
             owns = [by_core(own, frame) for frame in frames]
-            parts = key_sum(owns, [by_core(near, f)], column)
+            parts = key_sum(owns, [near(f)], column)
             add_key_sums(totals[1:], frames, column, parts)
     for frame in range(FRAMES):
-        nears = [by_core(near, f) for f in frames_near(frame)]
+        nears = [near(f) for f in frames_near(frame)]
         for column in range(BLOCKS):
             totals[0][frame, column] = query_sum(by_core(own, frame), nears, column)
-    wait_all(copies[4:])
+    wait_all(copies[5:])
     for column in range(BLOCKS):
         sums = [total[:, column] for total in totals]
         finish(sums, [first_totals[part, :, column] for part in range(3)], column, done)
-    mine[...] = done[core]
-    other[...] = done[1 - core]
+    copies = start_all([(done.at[core], mine), (done.at[1 - core], other)], sems)
     edge = edge_frame()
     for part, total in enumerate(totals):
         edges[part] = total[edge] + first_totals[part, edge]
+    wait_all(copies)
 
 
 def jump_kernel(arrived, swapped, jump, jump_swapped, jump_row, edges, mine_in, other_in, *rest):
@@ -338,19 +350,19 @@
         sems,
     )
     wait_all(copies)
-    jumps = [by_core(jumped, 0), by_core(jumped, 1), by_column(jumped_row)]
+    jumps = [by_core(jumped, 0), by_core(jumped, 1), by_core(jumped_row)]
     for column in range(BLOCKS):
         parts = (query_sum(by_core(own), jumps, column), *key_sum([by_core(own)], jumps, column))
         finish(parts, [sums[part, column] for part in range(3)], column, done)
     wait_all(start_all([(done.at[core], mine.at[edge]), (done.at[1 - core], other.at[edge])], sems))
 
 
-KERNEL_FLOPS = 1 << 10
+BORDER_FLOPS = 1 << 33
 TOTALS = (FRAMES, BLOCKS, TOKENS, HEAD_DIM)
 DONE = (FRAMES, 2, 3 * TOKENS, HEAD_DIM)
 
 
-def attend(kernel, name, args, in_specs, out_specs, out_shape, scratch, aliases=None):
+def attend(kernel, name, args, in_specs, out_specs, out_shape, scratch, aliases=None, flops=1 << 10, vmem=56):
     return pl.pallas_call(
         kernel,
         out_shape=out_shape,
@@ -358,9 +370,9 @@
         out_specs=out_specs,
         scratch_shapes=scratch,
         input_output_aliases=aliases or {},
-        compiler_params=params(),
+        compiler_params=pltpu.CompilerParams(vmem_limit_bytes=vmem << 20),
         cost_estimate=pl.CostEstimate(
-            flops=KERNEL_FLOPS, bytes_accessed=KERNEL_FLOPS, transcendentals=0
+            flops=flops, bytes_accessed=flops >> 8, transcendentals=0
         ),
         name=name,
     )(*args)
@@ -370,16 +382,47 @@
     return [pl.BlockSpec(memory_space=pl.ANY)] * count
 
 
-def first_part(kernel, name, parts, *args):
+def first_part(*args):
     return attend(
-        kernel,
-        name,
+        first_kernel,
+        "first_part",
         args,
         vmem_specs(len(args)),
-        vmem_specs(parts),
-        [jax.ShapeDtypeStruct(TOTALS, jnp.float32)] * parts,
+        vmem_specs(3),
+        [jax.ShapeDtypeStruct(TOTALS, jnp.float32)] * 3,
         [pltpu.VMEM((2, FRAMES, 2, 2, ROWS, HEAD_DIM), jnp.bfloat16)],
     )
+
+
+def border_kernel(jump, jump_swapped, out):
+    core = lax.axis_index("space") % 2
+    place(out, core, jump[core], jump_swapped[core])
+
+
+def border_part(*args):
+    return attend(
+        border_kernel,
+        "border_part",
+        args,
+        vmem_specs(len(args)),
+        vmem_specs(1),
+        [jax.ShapeDtypeStruct((2, 2, ROWS, HEAD_DIM), jnp.bfloat16)],
+        [],
+        flops=BORDER_FLOPS,
+        vmem=8,
+    )[0]
+
+
+def rest_part(*args):
+    return attend(
+        rest_kernel,
+        "rest_part",
+        args,
+        any_specs(len(args)),
+        vmem_specs(1),
+        [jax.ShapeDtypeStruct((2, FRAMES, 2, ROWS - RAW, HEAD_DIM), jnp.bfloat16)],
+        [pltpu.SemaphoreType.DMA((len(args),))],
+    )[0]
 
 
 def row_part(*args):
@@ -388,17 +431,19 @@
         "row_part",
         args,
         any_specs(len(args)),
-        vmem_specs(3),
+        any_specs(2) + vmem_specs(1),
         [jax.ShapeDtypeStruct(DONE, jnp.bfloat16)] * 2
         + [jax.ShapeDtypeStruct((3, *TOTALS[1:]), jnp.float32)],
         [
             pltpu.VMEM((2, FRAMES, 2, ROWS, HEAD_DIM), jnp.bfloat16),
-            pltpu.VMEM((2, FRAMES, 2, ROWS, HEAD_DIM), jnp.bfloat16),
+            pltpu.VMEM((2, FRAMES, 2, RAW, HEAD_DIM), jnp.bfloat16),
+            pltpu.VMEM((2, FRAMES, 2, ROWS - RAW, HEAD_DIM), jnp.bfloat16),
             pltpu.VMEM((2, *DONE), jnp.bfloat16),
             pltpu.VMEM((3, *TOTALS), jnp.float32),
         ]
         + [pltpu.VMEM(TOTALS, jnp.float32)] * 3
         + [pltpu.SemaphoreType.DMA((len(args),))],
+        vmem=32,
     )
 
 
@@ -419,6 +464,7 @@
             pltpu.SemaphoreType.DMA((len(args),)),
         ],
         {6: 0, 7: 1},
+        vmem=16,
     )
 
 
@@ -489,12 +535,6 @@
     return jnp.stack([first, second], axis=axis)
 
 
-def own_row(core, arrived, swapped, axis):
-    mine = lax.dynamic_index_in_dim(arrived, core, axis, keepdims=False)
-    other = lax.dynamic_index_in_dim(swapped, core, axis, keepdims=False)
-    return two_ways(core, mine, other, axis + 1)
-
-
 def shards(query, key, value, grad_out, log_norm, delta, tile_valid):
     core = lax.axis_index("space") % 2
     shape = query.shape
@@ -502,25 +542,26 @@
     def flat(array):
         return array.reshape(TOKENS, array.shape[-1])
 
-    heads, packed = pack(
+    packed, raw = pack(
         tile_valid, *(flat(v) for v in (key, value, query, grad_out, log_norm, delta))
     )
-    shifted = refill(row_shift(heads))
+    shifted = refill(row_shift(raw))
     arrived = plane_exchange(packed)
     arrived, shifted = lax.optimization_barrier((arrived, shifted))
     arrived = arrived.reshape(FRAMES, 2, 2, ROWS, HEAD_DIM)
     jump = half_swap(lax.dynamic_index_in_dim(arrived, edge_frame(), 0, keepdims=False))
     swapped = core_swap(arrived)
-    row = plane_exchange(shifted).reshape(FRAMES, 2, 2, ROWS, HEAD_DIM)
-    firsts = [
-        *first_part(first_query_kernel, "first_query", 1, arrived, swapped),
-        *first_part(first_key_kernel, "first_key", 2, arrived, swapped),
-    ]
+    row = plane_exchange(shifted).reshape(FRAMES, 2, 2, RAW, HEAD_DIM)
+    row_rest = row_swap(rest_part(arrived, swapped))
+    firsts = first_part(arrived, swapped)
     jump, firsts = lax.optimization_barrier((jump, firsts))
     jump_swapped = core_swap(jump)
-    jump_row = row_swap(own_row(core, jump, jump_swapped, 0))
+    jump_swapped, row_rest = lax.optimization_barrier((jump_swapped, row_rest))
+    border = border_part(jump, jump_swapped)
+    row, border = lax.optimization_barrier((row, border))
+    jump_row = row_swap(border)
     row_swapped = core_swap(lax.dynamic_index_in_dim(row, core, 1, keepdims=False))
-    mine, other, edges = row_part(arrived, swapped, row, row_swapped, *firsts)
+    mine, other, edges = row_part(arrived, swapped, row, row_swapped, row_rest, *firsts)
     jump_row, edges = lax.optimization_barrier((jump_row, edges))
     mine, other = jump_part(
         arrived, swapped, jump, jump_swapped, jump_row, edges, mine, other

time: 144 us -> 140 us (0.972)
  local copies, waits for them, and re-layouts: 2.32 us -> 8.42 us
  Pallas kernels: 43.5 us -> 39.3 us
  waiting for transfers between devices: 38.4 us -> 34.8 us
    ppermute x1, waiting for transfers between devices: 25.6 us -> 17.1 us  [row_shift(): lax.ppermute(array, 'space', [(a, b) for a, b in route if 0 <= b < count])]
    unnamed x10 -> x26, local copies, waits for them, and re-layouts: 0.83 us -> 6.17 us
    pallas_call x4 -> x5, Pallas kernels: 35.1 us -> 31.6 us  [attend(): pl.pallas_call(kernel, out_shape=out_shape, in_specs=in_specs, out_specs=...]
    ppermute x1 -> x2, waiting for transfers between devices: 0.01 us -> 3.05 us  [row_swap(): return lax.ppermute(array, 'space', route)]
    ppermute x1 -> x2, starting transfers between devices: 3.95 us -> 6.65 us  [row_swap(): return lax.ppermute(array, 'space', route)]
    ppermute x4, waiting for transfers between devices: 2.49 us -> 4.39 us  [core_swap(): lax.ppermute(array, 'space', [(s, s ^ 1) for s in range(lax.axis_size('sp...]
    ppermute x4, starting transfers between devices: 4.41 us -> 2.61 us  [core_swap(): lax.ppermute(array, 'space', [(s, s ^ 1) for s in range(lax.axis_size('sp...]
  transfers between devices with their start and end apart: 9 -> 10, of which waited for: 4 -> 5; matrix products, arithmetic and copies ran while one was open for 1% -> 1% of each run, Pallas kernels for 23% -> 21%
where the time goes in v5:
time: 140 us
  Pallas kernels  39.3 us (28%)
  waiting for transfers between devices  34.8 us (25%)
  starting transfers between devices  30.9 us (22%)
  blocking collectives  25.2 us (18%)
  local copies, waits for them, and re-layouts  8.42 us (6%)
    pallas_call x5, Pallas kernels, attend(): pl.pallas_call(kernel, out_shape=out_shape, in_specs=in_specs, out_specs=...  31.6 us
    all_to_all x1, blocking collectives, plane_exchange(): return lax.all_to_all(array, AXES, 0, 0, axis_index_groups=groups)  25.2 us
    ppermute x1, waiting for transfers between devices, row_shift(): lax.ppermute(array, 'space', [(a, b) for a, b in route if 0 <= b < count])  17.1 us
    all_to_all x2, starting transfers between devices, plane_exchange(): return lax.all_to_all(array, AXES, 0, 0, axis_index_groups=groups)  14.3 us
    all_to_all x2, waiting for transfers between devices, plane_exchange(): return lax.all_to_all(array, AXES, 0, 0, axis_index_groups=groups)  10.2 us
    ppermute x2, starting transfers between devices, row_swap(): return lax.ppermute(array, 'space', route)  6.65 us
    unnamed x26, local copies, waits for them, and re-layouts  6.17 us
    ppermute x1, starting transfers between devices, half_swap(): lax.ppermute(array, 'frame', [(f, (f + FRAMES) % count) for f in range(co...  6.02 us
  transfers between devices with their start and end apart: 10, of which 5 were waited for; matrix products, arithmetic and copies ran while one was open for 1% of the time, Pallas kernels for 21%

profile of v5, /device:TPU:1, one launch (start us, length us, event | category | flops | bytes accessed | tf_op | source)
XLA Modules:
  0.0 139.7 jit_solution(3910007323735883068)
XLA Ops:
  0.6 3.7 %pack.1 = (bf16[16,528,128]{2,1,0:T(8,128)(2,1)}, bf16[12,384,128]{2,1,0:T(8,128)(2,1)}) custom-call(s32[16]{0:T(128)} %tile_valid.3, bf16[128,1536]{1,0:T(8,128)(2,1)} %bitcast.33, bf16[128,1536]{1,0:T(8,128)(2,1)} %bitcast.34, bf16[128,1536]{1,0:T(8,128)(2,1)} %bitcast.35, bf16[128,1536]{1,0:T(8,128)(2,1)} %bitcast.36, f32[128,12]{1,0:T(8,128)} %bitcast.37, ...), custom_call_target="tpu_custom_call" | custom-call | tf_op jit(solution)/shard_map/pack/pallas_call | solution.py:89
  4.4 1.3 collective-permute-start
  5.7 9.9 %all-to-all-start = ((bf16[16,528,128]{2,1,0:T(8,128)(2,1)}), bf16[16,528,128]{2,1,0:T(8,128)(2,1)S(1)}, u32[]{:S(2)}, u32[]{:S(2)}) async-start(bf16[16,528,128]{2,1,0:T(8,128)(2,1)} %get-tuple-element.28), calls=%async_computation | async-start | bytes 4325376 | tf_op jit(solution)/shard_map/all_to_all | solution.py:503
  15.6 17.1 %collective-permute-done.heads = bf16[12,384,128]{2,1,0:T(8,128)(2,1)S(1)} collective-permute-done((bf16[12,384,128]{2,1,0:T(8,128)(2,1)}, bf16[12,384,128]{2,1,0:T(8,128)(2,1)S(1)}, u32[]{:S(2)}, u32[]{:S(2)}) %collective-permute-start) | collective-permute-done | bytes 1179680 | tf_op jit(solution)/shard_map/ppermute | solution.py:524
  32.7 0.0 copy-start.12
  32.7 1.1 copy-done.12
  33.8 2.2 %refill.1 = bf16[16,384,128]{2,1,0:T(8,128)(2,1)} custom-call(bf16[12,384,128]{2,1,0:T(8,128)(2,1)} %copy-done.12), custom_call_target="tpu_custom_call" | custom-call | flops 17179869184 | bytes 67108864 | tf_op jit(solution)/shard_map/refill/pallas_call | solution.py:123
  36.0 10.2 %all-to-all-done = bf16[16,528,128]{2,1,0:T(8,128)(2,1)S(1)} async-done(((bf16[16,528,128]{2,1,0:T(8,128)(2,1)}), bf16[16,528,128]{2,1,0:T(8,128)(2,1)S(1)}, u32[]{:S(2)}, u32[]{:S(2)}) %all-to-all-start) | async-done | bytes 2162720 | tf_op jit(solution)/shard_map/all_to_all | solution.py:503
  46.2 0.0 copy-start
  46.2 2.4 %collective-permute-start.1 = (bf16[4,2,2,528,128]{4,3,2,1,0:T(8,128)(2,1)S(1)}, bf16[4,2,2,528,128]{4,3,2,1,0:T(8,128)(2,1)}, u32[]{:S(2)}, u32[]{:S(2)}) collective-permute-start(bf16[4,2,2,528,128]{4,3,2,1,0:T(8,128)(2,1)S(1)} %bitcast.26), channel_id=1, source_target_pairs={{0,1},{1,0},{2,3},{3,2},{4,5},{5,4},{6,7},{7,6},{8,9},{9,8},{10,11... | collective-permute-start | bytes 6488072 | tf_op jit(solution)/shard_map/ppermute | solution.py:511
  48.6 0.8 dynamic-slice_bitcast_fusion.1
  49.5 6.0 %collective-permute-start.2 = (bf16[2,2,528,128]{3,2,1,0:T(8,128)(2,1)}, bf16[2,2,528,128]{3,2,1,0:T(8,128)(2,1)S(1)}, u32[]{:S(2)}, u32[]{:S(2)}) collective-permute-start(bf16[2,2,528,128]{3,2,1,0:T(8,128)(2,1)} %dynamic-slice_bitcast_fusion.1), channel_id=1, source_target_pairs={{0,128},{32,160},{64,192},{96,224},{128,0},{160,32},{192,64},{224,... | collective-permute-start | bytes 1622024 | tf_op jit(solution)/shard_map/ppermute | solution.py:529
  55.5 0.0 copy-done
  55.5 4.4 %all-to-all-start.1 = ((bf16[16,384,128]{2,1,0:T(8,128)(2,1)}), bf16[16,384,128]{2,1,0:T(8,128)(2,1)}, u32[]{:S(2)}, u32[]{:S(2)}) async-start(bf16[16,384,128]{2,1,0:T(8,128)(2,1)} %refill.1), calls=%async_computation.1 | async-start | bytes 3145728 | tf_op jit(solution)/shard_map/all_to_all | solution.py:503
  59.9 0.0 collective-permute-done.1.swapped
  59.9 1.9 %rest_part.1 = bf16[2,4,2,144,128]{4,3,2,1,0:T(8,128)(2,1)} custom-call(bf16[4,2,2,528,128]{4,3,2,1,0:T(8,128)(2,1)} %bitcast.28, bf16[4,2,2,528,128]{4,3,2,1,0:T(8,128)(2,1)} %collective-permute-done.1.swapped), custom_call_target="tpu_custom_call" | custom-call | flops 1024 | bytes 4 | tf_op jit(solution)/shard_map/rest_part/pallas_call | solution.py:366
  61.8 3.0 %collective-permute-start.4 = (bf16[2,4,2,144,128]{4,3,2,1,0:T(8,128)(2,1)}, bf16[2,4,2,144,128]{4,3,2,1,0:T(8,128)(2,1)S(1)}, u32[]{:S(2)}, u32[]{:S(2)}) collective-permute-start(bf16[2,4,2,144,128]{4,3,2,1,0:T(8,128)(2,1)} %rest_part.1), channel_id=1, source_target_pairs={{1,8},{8,1},{3,10},{10,3},{5,12},{12,5},{7,14},{14,7},{9,16},{16,9... | collective-permute-start | bytes 1769480 | tf_op jit(solution)/shard_map/ppermute | solution.py:518
  64.8 15.9 %first_part.1 = (f32[4,4,128,128]{3,2,1,0:T(8,128)}, f32[4,4,128,128]{3,2,1,0:T(8,128)}, f32[4,4,128,128]{3,2,1,0:T(8,128)}) custom-call(bf16[4,2,2,528,128]{4,3,2,1,0:T(8,128)(2,1)} %bitcast.29, bf16[4,2,2,528,128]{4,3,2,1,0:T(8,128)(2,1)} %collective-permute-done.1.swapped), custom_call_target="tpu_custom_call" | custom-call | flops 1024 | bytes 4 | tf_op jit(solution)/shard_map/first_part/pallas_call | solution.py:366
  80.7 0.0 collective-permute-done.2.jump
  80.8 0.0 copy-start.5
  80.8 0.0 collective-permute-start.3
  80.8 1.9 %collective-permute-done.3.jump_swapped = bf16[2,2,528,128]{3,2,1,0:T(8,128)(2,1)S(1)} collective-permute-done((bf16[2,2,528,128]{3,2,1,0:T(8,128)(2,1)S(1)}, bf16[2,2,528,128]{3,2,1,0:T(8,128)(2,1)S(1)}, u32[]{:S(2)}, u32[]{:S(2)}) %collective-permute-start.3) | collective-permute-done | bytes 540704 | tf_op jit(solution)/shard_map/ppermute | solution.py:511
  82.7 0.0 copy-start.7
  82.7 0.8 copy-done.7
  83.5 3.1 %collective-permute-done.4.row_rest = bf16[2,4,2,144,128]{4,3,2,1,0:T(8,128)(2,1)S(1)} collective-permute-done((bf16[2,4,2,144,128]{4,3,2,1,0:T(8,128)(2,1)}, bf16[2,4,2,144,128]{4,3,2,1,0:T(8,128)(2,1)S(1)}, u32[]{:S(2)}, u32[]{:S(2)}) %collective-permute-start.4) | collective-permute-done | bytes 589856 | tf_op jit(solution)/shard_map/ppermute | solution.py:518
  86.5 0.0 copy-start.8
  86.5 1.0 copy-done.8
  87.6 0.0 copy-start.1
  87.6 0.0 copy-done.5
  87.6 0.0 copy-start.11
  87.7 0.8 copy-done.11
  88.4 0.0 all-to-all-done.1
  88.5 0.0 copy-start.2
  88.5 1.3 dynamic-slice_bitcast_fusion
  89.7 0.1 collective-permute-start.6
  89.8 3.7 %collective-permute-start.5 = (bf16[2,2,528,128]{3,2,1,0:T(8,128)(2,1)}, bf16[2,2,528,128]{3,2,1,0:T(8,128)(2,1)S(1)}, u32[]{:S(2)}, u32[]{:S(2)}) collective-permute-start(bf16[2,2,528,128]{3,2,1,0:T(8,128)(2,1)} %copy-done.11), channel_id=1, source_target_pairs={{1,8},{8,1},{3,10},{10,3},{5,12},{12,5},{7,14},{14,7},{9,16},{16,9... | collective-permute-start | bytes 1622024 | tf_op jit(solution)/shard_map/ppermute | solution.py:518
  93.5 0.0 collective-permute-done.6.row_swapped
  93.5 0.0 copy-done.1
  93.5 0.0 copy-done.2
  93.5 0.0 copy-start.3
  93.5 1.2 copy-done.3
  94.8 0.0 copy-start.4
  94.8 1.2 copy-done.4
  96.0 0.0 copy-start.6
  96.0 0.0 copy-start.9
  96.0 9.8 %row_part.1 = (bf16[4,2,384,128]{3,2,1,0:T(8,128)(2,1)S(1)}, bf16[4,2,384,128]{3,2,1,0:T(8,128)(2,1)}, f32[3,4,128,128]{3,2,1,0:T(8,128)S(1)}) custom-call(bf16[4,2,2,528,128]{4,3,2,1,0:T(8,128)(2,1)S(1)} %bitcast.30, bf16[4,2,2,528,128]{4,3,2,1,0:T(8,128)(2,1)} %collective-permute-done.1.swapped, bf16[4,2,2,384,128]{4,3,2,1,0:T(8,128)(2,1)} %bitcast.8.row, ...), custom_call_target="tpu_custom_call" | custom-call | flops 1024 | bytes 4 | tf_op jit(solution)/shard_map/row_part/pallas_call | solution.py:366
  105.8 0.0 collective-permute-done.5.jump_row
  105.8 0.0 copy-done.6
  105.8 0.0 copy-done.9
  105.8 3.9 %jump_part.1 = (bf16[4,2,384,128]{3,2,1,0:T(8,128)(2,1)S(1)}, bf16[4,2,384,128]{3,2,1,0:T(8,128)(2,1)}) custom-call(bf16[4,2,2,528,128]{4,3,2,1,0:T(8,128)(2,1)S(1)} %bitcast.31, bf16[4,2,2,528,128]{4,3,2,1,0:T(8,128)(2,1)} %collective-permute-done.1.swapped, bf16[2,2,528,128]{3,2,1,0:T(8,128)(2,1)S(1)} %copy-done.6, ...), custom_call_target="tpu_custom_call", output_to_operand_aliasing={{0}: (6, {}), {1}: (7, {})} | custom-call | flops 1024 | bytes 4 | tf_op jit(solution)/shard_map/jump_part/pallas_call | solution.py:366
  109.7 0.1 collective-permute-start.7
  109.8 2.5 %collective-permute-done.7 = bf16[4,2,384,128]{3,2,1,0:T(8,128)(2,1)S(1)} collective-permute-done((bf16[4,2,384,128]{3,2,1,0:T(8,128)(2,1)}, bf16[4,2,384,128]{3,2,1,0:T(8,128)(2,1)S(1)}, u32[]{:S(2)}, u32[]{:S(2)}) %collective-permute-start.7) | collective-permute-done | bytes 786464 | tf_op jit(solution)/shard_map/ppermute | solution.py:511
  112.3 0.1 select_bitcast_fusion.1
  112.4 0.1 pad_maximum_fusion
  112.6 0.1 copy.12
  112.7 0.0 copy-start.10
  112.7 25.2 %all_to_all.15.blocks = bf16[16,384,128]{2,1,0:T(8,128)(2,1)S(1)} all-to-all(bf16[16,384,128]{2,1,0:T(8,128)(2,1)S(1)} %bitcast.32), channel_id=1, replica_groups={{0,2,4,6,32,34,36,38,64,66,68,70,96,98,100,102},{1,3,5,7,33,35,37,39,65..., dimensions={0} | all-to-all | bytes 3145728 | tf_op jit(solution)/shard_map/all_to_all | solution.py:503
  137.9 0.0 copy-done.10
  137.9 1.8 %unpack.1 = (bf16[128,1536]{1,0:T(8,128)(2,1)}, bf16[128,1536]{1,0:T(8,128)(2,1)}, bf16[128,1536]{1,0:T(8,128)(2,1)}) custom-call(s32[16]{0:T(128)S(1)} %copy-done.10, bf16[16,384,128]{2,1,0:T(8,128)(2,1)S(1)} %all_to_all.15.blocks), custom_call_target="tpu_custom_call" | custom-call | tf_op jit(solution)/shard_map/unpack/pallas_call | solution.py:481
  (1 shorter events, 0.0 us)
Async XLA Ops:
  4.4 28.3 %collective-permute-start = (bf16[12,384,128]{2,1,0:T(8,128)(2,1)}, bf16[12,384,128]{2,1,0:T(8,128)(2,1)S(1)}, u32[]{:S(2)}, u32[]{:S(2)}) collective-permute-start(bf16[12,384,128]{2,1,0:T(8,128)(2,1)} %get-tuple-element.29), channel_id=1, source_target_pairs={{4,12},{5,13},{6,14},{7,15},{8,0},{9,1},{10,2},{11,3},{12,20},{13,... | collective-permute-start | bytes 3538952 | tf_op jit(solution)/shard_map/ppermute | solution.py:524
  5.7 40.5 %all-to-all-start = ((bf16[16,528,128]{2,1,0:T(8,128)(2,1)}), bf16[16,528,128]{2,1,0:T(8,128)(2,1)S(1)}, u32[]{:S(2)}, u32[]{:S(2)}) async-start(bf16[16,528,128]{2,1,0:T(8,128)(2,1)} %get-tuple-element.28), calls=%async_computation | async-start | bytes 4325376 | tf_op jit(solution)/shard_map/all_to_all | solution.py:503
  32.7 1.1 copy-start.12
  46.2 9.3 %copy-start = (bf16[16,528,128]{2,1,0:T(8,128)(2,1)}, bf16[16,528,128]{2,1,0:T(8,128)(2,1)S(1)}, u32[]{:S(2)}) copy-start(bf16[16,528,128]{2,1,0:T(8,128)(2,1)S(1)} %all-to-all-done) | copy-start | bytes 6488068
  46.2 13.7 %collective-permute-start.1 = (bf16[4,2,2,528,128]{4,3,2,1,0:T(8,128)(2,1)S(1)}, bf16[4,2,2,528,128]{4,3,2,1,0:T(8,128)(2,1)}, u32[]{:S(2)}, u32[]{:S(2)}) collective-permute-start(bf16[4,2,2,528,128]{4,3,2,1,0:T(8,128)(2,1)S(1)} %bitcast.26), channel_id=1, source_target_pairs={{0,1},{1,0},{2,3},{3,2},{4,5},{5,4},{6,7},{7,6},{8,9},{9,8},{10,11... | collective-permute-start | bytes 6488072 | tf_op jit(solution)/shard_map/ppermute | solution.py:511
  49.5 31.3 %collective-permute-start.2 = (bf16[2,2,528,128]{3,2,1,0:T(8,128)(2,1)}, bf16[2,2,528,128]{3,2,1,0:T(8,128)(2,1)S(1)}, u32[]{:S(2)}, u32[]{:S(2)}) collective-permute-start(bf16[2,2,528,128]{3,2,1,0:T(8,128)(2,1)} %dynamic-slice_bitcast_fusion.1), channel_id=1, source_target_pairs={{0,128},{32,160},{64,192},{96,224},{128,0},{160,32},{192,64},{224,... | collective-permute-start | bytes 1622024 | tf_op jit(solution)/shard_map/ppermute | solution.py:529
  55.5 33.0 %all-to-all-start.1 = ((bf16[16,384,128]{2,1,0:T(8,128)(2,1)}), bf16[16,384,128]{2,1,0:T(8,128)(2,1)}, u32[]{:S(2)}, u32[]{:S(2)}) async-start(bf16[16,384,128]{2,1,0:T(8,128)(2,1)} %refill.1), calls=%async_computation.1 | async-start | bytes 3145728 | tf_op jit(solution)/shard_map/all_to_all | solution.py:503
  61.8 24.7 %collective-permute-start.4 = (bf16[2,4,2,144,128]{4,3,2,1,0:T(8,128)(2,1)}, bf16[2,4,2,144,128]{4,3,2,1,0:T(8,128)(2,1)S(1)}, u32[]{:S(2)}, u32[]{:S(2)}) collective-permute-start(bf16[2,4,2,144,128]{4,3,2,1,0:T(8,128)(2,1)} %rest_part.1), channel_id=1, source_target_pairs={{1,8},{8,1},{3,10},{10,3},{5,12},{12,5},{7,14},{14,7},{9,16},{16,9... | collective-permute-start | bytes 1769480 | tf_op jit(solution)/shard_map/ppermute | solution.py:518
  80.8 6.9 %copy-start.5 = (bf16[2,2,528,128]{3,2,1,0:T(8,128)(2,1)}, bf16[2,2,528,128]{3,2,1,0:T(8,128)(2,1)S(1)}, u32[]{:S(2)}) copy-start(bf16[2,2,528,128]{3,2,1,0:T(8,128)(2,1)S(1)} %collective-permute-done.2.jump) | copy-start | bytes 1622020
  80.8 1.9 %collective-permute-start.3 = (bf16[2,2,528,128]{3,2,1,0:T(8,128)(2,1)S(1)}, bf16[2,2,528,128]{3,2,1,0:T(8,128)(2,1)S(1)}, u32[]{:S(2)}, u32[]{:S(2)}) collective-permute-start(bf16[2,2,528,128]{3,2,1,0:T(8,128)(2,1)S(1)} %collective-permute-done.2.jump), channel_id=1, source_target_pairs={{0,1},{1,0},{2,3},{3,2},{4,5},{5,4},{6,7},{7,6},{8,9},{9,8},{10,11... | collective-permute-start | bytes 1622024 | tf_op jit(solution)/shard_map/ppermute | solution.py:511
  82.7 0.8 copy-start.7
  86.5 1.0 copy-start.8
  87.6 5.9 %copy-start.1 = (bf16[16,528,128]{2,1,0:T(8,128)(2,1)S(1)}, bf16[16,528,128]{2,1,0:T(8,128)(2,1)}, u32[]{:S(2)}) copy-start(bf16[16,528,128]{2,1,0:T(8,128)(2,1)} %copy-done) | copy-start | bytes 6488068
  87.6 0.8 copy-start.11
  88.5 5.1 %copy-start.2 = (f32[4,4,128,128]{3,2,1,0:T(8,128)S(1)}, f32[4,4,128,128]{3,2,1,0:T(8,128)}, u32[]{:S(2)}) copy-start(f32[4,4,128,128]{3,2,1,0:T(8,128)} %get-tuple-element.40.rest_0_) | copy-start | bytes 3145732
  89.7 3.8 %collective-permute-start.6 = (bf16[4,2,384,128]{3,2,1,0:T(8,128)(2,1)S(1)}, bf16[4,2,384,128]{3,2,1,0:T(8,128)(2,1)S(1)}, u32[]{:S(2)}, u32[]{:S(2)}) collective-permute-start(bf16[4,2,384,128]{3,2,1,0:T(8,128)(2,1)S(1)} %dynamic-slice_bitcast_fusion), channel_id=1, source_target_pairs={{0,1},{1,0},{2,3},{3,2},{4,5},{5,4},{6,7},{7,6},{8,9},{9,8},{10,11... | collective-permute-start | bytes 2359304 | tf_op jit(solution)/shard_map/ppermute | solution.py:511
  89.8 16.0 %collective-permute-start.5 = (bf16[2,2,528,128]{3,2,1,0:T(8,128)(2,1)}, bf16[2,2,528,128]{3,2,1,0:T(8,128)(2,1)S(1)}, u32[]{:S(2)}, u32[]{:S(2)}) collective-permute-start(bf16[2,2,528,128]{3,2,1,0:T(8,128)(2,1)} %copy-done.11), channel_id=1, source_target_pairs={{1,8},{8,1},{3,10},{10,3},{5,12},{12,5},{7,14},{14,7},{9,16},{16,9... | collective-permute-start | bytes 1622024 | tf_op jit(solution)/shard_map/ppermute | solution.py:518
  93.5 1.2 copy-start.3
  94.8 1.2 copy-start.4
  96.0 9.8 %copy-start.6 = (bf16[2,2,528,128]{3,2,1,0:T(8,128)(2,1)S(1)}, bf16[2,2,528,128]{3,2,1,0:T(8,128)(2,1)}, u32[]{:S(2)}) copy-start(bf16[2,2,528,128]{3,2,1,0:T(8,128)(2,1)} %copy-done.5) | copy-start | bytes 1622020
  96.0 9.8 %copy-start.9 = (bf16[2,2,528,128]{3,2,1,0:T(8,128)(2,1)S(1)}, bf16[2,2,528,128]{3,2,1,0:T(8,128)(2,1)}, u32[]{:S(2)}) copy-start(bf16[2,2,528,128]{3,2,1,0:T(8,128)(2,1)} %copy-done.7) | copy-start | bytes 1622020
  109.7 2.6 %collective-permute-start.7 = (bf16[4,2,384,128]{3,2,1,0:T(8,128)(2,1)}, bf16[4,2,384,128]{3,2,1,0:T(8,128)(2,1)S(1)}, u32[]{:S(2)}, u32[]{:S(2)}) collective-permute-start(bf16[4,2,384,128]{3,2,1,0:T(8,128)(2,1)} %get-tuple-element.49), channel_id=1, source_target_pairs={{0,1},{1,0},{2,3},{3,2},{4,5},{5,4},{6,7},{7,6},{8,9},{9,8},{10,11... | collective-permute-start | bytes 2359304 | tf_op jit(solution)/shard_map/ppermute | solution.py:511
  112.7 25.2 %copy-start.10 = (s32[16]{0:T(128)S(1)}, s32[16]{0:T(128)}, u32[]{:S(2)}) copy-start(s32[16]{0:T(128)} %tile_valid.3) | copy-start | bytes 196

commit v6 on v5

--- a/solution.py
+++ b/solution.py
@@ -291,7 +291,7 @@
         done[column % 2, ..., column // 2, rows, :] = ((total + first) * scale).astype(jnp.bfloat16)
 
 
-def row_kernel(arrived, swapped, row, row_swapped, row_rest, *rest):
+def row_kernel(_, arrived, swapped, row, row_swapped, row_rest, *rest):
     firsts, (mine, other, edges), rest = rest[:3], rest[3:6], rest[6:]
     own, near_raw, near_rest, done, first_totals, *totals, sems = rest
     core = lax.axis_index("space") % 2
@@ -357,7 +357,7 @@
     wait_all(start_all([(done.at[core], mine.at[edge]), (done.at[1 - core], other.at[edge])], sems))
 
 
-BORDER_FLOPS = 1 << 33
+GATE_FLOPS = 1 << 33
 TOTALS = (FRAMES, BLOCKS, TOKENS, HEAD_DIM)
 DONE = (FRAMES, 2, 3 * TOKENS, HEAD_DIM)
 
@@ -391,6 +391,7 @@
         vmem_specs(3),
         [jax.ShapeDtypeStruct(TOTALS, jnp.float32)] * 3,
         [pltpu.VMEM((2, FRAMES, 2, 2, ROWS, HEAD_DIM), jnp.bfloat16)],
+        vmem=56,
     )
 
 
@@ -408,9 +409,29 @@
         vmem_specs(1),
         [jax.ShapeDtypeStruct((2, 2, ROWS, HEAD_DIM), jnp.bfloat16)],
         [],
-        flops=BORDER_FLOPS,
         vmem=8,
     )[0]
+
+
+def gate_kernel(border, out):
+    out[...] = border[...]
+
+
+def gate_part(border):
+    shape = (1, 1, STAT_ROWS, HEAD_DIM)
+    block = pl.BlockSpec(shape, lambda i: (0, 0, 0, 0))
+    return pl.pallas_call(
+        gate_kernel,
+        grid=(1,),
+        out_shape=jax.ShapeDtypeStruct(shape, jnp.bfloat16),
+        in_specs=[block],
+        out_specs=block,
+        compiler_params=pltpu.CompilerParams(vmem_limit_bytes=8 << 20),
+        cost_estimate=pl.CostEstimate(
+            flops=GATE_FLOPS, bytes_accessed=GATE_FLOPS >> 8, transcendentals=0
+        ),
+        name="gate",
+    )(border)
 
 
 def rest_part(*args):
@@ -443,7 +464,7 @@
         ]
         + [pltpu.VMEM(TOTALS, jnp.float32)] * 3
         + [pltpu.SemaphoreType.DMA((len(args),))],
-        vmem=32,
+        vmem=46,
     )
 
 
@@ -556,12 +577,12 @@
     firsts = first_part(arrived, swapped)
     jump, firsts = lax.optimization_barrier((jump, firsts))
     jump_swapped = core_swap(jump)
-    jump_swapped, row_rest = lax.optimization_barrier((jump_swapped, row_rest))
     border = border_part(jump, jump_swapped)
-    row, border = lax.optimization_barrier((row, border))
     jump_row = row_swap(border)
+    gated, row_rest = lax.optimization_barrier((border, row_rest))
+    row, gate = lax.optimization_barrier((row, gate_part(gated)))
     row_swapped = core_swap(lax.dynamic_index_in_dim(row, core, 1, keepdims=False))
-    mine, other, edges = row_part(arrived, swapped, row, row_swapped, row_rest, *firsts)
+    mine, other, edges = row_part(gate, arrived, swapped, row, row_swapped, row_rest, *firsts)
     jump_row, edges = lax.optimization_barrier((jump_row, edges))
     mine, other = jump_part(
         arrived, swapped, jump, jump_swapped, jump_row, edges, mine, other

time: 140 us -> 138 us (0.986)
  local copies, waits for them, and re-layouts: 8.42 us -> 3.91 us
    unnamed x26 -> x12, local copies, waits for them, and re-layouts: 6.17 us -> 2.46 us
    all_to_all x2, waiting for transfers between devices: 10.2 us -> 12.1 us  [plane_exchange(): return lax.all_to_all(array, AXES, 0, 0, axis_index_groups=groups)]
  transfers between devices with their start and end apart: 10 -> 10, of which waited for: 5 -> 5; matrix products, arithmetic and copies ran while one was open for 1% -> 0% of each run, Pallas kernels for 21% -> 22%
where the time goes in v6:
time: 138 us; the launch traced here: 137 us
  Pallas kernels  39.8 us (29%)
  waiting for transfers between devices  36.1 us (26%)
  starting transfers between devices  30.7 us (22%)
  blocking collectives  25.7 us (19%)
  local copies, waits for them, and re-layouts  3.91 us (3%)
    pallas_call x5, Pallas kernels, attend(): pl.pallas_call(kernel, out_shape=out_shape, in_specs=in_specs, out_specs=...  31.4 us
    all_to_all x1, blocking collectives, plane_exchange(): return lax.all_to_all(array, AXES, 0, 0, axis_index_groups=groups)  25.7 us
    ppermute x1, waiting for transfers between devices, row_shift(): lax.ppermute(array, 'space', [(a, b) for a, b in route if 0 <= b < count])  16.3 us
    all_to_all x2, starting transfers between devices, plane_exchange(): return lax.all_to_all(array, AXES, 0, 0, axis_index_groups=groups)  15.3 us
    all_to_all x2, waiting for transfers between devices, plane_exchange(): return lax.all_to_all(array, AXES, 0, 0, axis_index_groups=groups)  12.1 us
    ppermute x1, starting transfers between devices, half_swap(): lax.ppermute(array, 'frame', [(f, (f + FRAMES) % count) for f in range(co...  6.09 us
    ppermute x2, starting transfers between devices, row_swap(): return lax.ppermute(array, 'space', route)  5.41 us
    ppermute x4, waiting for transfers between devices, core_swap(): lax.ppermute(array, 'space', [(s, s ^ 1) for s in range(lax.axis_size('sp...  4.19 us
  transfers between devices with their start and end apart: 10, of which 5 were waited for; matrix products, arithmetic and copies ran while one was open for 0% of the time, Pallas kernels for 22%

profile of v6, /device:TPU:1, one launch (start us, length us, event | category | flops | bytes accessed | tf_op | source)
XLA Modules:
  0.0 137.2 jit_solution(12709365849712854751)
XLA Ops:
  0.6 3.7 %pack.1 = (bf16[16,528,128]{2,1,0:T(8,128)(2,1)}, bf16[12,384,128]{2,1,0:T(8,128)(2,1)}) custom-call(s32[16]{0:T(128)} %tile_valid.3, bf16[128,1536]{1,0:T(8,128)(2,1)} %bitcast.33, bf16[128,1536]{1,0:T(8,128)(2,1)} %bitcast.34, bf16[128,1536]{1,0:T(8,128)(2,1)} %bitcast.35, bf16[128,1536]{1,0:T(8,128)(2,1)} %bitcast.36, f32[128,12]{1,0:T(8,128)} %bitcast.37, ...), custom_call_target="tpu_custom_call" | custom-call | tf_op jit(solution)/shard_map/pack/pallas_call | solution.py:89
  4.4 1.3 collective-permute-start
  5.6 10.9 %all-to-all-start = ((bf16[16,528,128]{2,1,0:T(8,128)(2,1)}), bf16[16,528,128]{2,1,0:T(8,128)(2,1)S(1)}, u32[]{:S(2)}, u32[]{:S(2)}) async-start(bf16[16,528,128]{2,1,0:T(8,128)(2,1)} %get-tuple-element.28), calls=%async_computation | async-start | bytes 4325376 | tf_op jit(solution)/shard_map/all_to_all | solution.py:524
  16.5 16.3 %collective-permute-done.heads = bf16[12,384,128]{2,1,0:T(8,128)(2,1)} collective-permute-done((bf16[12,384,128]{2,1,0:T(8,128)(2,1)}, bf16[12,384,128]{2,1,0:T(8,128)(2,1)}, u32[]{:S(2)}, u32[]{:S(2)}) %collective-permute-start) | collective-permute-done | bytes 1179680 | tf_op jit(solution)/shard_map/ppermute | solution.py:545
  32.8 2.2 %refill.1 = bf16[16,384,128]{2,1,0:T(8,128)(2,1)} custom-call(bf16[12,384,128]{2,1,0:T(8,128)(2,1)} %collective-permute-done.heads), custom_call_target="tpu_custom_call" | custom-call | flops 17179869184 | bytes 67108864 | tf_op jit(solution)/shard_map/refill/pallas_call | solution.py:123
  35.0 12.1 %all-to-all-done = bf16[16,528,128]{2,1,0:T(8,128)(2,1)S(1)} async-done(((bf16[16,528,128]{2,1,0:T(8,128)(2,1)}), bf16[16,528,128]{2,1,0:T(8,128)(2,1)S(1)}, u32[]{:S(2)}, u32[]{:S(2)}) %all-to-all-start) | async-done | bytes 2162720 | tf_op jit(solution)/shard_map/all_to_all | solution.py:524
  47.1 0.0 copy-start
  47.1 2.4 %collective-permute-start.1 = (bf16[4,2,2,528,128]{4,3,2,1,0:T(8,128)(2,1)S(1)}, bf16[4,2,2,528,128]{4,3,2,1,0:T(8,128)(2,1)}, u32[]{:S(2)}, u32[]{:S(2)}) collective-permute-start(bf16[4,2,2,528,128]{4,3,2,1,0:T(8,128)(2,1)S(1)} %bitcast.26), channel_id=1, source_target_pairs={{0,1},{1,0},{2,3},{3,2},{4,5},{5,4},{6,7},{7,6},{8,9},{9,8},{10,11... | collective-permute-start | bytes 6488072 | tf_op jit(solution)/shard_map/ppermute | solution.py:532
  49.6 6.1 %collective-permute-start.2 = (bf16[2,2,528,128]{3,2,1,0:T(8,128)(2,1)S(1)}, bf16[2,2,528,128]{3,2,1,0:T(8,128)(2,1)S(1)}, u32[]{:S(2)}, u32[]{:S(2)}) collective-permute-start(bf16[2,2,528,128]{3,2,1,0:T(8,128)(2,1)S(1)} %dynamic-slice_bitcast_fusion.1), channel_id=1, source_target_pairs={{0,128},{32,160},{64,192},{96,224},{128,0},{160,32},{192,64},{224,... | collective-permute-start | bytes 1622024 | tf_op jit(solution)/shard_map/ppermute | solution.py:550
  55.7 0.0 copy-done
  55.7 4.4 %all-to-all-start.1 = ((bf16[16,384,128]{2,1,0:T(8,128)(2,1)}), bf16[16,384,128]{2,1,0:T(8,128)(2,1)}, u32[]{:S(2)}, u32[]{:S(2)}) async-start(bf16[16,384,128]{2,1,0:T(8,128)(2,1)} %refill.1), calls=%async_computation.1 | async-start | bytes 3145728 | tf_op jit(solution)/shard_map/all_to_all | solution.py:524
  60.1 0.0 collective-permute-done.1.swapped
  60.1 1.9 %rest_part.1 = bf16[2,4,2,144,128]{4,3,2,1,0:T(8,128)(2,1)} custom-call(bf16[4,2,2,528,128]{4,3,2,1,0:T(8,128)(2,1)} %bitcast.28, bf16[4,2,2,528,128]{4,3,2,1,0:T(8,128)(2,1)} %collective-permute-done.1.swapped), custom_call_target="tpu_custom_call" | custom-call | flops 1024 | bytes 4 | tf_op jit(solution)/shard_map/rest_part/pallas_call | solution.py:366
  62.0 2.1 %collective-permute-start.5 = (bf16[2,4,2,144,128]{4,3,2,1,0:T(8,128)(2,1)}, bf16[2,4,2,144,128]{4,3,2,1,0:T(8,128)(2,1)S(1)}, u32[]{:S(2)}, u32[]{:S(2)}) collective-permute-start(bf16[2,4,2,144,128]{4,3,2,1,0:T(8,128)(2,1)} %rest_part.1), channel_id=1, source_target_pairs={{1,8},{8,1},{3,10},{10,3},{5,12},{12,5},{7,14},{14,7},{9,16},{16,9... | collective-permute-start | bytes 1769480 | tf_op jit(solution)/shard_map/ppermute | solution.py:539
  64.1 15.9 %first_part.1 = (f32[4,4,128,128]{3,2,1,0:T(8,128)}, f32[4,4,128,128]{3,2,1,0:T(8,128)}, f32[4,4,128,128]{3,2,1,0:T(8,128)}) custom-call(bf16[4,2,2,528,128]{4,3,2,1,0:T(8,128)(2,1)} %bitcast.29, bf16[4,2,2,528,128]{4,3,2,1,0:T(8,128)(2,1)} %collective-permute-done.1.swapped), custom_call_target="tpu_custom_call" | custom-call | flops 1024 | bytes 4 | tf_op jit(solution)/shard_map/first_part/pallas_call | solution.py:366
  80.0 0.0 collective-permute-done.2.jump
  80.0 0.0 collective-permute-start.3
  80.0 1.9 %collective-permute-done.3.jump_swapped = bf16[2,2,528,128]{3,2,1,0:T(8,128)(2,1)S(1)} collective-permute-done((bf16[2,2,528,128]{3,2,1,0:T(8,128)(2,1)S(1)}, bf16[2,2,528,128]{3,2,1,0:T(8,128)(2,1)S(1)}, u32[]{:S(2)}, u32[]{:S(2)}) %collective-permute-start.3) | collective-permute-done | bytes 540704 | tf_op jit(solution)/shard_map/ppermute | solution.py:532
  82.0 0.8 border_part.1.border
  82.8 3.5 %collective-permute-done.5.row_rest = bf16[2,4,2,144,128]{4,3,2,1,0:T(8,128)(2,1)S(1)} collective-permute-done((bf16[2,4,2,144,128]{4,3,2,1,0:T(8,128)(2,1)}, bf16[2,4,2,144,128]{4,3,2,1,0:T(8,128)(2,1)S(1)}, u32[]{:S(2)}, u32[]{:S(2)}) %collective-permute-start.5) | collective-permute-done | bytes 589856 | tf_op jit(solution)/shard_map/ppermute | solution.py:539
  86.3 0.7 gate.1._
  86.9 0.0 all-to-all-done.1
  86.9 0.0 copy-start.2
  86.9 1.3 dynamic-slice_bitcast_fusion
  88.2 0.0 copy-start.1
  88.2 0.1 collective-permute-start.6
  88.3 3.3 %collective-permute-start.4 = (bf16[2,2,528,128]{3,2,1,0:T(8,128)(2,1)}, bf16[2,2,528,128]{3,2,1,0:T(8,128)(2,1)S(1)}, u32[]{:S(2)}, u32[]{:S(2)}) collective-permute-start(bf16[2,2,528,128]{3,2,1,0:T(8,128)(2,1)} %border_part.1.border), channel_id=1, source_target_pairs={{1,8},{8,1},{3,10},{10,3},{5,12},{12,5},{7,14},{14,7},{9,16},{16,9... | collective-permute-start | bytes 1622024 | tf_op jit(solution)/shard_map/ppermute | solution.py:539
  91.7 0.0 collective-permute-done.6.row_swapped
  91.7 0.0 copy-done.2
  91.7 0.0 copy-start.3
  91.7 1.2 copy-done.3
  92.9 0.0 copy-start.4
  92.9 1.2 copy-done.4
  94.1 9.2 %row_part.1 = (bf16[4,2,384,128]{3,2,1,0:T(8,128)(2,1)S(1)}, bf16[4,2,384,128]{3,2,1,0:T(8,128)(2,1)S(1)}, f32[3,4,128,128]{3,2,1,0:T(8,128)S(1)}) custom-call(bf16[1,1,16,128]{3,2,1,0:T(8,128)(2,1)S(1)} %gate.1._, bf16[4,2,2,528,128]{4,3,2,1,0:T(8,128)(2,1)} %bitcast.30, bf16[4,2,2,528,128]{4,3,2,1,0:T(8,128)(2,1)} %collective-permute-done.1.swapped, ...), custom_call_target="tpu_custom_call" | custom-call | flops 1024 | bytes 4 | tf_op jit(solution)/shard_map/row_part/pallas_call | solution.py:366
  103.4 0.0 collective-permute-done.4.jump_row
  103.4 0.0 copy-done.1
  103.4 3.5 %jump_part.1 = (bf16[4,2,384,128]{3,2,1,0:T(8,128)(2,1)S(1)}, bf16[4,2,384,128]{3,2,1,0:T(8,128)(2,1)S(1)}) custom-call(bf16[4,2,2,528,128]{4,3,2,1,0:T(8,128)(2,1)S(1)} %bitcast.31, bf16[4,2,2,528,128]{4,3,2,1,0:T(8,128)(2,1)} %collective-permute-done.1.swapped, ...), custom_call_target="tpu_custom_call", output_to_operand_aliasing={{0}: (6, {}), {1}: (7, {})} | custom-call | flops 1024 | bytes 4 | tf_op jit(solution)/shard_map/jump_part/pallas_call | solution.py:366
  106.9 0.1 collective-permute-start.7
  107.0 2.3 %collective-permute-done.7 = bf16[4,2,384,128]{3,2,1,0:T(8,128)(2,1)S(1)} collective-permute-done((bf16[4,2,384,128]{3,2,1,0:T(8,128)(2,1)S(1)}, bf16[4,2,384,128]{3,2,1,0:T(8,128)(2,1)S(1)}, u32[]{:S(2)}, u32[]{:S(2)}) %collective-permute-start.7) | collective-permute-done | bytes 786464 | tf_op jit(solution)/shard_map/ppermute | solution.py:532
  109.3 0.1 select_bitcast_fusion.1
  109.4 0.1 pad_maximum_fusion
  109.5 0.1 copy.12
  109.7 0.0 copy-start.5
  109.7 25.7 %all_to_all.15.blocks = bf16[16,384,128]{2,1,0:T(8,128)(2,1)S(1)} all-to-all(bf16[16,384,128]{2,1,0:T(8,128)(2,1)S(1)} %bitcast.32), channel_id=1, replica_groups={{0,2,4,6,32,34,36,38,64,66,68,70,96,98,100,102},{1,3,5,7,33,35,37,39,65..., dimensions={0} | all-to-all | bytes 3145728 | tf_op jit(solution)/shard_map/all_to_all | solution.py:524
  135.4 0.0 copy-done.5
  135.4 1.8 %unpack.1 = (bf16[128,1536]{1,0:T(8,128)(2,1)}, bf16[128,1536]{1,0:T(8,128)(2,1)}, bf16[128,1536]{1,0:T(8,128)(2,1)}) custom-call(s32[16]{0:T(128)S(1)} %copy-done.5, bf16[16,384,128]{2,1,0:T(8,128)(2,1)S(1)} %all_to_all.15.blocks), custom_call_target="tpu_custom_call" | custom-call | tf_op jit(solution)/shard_map/unpack/pallas_call | solution.py:502
  (1 shorter events, 0.0 us)
Async XLA Ops:
  4.4 28.4 %collective-permute-start = (bf16[12,384,128]{2,1,0:T(8,128)(2,1)}, bf16[12,384,128]{2,1,0:T(8,128)(2,1)}, u32[]{:S(2)}, u32[]{:S(2)}) collective-permute-start(bf16[12,384,128]{2,1,0:T(8,128)(2,1)} %get-tuple-element.29), channel_id=1, source_target_pairs={{4,12},{5,13},{6,14},{7,15},{8,0},{9,1},{10,2},{11,3},{12,20},{13,... | collective-permute-start | bytes 3538952 | tf_op jit(solution)/shard_map/ppermute | solution.py:545
  5.6 41.5 %all-to-all-start = ((bf16[16,528,128]{2,1,0:T(8,128)(2,1)}), bf16[16,528,128]{2,1,0:T(8,128)(2,1)S(1)}, u32[]{:S(2)}, u32[]{:S(2)}) async-start(bf16[16,528,128]{2,1,0:T(8,128)(2,1)} %get-tuple-element.28), calls=%async_computation | async-start | bytes 4325376 | tf_op jit(solution)/shard_map/all_to_all | solution.py:524
  47.1 8.6 %copy-start = (bf16[16,528,128]{2,1,0:T(8,128)(2,1)}, bf16[16,528,128]{2,1,0:T(8,128)(2,1)S(1)}, u32[]{:S(2)}) copy-start(bf16[16,528,128]{2,1,0:T(8,128)(2,1)S(1)} %all-to-all-done) | copy-start | bytes 6488068
  47.1 13.0 %collective-permute-start.1 = (bf16[4,2,2,528,128]{4,3,2,1,0:T(8,128)(2,1)S(1)}, bf16[4,2,2,528,128]{4,3,2,1,0:T(8,128)(2,1)}, u32[]{:S(2)}, u32[]{:S(2)}) collective-permute-start(bf16[4,2,2,528,128]{4,3,2,1,0:T(8,128)(2,1)S(1)} %bitcast.26), channel_id=1, source_target_pairs={{0,1},{1,0},{2,3},{3,2},{4,5},{5,4},{6,7},{7,6},{8,9},{9,8},{10,11... | collective-permute-start | bytes 6488072 | tf_op jit(solution)/shard_map/ppermute | solution.py:532
  49.6 30.4 %collective-permute-start.2 = (bf16[2,2,528,128]{3,2,1,0:T(8,128)(2,1)S(1)}, bf16[2,2,528,128]{3,2,1,0:T(8,128)(2,1)S(1)}, u32[]{:S(2)}, u32[]{:S(2)}) collective-permute-start(bf16[2,2,528,128]{3,2,1,0:T(8,128)(2,1)S(1)} %dynamic-slice_bitcast_fusion.1), channel_id=1, source_target_pairs={{0,128},{32,160},{64,192},{96,224},{128,0},{160,32},{192,64},{224,... | collective-permute-start | bytes 1622024 | tf_op jit(solution)/shard_map/ppermute | solution.py:550
  55.7 31.3 %all-to-all-start.1 = ((bf16[16,384,128]{2,1,0:T(8,128)(2,1)}), bf16[16,384,128]{2,1,0:T(8,128)(2,1)}, u32[]{:S(2)}, u32[]{:S(2)}) async-start(bf16[16,384,128]{2,1,0:T(8,128)(2,1)} %refill.1), calls=%async_computation.1 | async-start | bytes 3145728 | tf_op jit(solution)/shard_map/all_to_all | solution.py:524
  62.0 24.2 %collective-permute-start.5 = (bf16[2,4,2,144,128]{4,3,2,1,0:T(8,128)(2,1)}, bf16[2,4,2,144,128]{4,3,2,1,0:T(8,128)(2,1)S(1)}, u32[]{:S(2)}, u32[]{:S(2)}) collective-permute-start(bf16[2,4,2,144,128]{4,3,2,1,0:T(8,128)(2,1)} %rest_part.1), channel_id=1, source_target_pairs={{1,8},{8,1},{3,10},{10,3},{5,12},{12,5},{7,14},{14,7},{9,16},{16,9... | collective-permute-start | bytes 1769480 | tf_op jit(solution)/shard_map/ppermute | solution.py:539
  80.0 1.9 %collective-permute-start.3 = (bf16[2,2,528,128]{3,2,1,0:T(8,128)(2,1)S(1)}, bf16[2,2,528,128]{3,2,1,0:T(8,128)(2,1)S(1)}, u32[]{:S(2)}, u32[]{:S(2)}) collective-permute-start(bf16[2,2,528,128]{3,2,1,0:T(8,128)(2,1)S(1)} %collective-permute-done.2.jump), channel_id=1, source_target_pairs={{0,1},{1,0},{2,3},{3,2},{4,5},{5,4},{6,7},{7,6},{8,9},{9,8},{10,11... | collective-permute-start | bytes 1622024 | tf_op jit(solution)/shard_map/ppermute | solution.py:532
  86.9 4.7 %copy-start.2 = (f32[4,4,128,128]{3,2,1,0:T(8,128)S(1)}, f32[4,4,128,128]{3,2,1,0:T(8,128)}, u32[]{:S(2)}) copy-start(f32[4,4,128,128]{3,2,1,0:T(8,128)} %get-tuple-element.40.rest_0_) | copy-start | bytes 3145732
  88.2 15.2 %copy-start.1 = (bf16[16,528,128]{2,1,0:T(8,128)(2,1)S(1)}, bf16[16,528,128]{2,1,0:T(8,128)(2,1)}, u32[]{:S(2)}) copy-start(bf16[16,528,128]{2,1,0:T(8,128)(2,1)} %copy-done) | copy-start | bytes 6488068
  88.2 3.4 %collective-permute-start.6 = (bf16[4,2,384,128]{3,2,1,0:T(8,128)(2,1)S(1)}, bf16[4,2,384,128]{3,2,1,0:T(8,128)(2,1)S(1)}, u32[]{:S(2)}, u32[]{:S(2)}) collective-permute-start(bf16[4,2,384,128]{3,2,1,0:T(8,128)(2,1)S(1)} %dynamic-slice_bitcast_fusion), channel_id=1, source_target_pairs={{0,1},{1,0},{2,3},{3,2},{4,5},{5,4},{6,7},{7,6},{8,9},{9,8},{10,11... | collective-permute-start | bytes 2359304 | tf_op jit(solution)/shard_map/ppermute | solution.py:532
  88.3 15.0 %collective-permute-start.4 = (bf16[2,2,528,128]{3,2,1,0:T(8,128)(2,1)}, bf16[2,2,528,128]{3,2,1,0:T(8,128)(2,1)S(1)}, u32[]{:S(2)}, u32[]{:S(2)}) collective-permute-start(bf16[2,2,528,128]{3,2,1,0:T(8,128)(2,1)} %border_part.1.border), channel_id=1, source_target_pairs={{1,8},{8,1},{3,10},{10,3},{5,12},{12,5},{7,14},{14,7},{9,16},{16,9... | collective-permute-start | bytes 1622024 | tf_op jit(solution)/shard_map/ppermute | solution.py:539
  91.7 1.2 copy-start.3
  92.9 1.2 copy-start.4
  106.9 2.4 %collective-permute-start.7 = (bf16[4,2,384,128]{3,2,1,0:T(8,128)(2,1)S(1)}, bf16[4,2,384,128]{3,2,1,0:T(8,128)(2,1)S(1)}, u32[]{:S(2)}, u32[]{:S(2)}) collective-permute-start(bf16[4,2,384,128]{3,2,1,0:T(8,128)(2,1)S(1)} %get-tuple-element.49), channel_id=1, source_target_pairs={{0,1},{1,0},{2,3},{3,2},{4,5},{5,4},{6,7},{7,6},{8,9},{9,8},{10,11... | collective-permute-start | bytes 2359304 | tf_op jit(solution)/shard_map/ppermute | solution.py:532
  109.7 25.7 %copy-start.5 = (s32[16]{0:T(128)S(1)}, s32[16]{0:T(128)}, u32[]{:S(2)}) copy-start(s32[16]{0:T(128)} %tile_valid.3) | copy-start | bytes 196
